TPU v7x, 512 devices: a whole 4x8x8 slice. The times are simulated.
512 devices in a mesh: dp: 64 (over z_hi, y, core), fsdp: 8 (over z_lo, x).
Axes of the slice: x: 4, y: 8, z: 8 (z_hi: 4, z_lo: 2; z = z_hi * 2 + z_lo), core: 2. Of those that a mesh axis runs over, the one named last changes fastest.
Arguments:
- inputs: bfloat16 [768, 5120], P('dp', 'fsdp'), may hold values from -6 to 6
- upstream: bfloat16 [768, 5120], P('dp', 'fsdp'), may hold values from -6 to 6
- w_gate: bfloat16 [5120, 27648], P('fsdp', 'dp'), may hold values from -0.078125 to 0.078125
- w_up: bfloat16 [5120, 27648], P('fsdp', 'dp'), may hold values from -0.078125 to 0.078125
- w_down: bfloat16 [27648, 5120], P('dp', 'fsdp'), may hold values from -0.0390625 to 0.0390625
- lengths: int32 [64], replicated, may hold values from 1 to 12, as said below
- move_dest: int32 [64, 3], replicated, may hold values from 0 to 63, as said below
Outputs:
- grad_inputs: bfloat16 [384, 5120], P('dp', 'fsdp')
- grad_gate: bfloat16 [5120, 27648], P('fsdp', 'dp')
- grad_up: bfloat16 [5120, 27648], P('fsdp', 'dp')
- grad_down: bfloat16 [27648, 5120], P('dp', 'fsdp')
Inputs may be any that keep to these rules, and one draw needn't show every extreme that they name: `lengths`: exactly a quarter of the learners have all 12 rows valid; every other learner has at most 1 block that hold valid rows. move_dest[l, m] is l itself exactly when block 3 + m of learner l holds no valid row; no learner sends two blocks to the same learner; a learner that receives k blocks sends none and has no valid row in its last k of the first 3 block slots; no learner receives more than 1 block.
All inputs are finite; a program needn't handle non-finite values.
Results may differ from a plain program's by a relative error of at most 0.0049.
Values may be sent and summed in bfloat16 or wider, within the bound.
No kernel may reach another device: no remote copies, remote signals or barrier semaphores. Data moves between devices by JAX's collectives and lax.ppermute only.
A program may use at most 64 MiB of HBM per device.

v0:
```python
import jax
import jax.numpy as jnp
from jax import lax
from jax.sharding import PartitionSpec as P


def select_blocks(outgoing, tail_blocks):
    return jnp.einsum(
        "dm,mbf->dbf", outgoing, tail_blocks, preferred_element_type=jnp.float32
    ).astype(jnp.bfloat16)


def place_blocks(placing, received):
    return jnp.einsum("hs,sbf->hbf", placing, received, preferred_element_type=jnp.float32).astype(
        jnp.bfloat16
    )


def swiglu_grads(gate_value, up_value, back_hidden):
    sigmoid_gate = jax.nn.sigmoid(gate_value)
    activated = gate_value * sigmoid_gate
    hidden = (activated * up_value).astype(jnp.bfloat16)
    grad_gate_hidden = (
        back_hidden * up_value * sigmoid_gate * (1.0 + gate_value * (1.0 - sigmoid_gate))
    ).astype(jnp.bfloat16)
    grad_up_hidden = (back_hidden * activated).astype(jnp.bfloat16)
    return (hidden, grad_gate_hidden, grad_up_hidden)


def body(inputs, upstream, w_gate, w_up, w_down, lengths, move_dest):
    members = lax.axis_size("dp")
    myself = lax.axis_index("dp")
    slots_held = move_dest.shape[1]
    capacity = inputs.shape[0]
    block_rows = capacity // (2 * slots_held)
    features = inputs.shape[1]
    learners = jnp.arange(members, dtype=jnp.int32)
    is_mine = learners == myself
    own_length = jnp.sum(jnp.where(is_mine, lengths, 0))
    valid_rows = (jnp.arange(capacity, dtype=jnp.int32) < own_length)[:, None]
    zero_value = jnp.zeros((), jnp.bfloat16)
    inputs_kept = jnp.where(valid_rows, inputs, zero_value)
    upstream_kept = jnp.where(valid_rows, upstream, zero_value)
    grad_scale = lax.rsqrt(jnp.sum(lengths).astype(jnp.float32))
    own_targets = jnp.sum(jnp.where(is_mine[:, None], move_dest, 0), axis=0)
    outgoing = ((own_targets[None, :] == learners[:, None]) & (learners[:, None] != myself)).astype(
        jnp.bfloat16
    )
    arrivals_hit = (move_dest == myself) & (learners[:, None] != myself)
    arriving = jnp.any(arrivals_hit, axis=1).astype(jnp.int32)
    arrival_rank = jnp.cumsum(arriving) - arriving
    slot_index = jnp.arange(slots_held, dtype=jnp.int32)[:, None]
    placing = (
        (slot_index == slots_held - 1 - arrival_rank[None, :]) & (arriving[None, :] > 0)
    ).astype(jnp.bfloat16)
    contract_rows = (((0,), (0,)), ((), ()))
    contract_hidden = (((1,), (1,)), ((), ()))
    all_in = lax.all_gather(inputs_kept, "dp", axis=0, tiled=True)
    all_up = lax.all_gather(upstream_kept, "dp", axis=0, tiled=True)
    gate_value = jnp.dot(all_in, w_gate, preferred_element_type=jnp.float32)
    up_value = jnp.dot(all_in, w_up, preferred_element_type=jnp.float32)
    back_hidden = lax.dot_general(
        all_up, w_down, contract_hidden, preferred_element_type=jnp.float32
    )
    gate_value, up_value, back_hidden = lax.psum((gate_value, up_value, back_hidden), "fsdp")
    hidden, grad_gate_hidden, grad_up_hidden = swiglu_grads(gate_value, up_value, back_hidden)
    gate_total = lax.dot_general(
        all_in, grad_gate_hidden, contract_rows, preferred_element_type=jnp.float32
    )
    up_total = lax.dot_general(
        all_in, grad_up_hidden, contract_rows, preferred_element_type=jnp.float32
    )
    down_total = lax.dot_general(hidden, all_up, contract_rows, preferred_element_type=jnp.float32)
    total = lax.dot_general(
        grad_gate_hidden, w_gate, contract_hidden, preferred_element_type=jnp.float32
    )
    grad_rows = lax.psum_scatter(
        total
        + lax.dot_general(
            grad_up_hidden, w_up, contract_hidden, preferred_element_type=jnp.float32
        ),
        "dp",
        scatter_dimension=0,
        tiled=True,
    )
    grad_rows, gate_total, up_total, down_total = (
        grad_rows.astype(jnp.bfloat16),
        gate_total,
        up_total,
        down_total,
    )
    grad_blocks = grad_rows.reshape(2 * slots_held, block_rows, features)
    sent = select_blocks(outgoing, grad_blocks[slots_held:])
    got = lax.all_to_all(sent, "dp", split_axis=0, concat_axis=0, tiled=True)
    grad_inputs = (grad_blocks[:slots_held] + place_blocks(placing, got)).reshape(
        slots_held * block_rows, features
    )
    grad_gate = (gate_total * grad_scale).astype(jnp.bfloat16)
    grad_up = (up_total * grad_scale).astype(jnp.bfloat16)
    grad_down = (down_total * grad_scale).astype(jnp.bfloat16)
    return (grad_inputs, grad_gate, grad_up, grad_down)


def solution(mesh):
    in_specs = (
        P("dp", "fsdp"),
        P("dp", "fsdp"),
        P("fsdp", "dp"),
        P("fsdp", "dp"),
        P("dp", "fsdp"),
        P(),
        P(),
    )
    out_specs = (P("dp", "fsdp"), P("fsdp", "dp"), P("fsdp", "dp"), P("dp", "fsdp"))
    return jax.shard_map(body, mesh=mesh, in_specs=in_specs, out_specs=out_specs, check_vma=False)
```

profile of v0, /device:TPU:1, one launch (start us, length us, event | category | flops | bytes accessed | tf_op | source)
XLA Modules:
  0.0 553.5 jit_solution(17738186717509682768)
XLA Ops:
  7.2 1.3 fusion.22
  10.1 93.6 %all-gather.1 = bf16[64,12,640]{2,1,0:T(8,128)(2,1)S(1)} all-gather(bf16[1,12,640]{2,1,0:T(8,128)(2,1)S(1)} %get-tuple-element.31), channel_id=1, replica_groups=mesh['dp'=64,'fsdp'=8] {'dp'}, dimensions={0}, use_global_device_ids=true | all-gather | bytes 998400 | tf_op jit(solution)/shard_map/all_gather | solution.py:58
  104.8 1.8 fusion.26
  106.5 1.8 fusion.27
  108.3 80.0 %all-gather = bf16[64,12,640]{2,1,0:T(8,128)(2,1)S(1)} all-gather(bf16[1,12,640]{2,1,0:T(8,128)(2,1)S(1)} %get-tuple-element.30), channel_id=1, replica_groups=mesh['dp'=64,'fsdp'=8] {'dp'}, dimensions={0}, use_global_device_ids=true | all-gather | bytes 998400 | tf_op jit(solution)/shard_map/all_gather | solution.py:59
  189.5 3.0 fusion.25
  193.2 105.6 %all-reduce.5.cloned.1.call-done = (f32[768,432]{0,1:T(8,128)}, f32[768,432]{0,1:T(8,128)}, f32[768,432]{0,1:T(8,128)}) async-done(((f32[768,432]{0,1:T(8,128)}, f32[768,432]{0,1:T(8,128)}, f32[768,432]{0,1:T(8,128)}), (f32[768,432]{0,1:T(8,128)}, f32[768,432]{0,1:T(8,128)}, f32[768,432]{0,1:T(8,128)})) %all-reduce.5.cloned.1.call-update) | async-done | bytes 3981328 | tf_op jit(solution)/shard_map/psum | solution.py:65
  298.8 2.7 multiply_convert_fusion.1
  303.9 157.8 %fusion = f32[16,640]{1,0:T(8,128)S(1)} fusion(f32[768,640]{1,0:T(8,128)S(1)} %convolution_add_fusion), kind=kCustom, calls=%all-reduce-scatter | all-reduce-scatter fusion | flops 655361 | bytes 2009088
  461.7 1.3 collective-permute-start.15
  463.3 2.1 collective-permute-start
  465.4 1.3 collective-permute-start.1
  466.7 9.9 %collective-permute-start.10 = (bf16[16,640]{1,0:T(8,128)(2,1)S(1)}, bf16[16,640]{1,0:T(8,128)(2,1)S(1)}, u32[]{:S(2)}, u32[]{:S(2)}) collective-permute-start(bf16[16,640]{1,0:T(8,128)(2,1)S(1)} %convert.31), channel_id=1, source_target_pairs={{0,88},{8,96},{16,104},{24,112},{32,120},{40,128},{48,136},{56,144... | collective-permute-start | bytes 61448
  476.6 8.1 %collective-permute-start.11 = (bf16[16,640]{1,0:T(8,128)(2,1)S(1)}, bf16[16,640]{1,0:T(8,128)(2,1)S(1)}, u32[]{:S(2)}, u32[]{:S(2)}) collective-permute-start(bf16[16,640]{1,0:T(8,128)(2,1)S(1)} %convert.31), channel_id=1, source_target_pairs={{0,96},{8,104},{16,112},{24,120},{32,128},{40,136},{48,144},{56,15... | collective-permute-start | bytes 61448
  484.7 1.3 collective-permute-start.12
  486.0 1.4 collective-permute-start.13
  487.4 3.1 collective-permute-start.14
  490.5 3.6 collective-permute-start.2
  494.2 2.8 collective-permute-start.3
  497.0 1.3 collective-permute-start.4
  499.7 1.3 dynamic-slice.4
  501.7 5.9 %collective-permute-start.5 = (bf16[16,640]{1,0:T(8,128)(2,1)S(1)}, bf16[16,640]{1,0:T(8,128)(2,1)S(1)}, u32[]{:S(2)}, u32[]{:S(2)}) collective-permute-start(bf16[16,640]{1,0:T(8,128)(2,1)S(1)} %convert.31), channel_id=1, source_target_pairs={{0,48},{8,56},{16,64},{24,72},{32,80},{40,88},{48,96},{56,104},{64... | collective-permute-start | bytes 61448
  507.6 2.8 collective-permute-start.6
  510.4 3.1 collective-permute-start.7
  513.5 3.3 collective-permute-start.8
  516.9 1.9 collective-permute-start.9
  518.8 3.7 fusion.2
  522.5 2.6 concatenate
  526.4 6.5 %all-to-all-start = ((bf16[64,2,640]{2,1,0:T(2,128)(2,1)}), bf16[64,2,640]{2,1,0:T(2,128)(2,1)S(1)}, u32[]{:S(2)}, u32[]{:S(2)}) async-start(bf16[64,2,640]{2,1,0:T(2,128)(2,1)} %copy.28), calls=%async_computation | async-start | bytes 327680 | tf_op jit(solution)/shard_map/all_to_all | solution.py:94
  532.9 1.5 fusion.3
  534.4 1.5 fusion.4
  535.9 10.0 %all-to-all-done = bf16[64,2,640]{2,1,0:T(2,128)(2,1)S(1)} async-done(((bf16[64,2,640]{2,1,0:T(2,128)(2,1)}), bf16[64,2,640]{2,1,0:T(2,128)(2,1)S(1)}, u32[]{:S(2)}, u32[]{:S(2)}) %all-to-all-start) | async-done | bytes 163872 | tf_op jit(solution)/shard_map/all_to_all | solution.py:94
  (61 shorter events, 9.8 us)
Async XLA Ops:
  7.2 99.4 %copy-start = (bf16[640,432]{0,1:T(8,128)(2,1)S(1)}, bf16[640,432]{0,1:T(8,128)(2,1)}, u32[]{:S(2)}) copy-start(bf16[640,432]{0,1:T(8,128)(2,1)} %param.9) | copy-start | bytes 1658884
  7.2 291.6 %all-reduce.5.cloned.1.call-start = ((), (), s32[]{:S(2)}) async-start(), calls=%async_computation.1 | async-start | bytes 7962624 | tf_op jit(solution)/shard_map/psum | solution.py:65
  103.7 1.1 copy-start.5
  188.4 1.1 copy-start.7
  192.5 0.7 copy-start.8
  301.5 0.9 copy-start.1
  301.5 1.1 copy-start.3
  301.5 1.5 copy-start.6
  461.7 23.0 %collective-permute-start.15 = (bf16[12,640]{1,0:T(8,128)(2,1)S(1)}, bf16[12,640]{1,0:T(8,128)(2,1)S(1)}, u32[]{:S(2)}, u32[]{:S(2)}) collective-permute-start(bf16[12,640]{1,0:T(8,128)(2,1)S(1)} %slice.18), channel_id=1, source_target_pairs={{0,128},{8,136},{16,144},{24,152},{32,160},{40,168},{48,176},{56,1... | collective-permute-start | bytes 46088
  463.3 22.7 %collective-permute-start = (bf16[16,640]{1,0:T(8,128)(2,1)S(1)}, bf16[16,640]{1,0:T(8,128)(2,1)S(1)}, u32[]{:S(2)}, u32[]{:S(2)}) collective-permute-start(bf16[16,640]{1,0:T(8,128)(2,1)S(1)} %convert.31), channel_id=1, source_target_pairs={{0,8},{8,16},{16,24},{24,32},{32,40},{40,48},{48,56},{56,64},{64,7... | collective-permute-start | bytes 61448
  465.4 22.0 %collective-permute-start.1 = (bf16[16,640]{1,0:T(8,128)(2,1)S(1)}, bf16[16,640]{1,0:T(8,128)(2,1)S(1)}, u32[]{:S(2)}, u32[]{:S(2)}) collective-permute-start(bf16[16,640]{1,0:T(8,128)(2,1)S(1)} %convert.31), channel_id=1, source_target_pairs={{0,16},{8,24},{16,32},{24,40},{32,48},{40,56},{48,64},{56,72},{64,... | collective-permute-start | bytes 61448
  466.7 23.8 %collective-permute-start.10 = (bf16[16,640]{1,0:T(8,128)(2,1)S(1)}, bf16[16,640]{1,0:T(8,128)(2,1)S(1)}, u32[]{:S(2)}, u32[]{:S(2)}) collective-permute-start(bf16[16,640]{1,0:T(8,128)(2,1)S(1)} %convert.31), channel_id=1, source_target_pairs={{0,88},{8,96},{16,104},{24,112},{32,120},{40,128},{48,136},{56,144... | collective-permute-start | bytes 61448
  476.6 17.6 %collective-permute-start.11 = (bf16[16,640]{1,0:T(8,128)(2,1)S(1)}, bf16[16,640]{1,0:T(8,128)(2,1)S(1)}, u32[]{:S(2)}, u32[]{:S(2)}) collective-permute-start(bf16[16,640]{1,0:T(8,128)(2,1)S(1)} %convert.31), channel_id=1, source_target_pairs={{0,96},{8,104},{16,112},{24,120},{32,128},{40,136},{48,144},{56,15... | collective-permute-start | bytes 61448
  484.7 12.3 %collective-permute-start.12 = (bf16[16,640]{1,0:T(8,128)(2,1)S(1)}, bf16[16,640]{1,0:T(8,128)(2,1)S(1)}, u32[]{:S(2)}, u32[]{:S(2)}) collective-permute-start(bf16[16,640]{1,0:T(8,128)(2,1)S(1)} %convert.31), channel_id=1, source_target_pairs={{0,104},{8,112},{16,120},{24,128},{32,136},{40,144},{48,152},{56,1... | collective-permute-start | bytes 61448
  486.0 15.6 %collective-permute-start.13 = (bf16[16,640]{1,0:T(8,128)(2,1)S(1)}, bf16[16,640]{1,0:T(8,128)(2,1)S(1)}, u32[]{:S(2)}, u32[]{:S(2)}) collective-permute-start(bf16[16,640]{1,0:T(8,128)(2,1)S(1)} %convert.31), channel_id=1, source_target_pairs={{0,112},{8,120},{16,128},{24,136},{32,144},{40,152},{48,160},{56,1... | collective-permute-start | bytes 61448
  487.4 20.2 %collective-permute-start.14 = (bf16[16,640]{1,0:T(8,128)(2,1)S(1)}, bf16[16,640]{1,0:T(8,128)(2,1)S(1)}, u32[]{:S(2)}, u32[]{:S(2)}) collective-permute-start(bf16[16,640]{1,0:T(8,128)(2,1)S(1)} %convert.31), channel_id=1, source_target_pairs={{0,120},{8,128},{16,136},{24,144},{32,152},{40,160},{48,168},{56,1... | collective-permute-start | bytes 61448
  490.5 19.9 %collective-permute-start.2 = (bf16[16,640]{1,0:T(8,128)(2,1)S(1)}, bf16[16,640]{1,0:T(8,128)(2,1)S(1)}, u32[]{:S(2)}, u32[]{:S(2)}) collective-permute-start(bf16[16,640]{1,0:T(8,128)(2,1)S(1)} %convert.31), channel_id=1, source_target_pairs={{0,24},{8,32},{16,40},{24,48},{32,56},{40,64},{48,72},{56,80},{64,... | collective-permute-start | bytes 61448
  494.2 19.3 %collective-permute-start.3 = (bf16[16,640]{1,0:T(8,128)(2,1)S(1)}, bf16[16,640]{1,0:T(8,128)(2,1)S(1)}, u32[]{:S(2)}, u32[]{:S(2)}) collective-permute-start(bf16[16,640]{1,0:T(8,128)(2,1)S(1)} %convert.31), channel_id=1, source_target_pairs={{0,32},{8,40},{16,48},{24,56},{32,64},{40,72},{48,80},{56,88},{64,... | collective-permute-start | bytes 61448
  497.0 19.9 %collective-permute-start.4 = (bf16[16,640]{1,0:T(8,128)(2,1)S(1)}, bf16[16,640]{1,0:T(8,128)(2,1)S(1)}, u32[]{:S(2)}, u32[]{:S(2)}) collective-permute-start(bf16[16,640]{1,0:T(8,128)(2,1)S(1)} %convert.31), channel_id=1, source_target_pairs={{0,40},{8,48},{16,56},{24,64},{32,72},{40,80},{48,88},{56,96},{64,... | collective-permute-start | bytes 61448
  501.7 20.8 %collective-permute-start.5 = (bf16[16,640]{1,0:T(8,128)(2,1)S(1)}, bf16[16,640]{1,0:T(8,128)(2,1)S(1)}, u32[]{:S(2)}, u32[]{:S(2)}) collective-permute-start(bf16[16,640]{1,0:T(8,128)(2,1)S(1)} %convert.31), channel_id=1, source_target_pairs={{0,48},{8,56},{16,64},{24,72},{32,80},{40,88},{48,96},{56,104},{64... | collective-permute-start | bytes 61448
  507.6 14.9 %collective-permute-start.6 = (bf16[16,640]{1,0:T(8,128)(2,1)S(1)}, bf16[16,640]{1,0:T(8,128)(2,1)S(1)}, u32[]{:S(2)}, u32[]{:S(2)}) collective-permute-start(bf16[16,640]{1,0:T(8,128)(2,1)S(1)} %convert.31), channel_id=1, source_target_pairs={{0,56},{8,64},{16,72},{24,80},{32,88},{40,96},{48,104},{56,112},{6... | collective-permute-start | bytes 61448
  510.4 12.1 %collective-permute-start.7 = (bf16[16,640]{1,0:T(8,128)(2,1)S(1)}, bf16[16,640]{1,0:T(8,128)(2,1)S(1)}, u32[]{:S(2)}, u32[]{:S(2)}) collective-permute-start(bf16[16,640]{1,0:T(8,128)(2,1)S(1)} %convert.31), channel_id=1, source_target_pairs={{0,64},{8,72},{16,80},{24,88},{32,96},{40,104},{48,112},{56,120},{... | collective-permute-start | bytes 61448
  513.5 9.0 %collective-permute-start.8 = (bf16[16,640]{1,0:T(8,128)(2,1)S(1)}, bf16[16,640]{1,0:T(8,128)(2,1)S(1)}, u32[]{:S(2)}, u32[]{:S(2)}) collective-permute-start(bf16[16,640]{1,0:T(8,128)(2,1)S(1)} %convert.31), channel_id=1, source_target_pairs={{0,72},{8,80},{16,88},{24,96},{32,104},{40,112},{48,120},{56,128},... | collective-permute-start | bytes 61448
  516.9 5.6 %collective-permute-start.9 = (bf16[16,640]{1,0:T(8,128)(2,1)S(1)}, bf16[16,640]{1,0:T(8,128)(2,1)S(1)}, u32[]{:S(2)}, u32[]{:S(2)}) collective-permute-start(bf16[16,640]{1,0:T(8,128)(2,1)S(1)} %convert.31), channel_id=1, source_target_pairs={{0,80},{8,88},{16,96},{24,104},{32,112},{40,120},{48,128},{56,136}... | collective-permute-start | bytes 61448
  522.5 10.4 %copy-start.2 = (bf16[768,432]{0,1:T(8,128)(2,1)S(1)}, bf16[768,432]{0,1:T(8,128)(2,1)}, u32[]{:S(2)}) copy-start(bf16[768,432]{0,1:T(8,128)(2,1)} %copy-done.1) | copy-start | bytes 1990660
  526.4 19.5 %all-to-all-start = ((bf16[64,2,640]{2,1,0:T(2,128)(2,1)}), bf16[64,2,640]{2,1,0:T(2,128)(2,1)S(1)}, u32[]{:S(2)}, u32[]{:S(2)}) async-start(bf16[64,2,640]{2,1,0:T(2,128)(2,1)} %copy.28), calls=%async_computation | async-start | bytes 327680 | tf_op jit(solution)/shard_map/all_to_all | solution.py:94
  532.9 1.5 copy-start.4
Sparse Core Ops, SparseCore 0:
  192.7 106.0 all-reduce.4
where the time goes:
time: 554 us
  blocking collectives  331 us (60%)
  waiting for transfers between devices  116 us (21%)
  starting transfers between devices  59.7 us (11%)
  between operations  15.8 us (3%)
  matrix products  15.3 us (3%)
  local copies, waits for them, and re-layouts  8.5 us (2%)
  other arithmetic  7.12 us (1%)
    unnamed x1, blocking collectives  158 us
    psum x1, waiting for transfers between devices, body(): lax.psum((gate_value, up_value, back_hidden), 'fsdp')  106 us
    all_gather x1, blocking collectives, body(): all_in = lax.all_gather(inputs_kept, 'dp', axis=0, tiled=True)  93.6 us
    all_gather x1, blocking collectives, body(): all_up = lax.all_gather(upstream_kept, 'dp', axis=0, tiled=True)  80 us
    unnamed x16, starting transfers between devices  53.1 us
  transfers between devices with their start and end apart: 18, of which 2 were waited for; matrix products, arithmetic and copies ran while one was open for 2% of the time, Pallas kernels for 0%

commit v1 on v0

v1 whole, which is shorter than its diff:
```python
import jax
import jax.numpy as jnp
from jax import lax
from jax.sharding import PartitionSpec as P

LANES = 128
CORES = 2
Y_CHIPS = 8
Z_CHIPS = 4
BF16 = jnp.bfloat16
F32 = jnp.float32
SUM_TYPE = jnp.bfloat16


def dp_index(z, y, c):
    return (z * Y_CHIPS + y) * CORES + c


Z_GROUPS = [
    [dp_index(z, y, c) for z in range(Z_CHIPS)] for y in range(Y_CHIPS) for c in range(CORES)
]
Y_GROUPS = [
    [dp_index(z, y, c) for y in range(Y_CHIPS)] for z in range(Z_CHIPS) for c in range(CORES)
]


def exchange(x, axis, groups=None):
    return lax.all_to_all(x, axis, 0, 0, tiled=True, axis_index_groups=groups)


def copies(x, count):
    return jnp.broadcast_to(x[None], (count,) + x.shape)


def dense(x):
    n, rows, columns = x.shape
    tiles = columns // LANES
    x = x.reshape(n, rows, tiles, LANES).transpose(0, 2, 1, 3).reshape(n, tiles * rows, LANES)
    return jnp.pad(x, ((0, 0), (0, -(tiles * rows) % 16), (0, 0)))


def undense(x, rows):
    n, flat, _ = x.shape
    tiles = flat // rows
    x = x[:, : tiles * rows].reshape(n, tiles, rows, LANES).transpose(0, 2, 1, 3)
    return x.reshape(n, rows, tiles * LANES)


def body(inputs, upstream, w_gate, w_up, w_down, lengths, move_dest):
    members = lax.axis_size("dp")
    shards = lax.axis_size("fsdp")
    core = lax.axis_index("dp") % CORES
    capacity, features = inputs.shape
    hidden_units = w_gate.shape[1]
    heavy = members // 4
    rows = members * 4 + heavy * 2
    shard_rows = rows // shards
    width = 3 * hidden_units
    padding = -width % LANES

    is_full = lengths == capacity
    full_rank = jnp.cumsum(is_full.astype(jnp.int32)) - is_full
    learner = jnp.arange(members, dtype=jnp.int32)[:, None]
    row = jnp.arange(capacity, dtype=jnp.int32)[None, :]
    target = jnp.repeat(move_dest, 2, axis=1)
    target = jnp.concatenate([jnp.zeros_like(target), target], axis=1)
    place = jnp.where(
        row < 2,
        learner * 4 + row,
        jnp.where(
            row < 4,
            members * 4 + full_rank[:, None] * 2 + row - 2,
            jnp.where(row < 6, learner * 4 + row - 2, target * 4 + 2 + row % 2),
        ),
    )
    place = jnp.where(row < lengths[:, None], place, -1)
    place = place.reshape(Z_CHIPS, Y_CHIPS, CORES, capacity).transpose(2, 1, 0, 3)
    place = jnp.where(core == 0, place[0], place[1]).reshape(-1)
    pick = (jnp.arange(rows, dtype=jnp.int32)[:, None] == place[None, :]).astype(BF16)
    spread = (
        is_full[:, None] & (full_rank[:, None] == jnp.arange(heavy, dtype=jnp.int32)[None, :])
    ).astype(BF16)
    grad_scale = lax.rsqrt(jnp.sum(lengths).astype(F32))

    both = jnp.concatenate([inputs, upstream], axis=1)[None]
    with jax.named_scope("gather_z"):
        got = exchange(copies(dense(both)[0], Z_CHIPS), "dp", Z_GROUPS)
        got = undense(got, capacity).reshape(1, Z_CHIPS * capacity, 2 * features)
    with jax.named_scope("gather_y"):
        got = exchange(copies(dense(got)[0], Y_CHIPS), "dp", Y_GROUPS)
        got = undense(got, Z_CHIPS * capacity).reshape(-1, 2 * features)
    with jax.named_scope("gather_core"):
        mine = jnp.dot(pick, got, preferred_element_type=F32).astype(BF16)
        other = lax.ppermute(mine, "dp", [(i, i ^ 1) for i in range(members)])
        kept = mine + other
    kept_in, kept_up = kept[:, :features], kept[:, features:]

    w_in = jnp.concatenate([w_gate, w_up], axis=1)
    with jax.named_scope("partial_sums"):
        partial_in = jnp.dot(kept_in, w_in, preferred_element_type=F32)
        partial_back = lax.dot_general(
            kept_up, w_down, (((1,), (1,)), ((), ())), preferred_element_type=F32
        )
        partial = jnp.concatenate(
            [partial_in, partial_back, jnp.zeros((rows, padding), F32)], axis=1
        ).astype(SUM_TYPE)
        partial = dense(partial.reshape(shards, shard_rows, width + padding))
    with jax.named_scope("sum_features"):
        parts = exchange(partial, "fsdp")
        total = undense(jnp.sum(parts.astype(F32), axis=0, keepdims=True), shard_rows)[0]
    gate_value = total[:, :hidden_units]
    up_value = total[:, hidden_units : 2 * hidden_units]
    back_hidden = total[:, 2 * hidden_units : width]
    with jax.named_scope("activation"):
        sigmoid_gate = jax.nn.sigmoid(gate_value)
        activated = gate_value * sigmoid_gate
        hidden = (activated * up_value).astype(BF16)
        grad_gate_hidden = (
            back_hidden * up_value * sigmoid_gate * (1.0 + gate_value * (1.0 - sigmoid_gate))
        ).astype(BF16)
        grad_up_hidden = (back_hidden * activated).astype(BF16)
        shard = jnp.concatenate(
            [
                grad_gate_hidden,
                grad_up_hidden,
                hidden,
                jnp.zeros((shard_rows, padding), BF16),
            ],
            axis=1,
        )
    with jax.named_scope("gather_hidden"):
        all_hidden = exchange(copies(dense(shard[None])[0], shards), "fsdp")
        all_hidden = undense(all_hidden, shard_rows).reshape(rows, width + padding)
    grad_in_hidden = all_hidden[:, : 2 * hidden_units]
    hidden = all_hidden[:, 2 * hidden_units : width]

    with jax.named_scope("grad_rows"):
        grad_rows = lax.dot_general(
            grad_in_hidden, w_in, (((1,), (1,)), ((), ())), preferred_element_type=F32
        ).astype(BF16)
        outer = grad_rows[: members * 4].reshape(members, 2, 2, features)
        middle = jnp.einsum(
            "lh,htf->ltf",
            spread,
            grad_rows[members * 4 :].reshape(heavy, 2, features),
            preferred_element_type=F32,
        ).astype(BF16)
        slots = jnp.stack([outer[:, 0], middle, outer[:, 1]], axis=1).reshape(members, 6, features)
        arrived = exchange(dense(slots), "dp")
        grad_inputs = undense(jnp.sum(arrived.astype(F32), axis=0, keepdims=True), 6)[0].astype(BF16)

    contract_rows = (((0,), (0,)), ((), ()))
    with jax.named_scope("grad_weights"):
        in_total = lax.dot_general(
            kept_in, grad_in_hidden, contract_rows, preferred_element_type=F32
        )
        grad_in = (in_total * grad_scale).astype(BF16)
        down_total = lax.dot_general(hidden, kept_up, contract_rows, preferred_element_type=F32)
        grad_down = (down_total * grad_scale).astype(BF16)
    return (grad_inputs, grad_in[:, :hidden_units], grad_in[:, hidden_units:], grad_down)


def solution(mesh):
    in_specs = (
        P("dp", "fsdp"),
        P("dp", "fsdp"),
        P("fsdp", "dp"),
        P("fsdp", "dp"),
        P("dp", "fsdp"),
        P(),
        P(),
    )
    out_specs = (P("dp", "fsdp"), P("fsdp", "dp"), P("fsdp", "dp"), P("dp", "fsdp"))
    return jax.shard_map(body, mesh=mesh, in_specs=in_specs, out_specs=out_specs, check_vma=False)
```

time: 554 us -> 129 us (0.23)
  blocking collectives: 331 us -> 50.2 us
  waiting for transfers between devices: 116 us -> 40.3 us
  starting transfers between devices: 59.7 us -> 18.3 us
  between operations: 15.8 us -> 1.83 us
  matrix products: 15.3 us -> 4.9 us
    all_gather x2 -> x0, blocking collectives: 174 us -> none  [the longest x1 93.6 us: body(): all_in = lax.all_gather(inputs_kept, 'dp', axis=0, tiled=True)]
    unnamed x1 -> x0, blocking collectives: 158 us -> none
    psum x1 -> x0, waiting for transfers between devices: 106 us -> none  [body(): lax.psum((gate_value, up_value, back_hidden), 'fsdp')]
    unnamed x16 -> x0, starting transfers between devices: 53.1 us -> none
    all_to_all x0 -> x3, blocking collectives: none -> 50.2 us  [exchange(): return lax.all_to_all(x, axis, 0, 0, tiled=True, axis_index_groups=groups)]
    all_to_all x1 -> x2, waiting for transfers between devices: 9.96 us -> 38.7 us  [exchange(): return lax.all_to_all(x, axis, 0, 0, tiled=True, axis_index_groups=groups)]
    dot_general x10 -> x7, matrix products: 15.3 us -> 4.9 us  [the longest x1 1.55 us: body(): lax.dot_general(hidden, kept_up, contract_rows, preferred_element_type=F32)]
    all_to_all x1 -> x2, starting transfers between devices: 6.5 us -> 13.6 us  [exchange(): return lax.all_to_all(x, axis, 0, 0, tiled=True, axis_index_groups=groups)]
  transfers between devices with their start and end apart: 18 -> 3, of which waited for: 2 -> 3; matrix products, arithmetic and copies ran while one was open for 2% -> 4% of each run, Pallas kernels for 0% -> 0%
where the time goes in v1:
time: 129 us; the launch traced here: 128 us
  blocking collectives  50.2 us (39%)
  waiting for transfers between devices  40.3 us (31%)
  starting transfers between devices  18.3 us (14%)
  local copies, waits for them, and re-layouts  10.2 us (8%)
  matrix products  4.9 us (4%)
  other arithmetic  2.34 us (2%)
  between operations  1.83 us (1%)
    all_to_all x3, blocking collectives, exchange(): return lax.all_to_all(x, axis, 0, 0, tiled=True, axis_index_groups=groups)  50.2 us
    all_to_all x2, waiting for transfers between devices, exchange(): return lax.all_to_all(x, axis, 0, 0, tiled=True, axis_index_groups=groups)  38.7 us
    all_to_all x2, starting transfers between devices, exchange(): return lax.all_to_all(x, axis, 0, 0, tiled=True, axis_index_groups=groups)  13.6 us
    ppermute x1, starting transfers between devices, body(): other = lax.ppermute(mine, 'dp', [(i, i ^ 1) for i in range(members)])  4.74 us
  transfers between devices with their start and end apart: 3, of which 3 were waited for; matrix products, arithmetic and copies ran while one was open for 4% of the time, Pallas kernels for 0%

profile of v1, /device:TPU:1, one launch (start us, length us, event | category | flops | bytes accessed | tf_op | source)
XLA Modules:
  0.0 128.2 jit_solution(6000247361509094582)
XLA Ops:
  0.6 0.8 pad_maximum_fusion.1
  1.6 18.2 %all_to_all.25 = bf16[4,128,128]{2,1,0:T(8,128)(2,1)S(1)} all-to-all(bf16[4,128,128]{2,1,0:T(8,128)(2,1)S(1)} %broadcast_in_dim.77), channel_id=1, replica_groups={{0,128,256,384},{8,136,264,392},{16,144,272,400},{24,152,280,408},{32,1..., dimensions={0} | all-to-all | bytes 262144 | tf_op jit(solution)/shard_map/gather_z/all_to_all | solution.py:28
  19.9 1.1 broadcast_in_dim.79
  21.0 7.0 %all-to-all-start.1 = ((bf16[8,480,128]{2,1,0:T(8,128)(2,1)}), bf16[8,480,128]{2,1,0:T(8,128)(2,1)S(1)}, u32[]{:S(2)}, u32[]{:S(2)}) async-start(bf16[8,480,128]{2,1,0:T(8,128)(2,1)} %broadcast_in_dim.79), calls=%async_computation.1 | async-start | bytes 1966080 | tf_op jit(solution)/shard_map/gather_y/all_to_all | solution.py:28
  28.4 0.6 multiply_add_fusion
  29.3 24.1 %all-to-all-done.1 = bf16[8,480,128]{2,1,0:T(8,128)(2,1)S(1)} async-done(((bf16[8,480,128]{2,1,0:T(8,128)(2,1)}), bf16[8,480,128]{2,1,0:T(8,128)(2,1)S(1)}, u32[]{:S(2)}, u32[]{:S(2)}) %all-to-all-start.1) | async-done | bytes 983072 | tf_op jit(solution)/shard_map/gather_y/all_to_all | solution.py:28
  53.5 0.4 copy.48
  53.9 0.6 convolution_convert_fusion
  54.4 4.7 %collective-permute-start = (bf16[288,1280]{1,0:T(8,128)(2,1)S(1)}, bf16[288,1280]{1,0:T(8,128)(2,1)S(1)}, u32[]{:S(2)}, u32[]{:S(2)}) collective-permute-start(bf16[288,1280]{1,0:T(8,128)(2,1)S(1)} %convolution_convert_fusion), channel_id=1, source_target_pairs={{0,8},{8,0},{16,24},{24,16},{32,40},{40,32},{48,56},{56,48},{64,72... | collective-permute-start | bytes 2211848 | tf_op jit(solution)/shard_map/gather_core/ppermute | solution.py:94
  59.4 1.6 %collective-permute-done = bf16[288,1280]{1,0:T(8,128)(2,1)S(1)} collective-permute-done((bf16[288,1280]{1,0:T(8,128)(2,1)S(1)}, bf16[288,1280]{1,0:T(8,128)(2,1)S(1)}, u32[]{:S(2)}, u32[]{:S(2)}) %collective-permute-start) | collective-permute-done | bytes 737312 | tf_op jit(solution)/shard_map/gather_core/ppermute | solution.py:94
  61.2 0.7 convolution_convert_fusion.1
  61.9 0.4 convolution_convert_fusion.3
  62.3 0.5 concatenate.19
  62.8 0.5 convert_element_type.64
  63.3 0.6 copy.49
  64.1 17.1 %all_to_all.26 = bf16[8,400,128]{2,1,0:T(8,128)(2,1)S(1)} all-to-all(bf16[8,400,128]{2,1,0:T(8,128)(2,1)S(1)} %pad.18.clone), channel_id=1, replica_groups=mesh['dp'=64,'fsdp'=8] {'fsdp'}, dimensions={0} | all-to-all | bytes 1638400 | tf_op jit(solution)/shard_map/sum_features/all_to_all | solution.py:28
  82.1 14.9 %all_to_all.27 = bf16[8,400,128]{2,1,0:T(8,128)(2,1)S(1)} all-to-all(bf16[8,400,128]{2,1,0:T(8,128)(2,1)S(1)} %broadcast_in_dim.85), channel_id=1, replica_groups=mesh['dp'=64,'fsdp'=8] {'fsdp'}, dimensions={0} | all-to-all | bytes 1638400 | tf_op jit(solution)/shard_map/gather_hidden/all_to_all | solution.py:28
  97.2 0.4 copy.54
  97.6 0.2 copy.76
  97.8 1.0 copy-done.4
  98.8 0.6 convolution_convert_fusion.2
  99.6 0.2 fusion.20
  99.9 0.3 fusion.1
  100.3 0.6 reshape.163
  100.9 0.3 copy.64
  101.3 0.9 pad.20.clone
  102.1 6.6 %all-to-all-start.4 = ((bf16[64,32,128]{2,1,0:T(8,128)(2,1)}), bf16[64,32,128]{2,1,0:T(8,128)(2,1)S(1)}, u32[]{:S(2)}, u32[]{:S(2)}) async-start(bf16[64,32,128]{2,1,0:T(8,128)(2,1)} %pad.20.clone), calls=%async_computation.4 | async-start | bytes 1048576 | tf_op jit(solution)/shard_map/grad_rows/all_to_all | solution.py:28
  109.4 1.6 %fusion = bf16[432,640]{1,0:T(8,128)(2,1)} fusion(f32[]{:T(128)S(6)} %rsqrt.3, bf16[288,1280]{1,0:T(8,128)(2,1)S(1)} %add.98, bf16[288,1408]{1,0:T(8,128)(2,1)S(1)} %bitcast.84), kind=kOutput, calls=%fused_computation.4 | convolution fusion | flops 159805440 | bytes 1216516 | tf_op jit(solution)/shard_map/grad_weights/dot_general | solution.py:158
  111.0 0.8 multiply_convert_fusion
  111.9 1.1 fusion.19
  112.9 14.5 %all-to-all-done.4 = bf16[64,32,128]{2,1,0:T(8,128)(2,1)S(1)} async-done(((bf16[64,32,128]{2,1,0:T(8,128)(2,1)}), bf16[64,32,128]{2,1,0:T(8,128)(2,1)S(1)}, u32[]{:S(2)}, u32[]{:S(2)}) %all-to-all-start.4) | async-done | bytes 524320 | tf_op jit(solution)/shard_map/grad_rows/all_to_all | solution.py:28
  127.6 0.6 convert_element_type.72
  (65 shorter events, 2.8 us)
Async XLA Ops:
  0.6 61.2 %copy-start = (bf16[432,640]{1,0:T(8,128)(2,1)S(1)}, bf16[432,640]{1,0:T(8,128)(2,1)}, u32[]{:S(2)}) copy-start(bf16[432,640]{1,0:T(8,128)(2,1)} %param.11) | copy-start | bytes 1658884
  21.0 7.0 %copy-start.5 = (s32[64,3]{0,1:T(4,128)S(1)}, s32[64,3]{0,1:T(4,128)}, u32[]{:S(2)}) copy-start(s32[64,3]{0,1:T(4,128)} %param.13) | copy-start | bytes 2308
  21.0 7.0 %copy-start.6 = (s32[64]{0:T(128)S(1)}, s32[64]{0:T(128)}, u32[]{:S(2)}) copy-start(s32[64]{0:T(128)} %param.12) | copy-start | bytes 772
  21.0 32.4 %all-to-all-start.1 = ((bf16[8,480,128]{2,1,0:T(8,128)(2,1)}), bf16[8,480,128]{2,1,0:T(8,128)(2,1)S(1)}, u32[]{:S(2)}, u32[]{:S(2)}) async-start(bf16[8,480,128]{2,1,0:T(8,128)(2,1)} %broadcast_in_dim.79), calls=%async_computation.1 | async-start | bytes 1966080 | tf_op jit(solution)/shard_map/gather_y/all_to_all | solution.py:28
  53.8 5.4 %copy-start.1 = (bf16[640,432]{0,1:T(8,128)(2,1)S(1)}, bf16[640,432]{0,1:T(8,128)(2,1)}, u32[]{:S(2)}) copy-start(bf16[640,432]{0,1:T(8,128)(2,1)} %param.9) | copy-start | bytes 1658884
  53.9 5.4 %copy-start.2 = (bf16[640,432]{0,1:T(8,128)(2,1)S(1)}, bf16[640,432]{0,1:T(8,128)(2,1)}, u32[]{:S(2)}) copy-start(bf16[640,432]{0,1:T(8,128)(2,1)} %param.10) | copy-start | bytes 1658884
  54.4 6.6 %collective-permute-start = (bf16[288,1280]{1,0:T(8,128)(2,1)S(1)}, bf16[288,1280]{1,0:T(8,128)(2,1)S(1)}, u32[]{:S(2)}, u32[]{:S(2)}) collective-permute-start(bf16[288,1280]{1,0:T(8,128)(2,1)S(1)} %convolution_convert_fusion), channel_id=1, source_target_pairs={{0,8},{8,0},{16,24},{24,16},{32,40},{40,32},{48,56},{56,48},{64,72... | collective-permute-start | bytes 2211848 | tf_op jit(solution)/shard_map/gather_core/ppermute | solution.py:94
  59.4 1.8 %copy-start.3 = (bf16[640,864]{0,1:T(8,128)(2,1)}, bf16[640,864]{0,1:T(8,128)(2,1)S(1)}, u32[]{:S(2)}) copy-start(bf16[640,864]{0,1:T(8,128)(2,1)S(1)} %constant_dynamic-update-slice_fusion) | copy-start | bytes 3317764
  97.6 1.2 copy-start.4
  102.1 25.3 %all-to-all-start.4 = ((bf16[64,32,128]{2,1,0:T(8,128)(2,1)}), bf16[64,32,128]{2,1,0:T(8,128)(2,1)S(1)}, u32[]{:S(2)}, u32[]{:S(2)}) async-start(bf16[64,32,128]{2,1,0:T(8,128)(2,1)} %pad.20.clone), calls=%async_computation.4 | async-start | bytes 1048576 | tf_op jit(solution)/shard_map/grad_rows/all_to_all | solution.py:28

commit v2 on v1

--- a/solution.py
+++ b/solution.py
@@ -5,22 +5,13 @@
 
 LANES = 128
 CORES = 2
-Y_CHIPS = 8
-Z_CHIPS = 4
 BF16 = jnp.bfloat16
 F32 = jnp.float32
 SUM_TYPE = jnp.bfloat16
 
 
-def dp_index(z, y, c):
-    return (z * Y_CHIPS + y) * CORES + c
-
-
-Z_GROUPS = [
-    [dp_index(z, y, c) for z in range(Z_CHIPS)] for y in range(Y_CHIPS) for c in range(CORES)
-]
-Y_GROUPS = [
-    [dp_index(z, y, c) for y in range(Y_CHIPS)] for z in range(Z_CHIPS) for c in range(CORES)
+CORE_GROUPS = [
+    [chip * CORES + core for chip in range(32)] for core in range(CORES)
 ]
 
 
@@ -36,7 +27,7 @@
     n, rows, columns = x.shape
     tiles = columns // LANES
     x = x.reshape(n, rows, tiles, LANES).transpose(0, 2, 1, 3).reshape(n, tiles * rows, LANES)
-    return jnp.pad(x, ((0, 0), (0, -(tiles * rows) % 16), (0, 0)))
+    return jnp.pad(x, ((0, 0), (0, -(tiles * rows) % 8), (0, 0)))
 
 
 def undense(x, rows):
@@ -74,7 +65,7 @@
         ),
     )
     place = jnp.where(row < lengths[:, None], place, -1)
-    place = place.reshape(Z_CHIPS, Y_CHIPS, CORES, capacity).transpose(2, 1, 0, 3)
+    place = place.reshape(-1, CORES, capacity).transpose(1, 0, 2)
     place = jnp.where(core == 0, place[0], place[1]).reshape(-1)
     pick = (jnp.arange(rows, dtype=jnp.int32)[:, None] == place[None, :]).astype(BF16)
     spread = (
@@ -83,12 +74,9 @@
     grad_scale = lax.rsqrt(jnp.sum(lengths).astype(F32))
 
     both = jnp.concatenate([inputs, upstream], axis=1)[None]
-    with jax.named_scope("gather_z"):
-        got = exchange(copies(dense(both)[0], Z_CHIPS), "dp", Z_GROUPS)
-        got = undense(got, capacity).reshape(1, Z_CHIPS * capacity, 2 * features)
-    with jax.named_scope("gather_y"):
-        got = exchange(copies(dense(got)[0], Y_CHIPS), "dp", Y_GROUPS)
-        got = undense(got, Z_CHIPS * capacity).reshape(-1, 2 * features)
+    with jax.named_scope("gather_chips"):
+        got = exchange(copies(dense(both)[0], members // CORES), "dp", CORE_GROUPS)
+        got = undense(got, capacity).reshape(-1, 2 * features)
     with jax.named_scope("gather_core"):
         mine = jnp.dot(pick, got, preferred_element_type=F32).astype(BF16)
         other = lax.ppermute(mine, "dp", [(i, i ^ 1) for i in range(members)])

time: 129 us -> 125 us (0.969)
  blocking collectives: 50.2 us -> 32.4 us
  starting transfers between devices: 18.3 us -> 32.4 us
    all_to_all x3 -> x2, blocking collectives: 50.2 us -> 32.4 us  [exchange(): return lax.all_to_all(x, axis, 0, 0, tiled=True, axis_index_groups=groups)]
    all_to_all x2, starting transfers between devices: 13.6 us -> 26.5 us  [exchange(): return lax.all_to_all(x, axis, 0, 0, tiled=True, axis_index_groups=groups)]
where the time goes in v2:
time: 125 us; the launch traced here: 124 us
  waiting for transfers between devices  40 us (32%)
  starting transfers between devices  32.4 us (26%)
  blocking collectives  32.4 us (26%)
  local copies, waits for them, and re-layouts  10.6 us (8%)
  matrix products  4.89 us (4%)
  other arithmetic  2.37 us (2%)
  between operations  1.82 us (1%)
    all_to_all x2, waiting for transfers between devices, exchange(): return lax.all_to_all(x, axis, 0, 0, tiled=True, axis_index_groups=groups)  38.4 us
    all_to_all x2, blocking collectives, exchange(): return lax.all_to_all(x, axis, 0, 0, tiled=True, axis_index_groups=groups)  32.4 us
    all_to_all x2, starting transfers between devices, exchange(): return lax.all_to_all(x, axis, 0, 0, tiled=True, axis_index_groups=groups)  26.5 us
    ppermute x1, starting transfers between devices, body(): other = lax.ppermute(mine, 'dp', [(i, i ^ 1) for i in range(members)])  5.88 us
  transfers between devices with their start and end apart: 3, of which 3 were waited for; matrix products, arithmetic and copies ran while one was open for 4% of the time, Pallas kernels for 0%

profile of v2, /device:TPU:1, one launch (start us, length us, event | category | flops | bytes accessed | tf_op | source)
XLA Modules:
  0.0 124.4 jit_solution(13007657564818325600)
XLA Ops:
  0.6 0.8 pad_maximum_fusion.1
  1.5 1.1 broadcast_in_dim.70
  2.6 16.6 %all-to-all-start = ((bf16[32,120,128]{2,1,0:T(8,128)(2,1)}), bf16[32,120,128]{2,1,0:T(8,128)(2,1)S(1)}, u32[]{:S(2)}, u32[]{:S(2)}) async-start(bf16[32,120,128]{2,1,0:T(8,128)(2,1)} %broadcast_in_dim.70), calls=%async_computation | async-start | bytes 1966080 | tf_op jit(solution)/shard_map/gather_chips/all_to_all | solution.py:19
  19.7 0.6 multiply_add_fusion
  20.7 23.9 %all-to-all-done = bf16[32,120,128]{2,1,0:T(8,128)(2,1)S(1)} async-done(((bf16[32,120,128]{2,1,0:T(8,128)(2,1)}), bf16[32,120,128]{2,1,0:T(8,128)(2,1)S(1)}, u32[]{:S(2)}, u32[]{:S(2)}) %all-to-all-start) | async-done | bytes 983072 | tf_op jit(solution)/shard_map/gather_chips/all_to_all | solution.py:19
  44.7 0.7 copy.32
  45.5 0.6 convolution_convert_fusion
  46.1 5.9 %collective-permute-start = (bf16[288,1280]{1,0:T(8,128)(2,1)S(1)}, bf16[288,1280]{1,0:T(8,128)(2,1)S(1)}, u32[]{:S(2)}, u32[]{:S(2)}) collective-permute-start(bf16[288,1280]{1,0:T(8,128)(2,1)S(1)} %convolution_convert_fusion), channel_id=1, source_target_pairs={{0,8},{8,0},{16,24},{24,16},{32,40},{40,32},{48,56},{56,48},{64,72... | collective-permute-start | bytes 2211848 | tf_op jit(solution)/shard_map/gather_core/ppermute | solution.py:82
  52.1 1.6 %collective-permute-done = bf16[288,1280]{1,0:T(8,128)(2,1)S(1)} collective-permute-done((bf16[288,1280]{1,0:T(8,128)(2,1)S(1)}, bf16[288,1280]{1,0:T(8,128)(2,1)S(1)}, u32[]{:S(2)}, u32[]{:S(2)}) %collective-permute-start) | collective-permute-done | bytes 737312 | tf_op jit(solution)/shard_map/gather_core/ppermute | solution.py:82
  54.0 0.7 convolution_convert_fusion.1
  54.6 0.4 convolution_convert_fusion.3
  55.1 0.5 concatenate.19
  55.6 0.5 convert_element_type.62
  56.1 0.6 copy.33
  56.8 17.8 %all_to_all.20 = bf16[8,400,128]{2,1,0:T(8,128)(2,1)S(1)} all-to-all(bf16[8,400,128]{2,1,0:T(8,128)(2,1)S(1)} %pad.13.clone), channel_id=1, replica_groups=mesh['dp'=64,'fsdp'=8] {'fsdp'}, dimensions={0} | all-to-all | bytes 1638400 | tf_op jit(solution)/shard_map/sum_features/all_to_all | solution.py:19
  75.5 14.6 %all_to_all.21 = bf16[8,400,128]{2,1,0:T(8,128)(2,1)S(1)} all-to-all(bf16[8,400,128]{2,1,0:T(8,128)(2,1)S(1)} %broadcast_in_dim.76), channel_id=1, replica_groups=mesh['dp'=64,'fsdp'=8] {'fsdp'}, dimensions={0} | all-to-all | bytes 1638400 | tf_op jit(solution)/shard_map/gather_hidden/all_to_all | solution.py:19
  90.1 0.2 copy.44
  90.3 0.4 copy.38
  90.7 0.2 copy.60
  90.9 1.0 copy-done.4
  91.9 0.6 convolution_convert_fusion.2
  92.7 0.2 fusion.21
  93.0 0.3 fusion.1
  93.4 0.6 reshape.151
  94.1 0.3 copy.48
  94.4 0.9 pad.15.clone
  95.2 9.8 %all-to-all-start.3 = ((bf16[64,32,128]{2,1,0:T(8,128)(2,1)}), bf16[64,32,128]{2,1,0:T(8,128)(2,1)S(1)}, u32[]{:S(2)}, u32[]{:S(2)}) async-start(bf16[64,32,128]{2,1,0:T(8,128)(2,1)} %pad.15.clone), calls=%async_computation.3 | async-start | bytes 1048576 | tf_op jit(solution)/shard_map/grad_rows/all_to_all | solution.py:19
  105.8 1.5 %fusion = bf16[432,640]{1,0:T(8,128)(2,1)} fusion(f32[]{:T(128)S(6)} %rsqrt.3, bf16[288,1280]{1,0:T(8,128)(2,1)S(1)} %add.96, bf16[288,1408]{1,0:T(8,128)(2,1)S(1)} %bitcast.74), kind=kOutput, calls=%fused_computation.4 | convolution fusion | flops 159805440 | bytes 1216516 | tf_op jit(solution)/shard_map/grad_weights/dot_general | solution.py:146
  107.3 0.8 multiply_convert_fusion
  108.2 1.1 fusion.20
  109.3 14.4 %all-to-all-done.3 = bf16[64,32,128]{2,1,0:T(8,128)(2,1)S(1)} async-done(((bf16[64,32,128]{2,1,0:T(8,128)(2,1)}), bf16[64,32,128]{2,1,0:T(8,128)(2,1)S(1)}, u32[]{:S(2)}, u32[]{:S(2)}) %all-to-all-start.3) | async-done | bytes 524320 | tf_op jit(solution)/shard_map/grad_rows/all_to_all | solution.py:19
  123.8 0.6 convert_element_type.70
  (58 shorter events, 2.7 us)
Async XLA Ops:
  0.6 54.0 %copy-start = (bf16[432,640]{1,0:T(8,128)(2,1)S(1)}, bf16[432,640]{1,0:T(8,128)(2,1)}, u32[]{:S(2)}) copy-start(bf16[432,640]{1,0:T(8,128)(2,1)} %param.11) | copy-start | bytes 1658884
  2.6 16.7 %copy-start.5 = (s32[64,3]{0,1:T(4,128)S(1)}, s32[64,3]{0,1:T(4,128)}, u32[]{:S(2)}) copy-start(s32[64,3]{0,1:T(4,128)} %param.13) | copy-start | bytes 2308
  2.6 16.7 %copy-start.6 = (s32[64]{0:T(128)S(1)}, s32[64]{0:T(128)}, u32[]{:S(2)}) copy-start(s32[64]{0:T(128)} %param.12) | copy-start | bytes 772
  2.6 42.0 %all-to-all-start = ((bf16[32,120,128]{2,1,0:T(8,128)(2,1)}), bf16[32,120,128]{2,1,0:T(8,128)(2,1)S(1)}, u32[]{:S(2)}, u32[]{:S(2)}) async-start(bf16[32,120,128]{2,1,0:T(8,128)(2,1)} %broadcast_in_dim.70), calls=%async_computation | async-start | bytes 1966080 | tf_op jit(solution)/shard_map/gather_chips/all_to_all | solution.py:19
  45.5 6.5 %copy-start.1 = (bf16[640,432]{0,1:T(8,128)(2,1)S(1)}, bf16[640,432]{0,1:T(8,128)(2,1)}, u32[]{:S(2)}) copy-start(bf16[640,432]{0,1:T(8,128)(2,1)} %param.9) | copy-start | bytes 1658884
  45.5 6.6 %copy-start.2 = (bf16[640,432]{0,1:T(8,128)(2,1)S(1)}, bf16[640,432]{0,1:T(8,128)(2,1)}, u32[]{:S(2)}) copy-start(bf16[640,432]{0,1:T(8,128)(2,1)} %param.10) | copy-start | bytes 1658884
  46.1 7.7 %collective-permute-start = (bf16[288,1280]{1,0:T(8,128)(2,1)S(1)}, bf16[288,1280]{1,0:T(8,128)(2,1)S(1)}, u32[]{:S(2)}, u32[]{:S(2)}) collective-permute-start(bf16[288,1280]{1,0:T(8,128)(2,1)S(1)} %convolution_convert_fusion), channel_id=1, source_target_pairs={{0,8},{8,0},{16,24},{24,16},{32,40},{40,32},{48,56},{56,48},{64,72... | collective-permute-start | bytes 2211848 | tf_op jit(solution)/shard_map/gather_core/ppermute | solution.py:82
  52.1 2.5 %copy-start.3 = (bf16[640,864]{0,1:T(8,128)(2,1)}, bf16[640,864]{0,1:T(8,128)(2,1)S(1)}, u32[]{:S(2)}) copy-start(bf16[640,864]{0,1:T(8,128)(2,1)S(1)} %constant_dynamic-update-slice_fusion) | copy-start | bytes 3317764
  90.7 1.2 %copy-start.4 = (bf16[640,864]{0,1:T(8,128)(2,1)S(1)}, bf16[640,864]{0,1:T(8,128)(2,1)}, u32[]{:S(2)}) copy-start(bf16[640,864]{0,1:T(8,128)(2,1)} %copy-done.3) | copy-start | bytes 3317764
  95.2 28.4 %all-to-all-start.3 = ((bf16[64,32,128]{2,1,0:T(8,128)(2,1)}), bf16[64,32,128]{2,1,0:T(8,128)(2,1)S(1)}, u32[]{:S(2)}, u32[]{:S(2)}) async-start(bf16[64,32,128]{2,1,0:T(8,128)(2,1)} %pad.15.clone), calls=%async_computation.3 | async-start | bytes 1048576 | tf_op jit(solution)/shard_map/grad_rows/all_to_all | solution.py:19

commit v3 on v2

--- a/solution.py
+++ b/solution.py
@@ -10,8 +10,28 @@
 SUM_TYPE = jnp.bfloat16
 
 
-CORE_GROUPS = [
-    [chip * CORES + core for chip in range(32)] for core in range(CORES)
+Y_CHIPS = 8
+Z_CHIPS = 4
+SIDES = 2
+
+
+def dp_index(z, y, core):
+    return (z * Y_CHIPS + y % Y_CHIPS) * CORES + core
+
+
+def moved(dy, dcore):
+    return [
+        (dp_index(z, y, core), dp_index(z, y + dy, core ^ dcore))
+        for z in range(Z_CHIPS)
+        for y in range(Y_CHIPS)
+        for core in range(CORES)
+    ]
+
+
+SIDE_GROUPS = [
+    [dp_index(z, y, core) for z in range(Z_CHIPS) for y in range(side, Y_CHIPS, SIDES)]
+    for side in range(SIDES)
+    for core in range(CORES)
 ]
 
 
@@ -40,7 +60,8 @@
 def body(inputs, upstream, w_gate, w_up, w_down, lengths, move_dest):
     members = lax.axis_size("dp")
     shards = lax.axis_size("fsdp")
-    core = lax.axis_index("dp") % CORES
+    core = lax.axis_index("dp") & 1
+    side = (lax.axis_index("dp") >> 1) & 1
     capacity, features = inputs.shape
     hidden_units = w_gate.shape[1]
     heavy = members // 4
@@ -65,8 +86,9 @@
         ),
     )
     place = jnp.where(row < lengths[:, None], place, -1)
-    place = place.reshape(-1, CORES, capacity).transpose(1, 0, 2)
-    place = jnp.where(core == 0, place[0], place[1]).reshape(-1)
+    place = place.reshape(Z_CHIPS, -1, SIDES, CORES, capacity).transpose(2, 3, 0, 1, 4)
+    place = jnp.where(core == 0, place[:, 0], place[:, 1]).reshape(SIDES, -1)
+    place = jnp.where(side == 0, place, place[::-1]).reshape(-1)
     pick = (jnp.arange(rows, dtype=jnp.int32)[:, None] == place[None, :]).astype(BF16)
     spread = (
         is_full[:, None] & (full_rank[:, None] == jnp.arange(heavy, dtype=jnp.int32)[None, :])
@@ -74,13 +96,17 @@
     grad_scale = lax.rsqrt(jnp.sum(lengths).astype(F32))
 
     both = jnp.concatenate([inputs, upstream], axis=1)[None]
-    with jax.named_scope("gather_chips"):
-        got = exchange(copies(dense(both)[0], members // CORES), "dp", CORE_GROUPS)
+    with jax.named_scope("gather_side"):
+        got = exchange(copies(dense(both)[0], members // (CORES * SIDES)), "dp", SIDE_GROUPS)
+    with jax.named_scope("gather_neighbours"):
+        half = got.shape[0] // 2
+        first = lax.ppermute(got[:half], "dp", moved(-1, 0))
+        second = lax.ppermute(got[half:], "dp", moved(1, 0))
+        got = jnp.concatenate([got, first, second], axis=0)
         got = undense(got, capacity).reshape(-1, 2 * features)
     with jax.named_scope("gather_core"):
         mine = jnp.dot(pick, got, preferred_element_type=F32).astype(BF16)
-        other = lax.ppermute(mine, "dp", [(i, i ^ 1) for i in range(members)])
-        kept = mine + other
+        kept = mine + lax.ppermute(mine, "dp", moved(0, 1))
     kept_in, kept_up = kept[:, :features], kept[:, features:]
 
     w_in = jnp.concatenate([w_gate, w_up], axis=1)

time: 125 us -> 126 us (level)
  starting transfers between devices: 32.4 us -> 36.4 us
  waiting for transfers between devices: 40 us -> 37.9 us
    all_to_all x2, waiting for transfers between devices: 38.4 us -> 30.9 us  [exchange(): return lax.all_to_all(x, axis, 0, 0, tiled=True, axis_index_groups=groups)]
    ppermute x1 -> x3, waiting for transfers between devices: 1.65 us -> 6.99 us  [the longest x1 4.03 us: body(): first = lax.ppermute(got[:half], 'dp', moved(-1, 0))]
    ppermute x1 -> x3, starting transfers between devices: 5.88 us -> 10.3 us  [the longest x1 4.57 us: body(): first = lax.ppermute(got[:half], 'dp', moved(-1, 0))]
  transfers between devices with their start and end apart: 3 -> 5, of which waited for: 3 -> 5; matrix products, arithmetic and copies ran while one was open for 4% -> 4% of each run, Pallas kernels for 0% -> 0%
where the time goes in v3:
time: 126 us
  waiting for transfers between devices  37.9 us (30%)
  starting transfers between devices  36.4 us (29%)
  blocking collectives  31.9 us (25%)
  local copies, waits for them, and re-layouts  10.5 us (8%)
  matrix products  4.9 us (4%)
  other arithmetic  2.5 us (2%)
  between operations  1.89 us (2%)
    all_to_all x2, blocking collectives, exchange(): return lax.all_to_all(x, axis, 0, 0, tiled=True, axis_index_groups=groups)  31.9 us
    all_to_all x2, waiting for transfers between devices, exchange(): return lax.all_to_all(x, axis, 0, 0, tiled=True, axis_index_groups=groups)  30.9 us
    all_to_all x2, starting transfers between devices, exchange(): return lax.all_to_all(x, axis, 0, 0, tiled=True, axis_index_groups=groups)  26.1 us
    ppermute x1, starting transfers between devices, body(): first = lax.ppermute(got[:half], 'dp', moved(-1, 0))  4.57 us
    ppermute x1, waiting for transfers between devices, body(): first = lax.ppermute(got[:half], 'dp', moved(-1, 0))  4.03 us
    ppermute x1, starting transfers between devices, body(): kept = mine + lax.ppermute(mine, 'dp', moved(0, 1))  3.85 us
  transfers between devices with their start and end apart: 5, of which 5 were waited for; matrix products, arithmetic and copies ran while one was open for 4% of the time, Pallas kernels for 0%

profile of v3, /device:TPU:1, one launch (start us, length us, event | category | flops | bytes accessed | tf_op | source)
XLA Modules:
  0.0 126.0 jit_solution(1696128513876590915)
XLA Ops:
  0.7 0.8 pad_maximum_fusion.2
  1.6 0.8 broadcast_in_dim.70
  2.4 16.2 %all-to-all-start = ((bf16[16,120,128]{2,1,0:T(8,128)(2,1)}), bf16[16,120,128]{2,1,0:T(8,128)(2,1)S(1)}, u32[]{:S(2)}, u32[]{:S(2)}) async-start(bf16[16,120,128]{2,1,0:T(8,128)(2,1)} %broadcast_in_dim.70), calls=%async_computation | async-start | bytes 983040 | tf_op jit(solution)/shard_map/gather_side/all_to_all | solution.py:39
  19.0 0.6 multiply_add_fusion
  19.8 16.5 %all-to-all-done = bf16[16,120,128]{2,1,0:T(8,128)(2,1)S(1)} async-done(((bf16[16,120,128]{2,1,0:T(8,128)(2,1)}), bf16[16,120,128]{2,1,0:T(8,128)(2,1)S(1)}, u32[]{:S(2)}, u32[]{:S(2)}) %all-to-all-start) | async-done | bytes 491552 | tf_op jit(solution)/shard_map/gather_side/all_to_all | solution.py:39
  36.5 1.9 %collective-permute-start.1 = (bf16[8,120,128]{2,0,1:T(8,128)(2,1)S(1)}, bf16[8,120,128]{2,0,1:T(8,128)(2,1)S(1)}, u32[]{:S(2)}, u32[]{:S(2)}) collective-permute-start(bf16[8,120,128]{2,0,1:T(8,128)(2,1)S(1)} %get-tuple-element.9), channel_id=1, source_target_pairs={{0,16},{8,24},{16,32},{24,40},{32,48},{40,56},{48,64},{56,72},{64,... | collective-permute-start | bytes 737288 | tf_op jit(solution)/shard_map/gather_neighbours/ppermute | solution.py:104
  38.4 4.6 %collective-permute-start = (bf16[8,120,128]{2,0,1:T(8,128)(2,1)S(1)}, bf16[8,120,128]{2,0,1:T(8,128)(2,1)S(1)}, u32[]{:S(2)}, u32[]{:S(2)}) collective-permute-start(bf16[8,120,128]{2,0,1:T(8,128)(2,1)S(1)} %get-tuple-element.8), channel_id=1, source_target_pairs={{0,112},{8,120},{16,0},{24,8},{32,16},{40,24},{48,32},{56,40},{64,... | collective-permute-start | bytes 737288 | tf_op jit(solution)/shard_map/gather_neighbours/ppermute | solution.py:103
  43.3 1.3 %collective-permute-done.1 = bf16[8,120,128]{2,0,1:T(8,128)(2,1)S(1)} collective-permute-done((bf16[8,120,128]{2,0,1:T(8,128)(2,1)S(1)}, bf16[8,120,128]{2,0,1:T(8,128)(2,1)S(1)}, u32[]{:S(2)}, u32[]{:S(2)}) %collective-permute-start.1) | collective-permute-done | bytes 245792 | tf_op jit(solution)/shard_map/gather_neighbours/ppermute | solution.py:104
  44.6 4.0 %collective-permute-done = bf16[8,120,128]{2,0,1:T(8,128)(2,1)S(1)} collective-permute-done((bf16[8,120,128]{2,0,1:T(8,128)(2,1)S(1)}, bf16[8,120,128]{2,0,1:T(8,128)(2,1)S(1)}, u32[]{:S(2)}, u32[]{:S(2)}) %collective-permute-start) | collective-permute-done | bytes 245792 | tf_op jit(solution)/shard_map/gather_neighbours/ppermute | solution.py:103
  48.8 0.7 copy.48
  49.6 0.6 convolution_convert_fusion
  50.1 3.9 %collective-permute-start.2 = (bf16[288,1280]{1,0:T(8,128)(2,1)S(1)}, bf16[288,1280]{1,0:T(8,128)(2,1)S(1)}, u32[]{:S(2)}, u32[]{:S(2)}) collective-permute-start(bf16[288,1280]{1,0:T(8,128)(2,1)S(1)} %convolution_convert_fusion), channel_id=1, source_target_pairs={{0,8},{8,0},{16,24},{24,16},{32,40},{40,32},{48,56},{56,48},{64,72... | collective-permute-start | bytes 2211848 | tf_op jit(solution)/shard_map/gather_core/ppermute | solution.py:109
  54.2 1.6 %collective-permute-done.2 = bf16[288,1280]{1,0:T(8,128)(2,1)S(1)} collective-permute-done((bf16[288,1280]{1,0:T(8,128)(2,1)S(1)}, bf16[288,1280]{1,0:T(8,128)(2,1)S(1)}, u32[]{:S(2)}, u32[]{:S(2)}) %collective-permute-start.2) | collective-permute-done | bytes 737312 | tf_op jit(solution)/shard_map/gather_core/ppermute | solution.py:109
  56.0 0.7 convolution_convert_fusion.1
  56.7 0.4 convolution_convert_fusion.3
  57.1 0.5 concatenate.23
  57.6 0.5 convert_element_type.62
  58.1 0.6 copy.49
  58.9 17.4 %all_to_all.20 = bf16[8,400,128]{2,1,0:T(8,128)(2,1)S(1)} all-to-all(bf16[8,400,128]{2,1,0:T(8,128)(2,1)S(1)} %pad.13.clone), channel_id=1, replica_groups=mesh['dp'=64,'fsdp'=8] {'fsdp'}, dimensions={0} | all-to-all | bytes 1638400 | tf_op jit(solution)/shard_map/sum_features/all_to_all | solution.py:39
  77.1 14.6 %all_to_all.21 = bf16[8,400,128]{2,1,0:T(8,128)(2,1)S(1)} all-to-all(bf16[8,400,128]{2,1,0:T(8,128)(2,1)S(1)} %broadcast_in_dim.76), channel_id=1, replica_groups=mesh['dp'=64,'fsdp'=8] {'fsdp'}, dimensions={0} | all-to-all | bytes 1638400 | tf_op jit(solution)/shard_map/gather_hidden/all_to_all | solution.py:39
  91.9 0.4 copy.54
  92.5 1.0 copy-done.4
  93.5 0.6 convolution_convert_fusion.2
  95.0 0.6 reshape.146
  95.7 0.3 copy.64
  96.0 0.9 pad.15.clone
  96.9 9.8 %all-to-all-start.3 = ((bf16[64,32,128]{2,1,0:T(8,128)(2,1)}), bf16[64,32,128]{2,1,0:T(8,128)(2,1)S(1)}, u32[]{:S(2)}, u32[]{:S(2)}) async-start(bf16[64,32,128]{2,1,0:T(8,128)(2,1)} %pad.15.clone), calls=%async_computation.3 | async-start | bytes 1048576 | tf_op jit(solution)/shard_map/grad_rows/all_to_all | solution.py:39
  107.4 1.6 %fusion = bf16[432,640]{1,0:T(8,128)(2,1)} fusion(f32[]{:T(128)S(6)} %rsqrt.3, bf16[288,1280]{1,0:T(8,128)(2,1)S(1)} %add.91, bf16[288,1408]{1,0:T(8,128)(2,1)S(1)} %bitcast.76), kind=kOutput, calls=%fused_computation.4 | convolution fusion | flops 159805440 | bytes 1216516 | tf_op jit(solution)/shard_map/grad_weights/dot_general | solution.py:172
  108.9 0.8 multiply_convert_fusion
  109.8 1.1 fusion.19
  110.9 14.4 %all-to-all-done.3 = bf16[64,32,128]{2,1,0:T(8,128)(2,1)S(1)} async-done(((bf16[64,32,128]{2,1,0:T(8,128)(2,1)}), bf16[64,32,128]{2,1,0:T(8,128)(2,1)S(1)}, u32[]{:S(2)}, u32[]{:S(2)}) %all-to-all-start.3) | async-done | bytes 524320 | tf_op jit(solution)/shard_map/grad_rows/all_to_all | solution.py:39
  125.4 0.6 convert_element_type.70
  (68 shorter events, 3.8 us)
Async XLA Ops:
  0.6 56.0 %copy-start = (bf16[432,640]{1,0:T(8,128)(2,1)S(1)}, bf16[432,640]{1,0:T(8,128)(2,1)}, u32[]{:S(2)}) copy-start(bf16[432,640]{1,0:T(8,128)(2,1)} %param.11) | copy-start | bytes 1658884
  0.6 18.0 %copy-start.5 = (s32[64,3]{0,1:T(4,128)S(1)}, s32[64,3]{0,1:T(4,128)}, u32[]{:S(2)}) copy-start(s32[64,3]{0,1:T(4,128)} %param.13) | copy-start | bytes 2308
  0.7 18.0 %copy-start.6 = (s32[64]{0:T(128)S(1)}, s32[64]{0:T(128)}, u32[]{:S(2)}) copy-start(s32[64]{0:T(128)} %param.12) | copy-start | bytes 772
  2.4 33.9 %all-to-all-start = ((bf16[16,120,128]{2,1,0:T(8,128)(2,1)}), bf16[16,120,128]{2,1,0:T(8,128)(2,1)S(1)}, u32[]{:S(2)}, u32[]{:S(2)}) async-start(bf16[16,120,128]{2,1,0:T(8,128)(2,1)} %broadcast_in_dim.70), calls=%async_computation | async-start | bytes 983040 | tf_op jit(solution)/shard_map/gather_side/all_to_all | solution.py:39
  36.5 8.2 %collective-permute-start.1 = (bf16[8,120,128]{2,0,1:T(8,128)(2,1)S(1)}, bf16[8,120,128]{2,0,1:T(8,128)(2,1)S(1)}, u32[]{:S(2)}, u32[]{:S(2)}) collective-permute-start(bf16[8,120,128]{2,0,1:T(8,128)(2,1)S(1)} %get-tuple-element.9), channel_id=1, source_target_pairs={{0,16},{8,24},{16,32},{24,40},{32,48},{40,56},{48,64},{56,72},{64,... | collective-permute-start | bytes 737288 | tf_op jit(solution)/shard_map/gather_neighbours/ppermute | solution.py:104
  38.4 10.3 %collective-permute-start = (bf16[8,120,128]{2,0,1:T(8,128)(2,1)S(1)}, bf16[8,120,128]{2,0,1:T(8,128)(2,1)S(1)}, u32[]{:S(2)}, u32[]{:S(2)}) collective-permute-start(bf16[8,120,128]{2,0,1:T(8,128)(2,1)S(1)} %get-tuple-element.8), channel_id=1, source_target_pairs={{0,112},{8,120},{16,0},{24,8},{32,16},{40,24},{48,32},{56,40},{64,... | collective-permute-start | bytes 737288 | tf_op jit(solution)/shard_map/gather_neighbours/ppermute | solution.py:103
  49.5 4.5 %copy-start.1 = (bf16[640,432]{0,1:T(8,128)(2,1)S(1)}, bf16[640,432]{0,1:T(8,128)(2,1)}, u32[]{:S(2)}) copy-start(bf16[640,432]{0,1:T(8,128)(2,1)} %param.9) | copy-start | bytes 1658884
  49.6 4.5 %copy-start.2 = (bf16[640,432]{0,1:T(8,128)(2,1)S(1)}, bf16[640,432]{0,1:T(8,128)(2,1)}, u32[]{:S(2)}) copy-start(bf16[640,432]{0,1:T(8,128)(2,1)} %param.10) | copy-start | bytes 1658884
  50.1 5.7 %collective-permute-start.2 = (bf16[288,1280]{1,0:T(8,128)(2,1)S(1)}, bf16[288,1280]{1,0:T(8,128)(2,1)S(1)}, u32[]{:S(2)}, u32[]{:S(2)}) collective-permute-start(bf16[288,1280]{1,0:T(8,128)(2,1)S(1)} %convolution_convert_fusion), channel_id=1, source_target_pairs={{0,8},{8,0},{16,24},{24,16},{32,40},{40,32},{48,56},{56,48},{64,72... | collective-permute-start | bytes 2211848 | tf_op jit(solution)/shard_map/gather_core/ppermute | solution.py:109
  54.2 2.5 %copy-start.3 = (bf16[640,864]{0,1:T(8,128)(2,1)}, bf16[640,864]{0,1:T(8,128)(2,1)S(1)}, u32[]{:S(2)}) copy-start(bf16[640,864]{0,1:T(8,128)(2,1)S(1)} %constant_dynamic-update-slice_fusion) | copy-start | bytes 3317764
  92.3 1.2 copy-start.4
  96.9 28.4 %all-to-all-start.3 = ((bf16[64,32,128]{2,1,0:T(8,128)(2,1)}), bf16[64,32,128]{2,1,0:T(8,128)(2,1)S(1)}, u32[]{:S(2)}, u32[]{:S(2)}) async-start(bf16[64,32,128]{2,1,0:T(8,128)(2,1)} %pad.15.clone), calls=%async_computation.3 | async-start | bytes 1048576 | tf_op jit(solution)/shard_map/grad_rows/all_to_all | solution.py:39

commit v4 on v2

v4 whole, which is shorter than its diff:
```python
import jax
import jax.numpy as jnp
from jax import lax
from jax.sharding import PartitionSpec as P

LANES = 128
CORES = 2
BF16 = jnp.bfloat16
F32 = jnp.float32


CORE_GROUPS = [
    [chip * CORES + core for chip in range(32)] for core in range(CORES)
]


def exchange(x, axis, groups=None):
    return lax.all_to_all(x, axis, 0, 0, tiled=True, axis_index_groups=groups)


def copies(x, count):
    return jnp.broadcast_to(x[None], (count,) + x.shape)


def dense(x):
    n, rows, columns = x.shape
    tiles = columns // LANES
    x = x.reshape(n, rows, tiles, LANES).transpose(0, 2, 1, 3).reshape(n, tiles * rows, LANES)
    return jnp.pad(x, ((0, 0), (0, -(tiles * rows) % 8), (0, 0)))


def undense(x, rows):
    n, flat, _ = x.shape
    tiles = flat // rows
    x = x[:, : tiles * rows].reshape(n, tiles, rows, LANES).transpose(0, 2, 1, 3)
    return x.reshape(n, rows, tiles * LANES)


def pad_hidden(weights, axis):
    padding = [(0, 0), (0, 0)]
    padding[axis] = (0, -weights.shape[axis] % (4 * LANES))
    return jnp.pad(weights, padding)


def body(inputs, upstream, w_gate, w_up, w_down, lengths, move_dest):
    members = lax.axis_size("dp")
    shards = lax.axis_size("fsdp")
    core = lax.axis_index("dp") % CORES
    capacity, features = inputs.shape
    hidden_units = w_gate.shape[1]
    heavy = members // 4
    rows = members * 4 + heavy * 2

    is_full = lengths == capacity
    full_rank = jnp.cumsum(is_full.astype(jnp.int32)) - is_full
    learner = jnp.arange(members, dtype=jnp.int32)[:, None]
    row = jnp.arange(capacity, dtype=jnp.int32)[None, :]
    target = jnp.repeat(move_dest, 2, axis=1)
    target = jnp.concatenate([jnp.zeros_like(target), target], axis=1)
    place = jnp.where(
        row < 2,
        learner * 4 + row,
        jnp.where(
            row < 4,
            members * 4 + full_rank[:, None] * 2 + row - 2,
            jnp.where(row < 6, learner * 4 + row - 2, target * 4 + 2 + row % 2),
        ),
    )
    place = jnp.where(row < lengths[:, None], place, -1)
    place = place.reshape(-1, CORES, capacity).transpose(1, 0, 2)
    place = jnp.where(core == 0, place[0], place[1]).reshape(-1)
    pick = (jnp.arange(rows, dtype=jnp.int32)[:, None] == place[None, :]).astype(BF16)
    chips = jnp.arange(members // CORES, dtype=jnp.int32)[None, :] * CORES
    owner = chips + (jnp.arange(CORES, dtype=jnp.int32)[:, None] ^ core)
    middle = jnp.where(is_full, members * 4 + full_rank * 2, -2).reshape(-1, CORES).T
    middle = jnp.where(core == 0, middle, middle[::-1])
    source = jnp.stack([owner * 4, middle, owner * 4 + 2], axis=2)
    source = (source[..., None] + jnp.arange(2, dtype=jnp.int32)).reshape(-1)
    order = (source[:, None] == jnp.arange(rows, dtype=jnp.int32)[None, :]).astype(BF16)
    grad_scale = lax.rsqrt(jnp.sum(lengths).astype(F32))

    both = jnp.concatenate([inputs, upstream], axis=1)[None]
    with jax.named_scope("gather_chips"):
        got = exchange(copies(dense(both)[0], members // CORES), "dp", CORE_GROUPS)
        got = undense(got, capacity).reshape(-1, 2 * features)
    with jax.named_scope("gather_core"):
        mine = jnp.dot(pick, got, preferred_element_type=F32).astype(BF16)
        other = lax.ppermute(mine, "dp", [(i, i ^ 1) for i in range(members)])
        kept = mine + other
    kept_in, kept_up = kept[:, :features], kept[:, features:]

    with jax.named_scope("partial_sums"):
        w_in = jnp.concatenate([pad_hidden(w_gate, 1), pad_hidden(w_up, 1)], axis=1)
        w_back = pad_hidden(w_down, 0)
        padded = w_back.shape[0]
        partial_in = jnp.dot(kept_in, w_in, preferred_element_type=F32)
        partial_back = lax.dot_general(
            kept_up, w_back, (((1,), (1,)), ((), ())), preferred_element_type=F32
        )
        partial = jnp.concatenate([partial_in.astype(BF16), partial_back.astype(BF16)], axis=1)
        halves = shards * LANES // padded
        partial = partial.reshape(halves, rows // halves, 3, padded // LANES, LANES)
        partial = partial.transpose(3, 0, 2, 1, 4).reshape(shards, -1, LANES)
    with jax.named_scope("sum_features"):
        parts = exchange(partial, "fsdp").reshape(shards, 3, rows // halves, LANES)
        gate_value, up_value, back_hidden = jnp.sum(parts.astype(F32), axis=0)
    with jax.named_scope("activation"):
        sigmoid_gate = jax.nn.sigmoid(gate_value)
        activated = gate_value * sigmoid_gate
        hidden = (activated * up_value).astype(BF16)
        grad_gate_hidden = (
            back_hidden * up_value * sigmoid_gate * (1.0 + gate_value * (1.0 - sigmoid_gate))
        ).astype(BF16)
        grad_up_hidden = (back_hidden * activated).astype(BF16)
        shard = jnp.concatenate([grad_gate_hidden, grad_up_hidden, hidden], axis=0)
    with jax.named_scope("gather_hidden"):
        gathered = exchange(copies(shard, shards), "fsdp")
        gathered = gathered.reshape(padded // LANES, halves, 3, rows // halves, LANES)
        gathered = gathered.transpose(1, 3, 2, 0, 4).reshape(rows, 3 * padded)
    grad_in_hidden, hidden = gathered[:, : 2 * padded], gathered[:, 2 * padded :]

    with jax.named_scope("grad_rows"):
        in_slots = jnp.dot(order, grad_in_hidden, preferred_element_type=F32).astype(BF16)
        grad_rows = lax.dot_general(
            in_slots, w_in, (((1,), (1,)), ((), ())), preferred_element_type=F32
        )
        half = grad_rows.shape[0] // CORES
        grad_rows = grad_rows[:half] + lax.ppermute(
            grad_rows[half:], "dp", [(i, i ^ 1) for i in range(members)]
        )
        grad_rows = grad_rows.astype(BF16).reshape(members // CORES, -1, features)
        arrived = exchange(dense(grad_rows), "dp", CORE_GROUPS)
        grad_inputs = jnp.sum(arrived.astype(F32), axis=0, keepdims=True).astype(BF16)
        grad_inputs = undense(grad_inputs, grad_rows.shape[1])[0]

    contract_rows = (((0,), (0,)), ((), ()))
    with jax.named_scope("grad_weights"):
        in_total = lax.dot_general(
            kept_in, grad_in_hidden, contract_rows, preferred_element_type=F32
        )
        grad_in = (in_total * grad_scale).astype(BF16)
        down_total = lax.dot_general(hidden, kept_up, contract_rows, preferred_element_type=F32)
        grad_down = (down_total * grad_scale).astype(BF16)
    return (
        grad_inputs,
        grad_in[:, :hidden_units],
        grad_in[:, padded : padded + hidden_units],
        grad_down[:hidden_units],
    )


def solution(mesh):
    in_specs = (
        P("dp", "fsdp"),
        P("dp", "fsdp"),
        P("fsdp", "dp"),
        P("fsdp", "dp"),
        P("dp", "fsdp"),
        P(),
        P(),
    )
    out_specs = (P("dp", "fsdp"), P("fsdp", "dp"), P("fsdp", "dp"), P("dp", "fsdp"))
    return jax.shard_map(body, mesh=mesh, in_specs=in_specs, out_specs=out_specs, check_vma=False)
```

time: 125 us -> 126 us (level); the launches traced: 124 us -> 124 us
  blocking collectives: 32.4 us -> 18.1 us
  starting transfers between devices: 32.4 us -> 38.7 us
  waiting for transfers between devices: 40 us -> 45.7 us
  other arithmetic: 2.37 us -> 4.41 us
    all_to_all x2 -> x1, blocking collectives: 32.4 us -> 18.1 us  [exchange(): return lax.all_to_all(x, axis, 0, 0, tiled=True, axis_index_groups=groups)]
    ppermute x0 -> x1, starting transfers between devices: none -> 5.72 us  [body(): lax.ppermute(grad_rows[half:], 'dp', [(i, i ^ 1) for i in range(members)])]
    all_to_all x2 -> x3, waiting for transfers between devices: 38.4 us -> 43.9 us  [exchange(): return lax.all_to_all(x, axis, 0, 0, tiled=True, axis_index_groups=groups)]
    convert_element_type x1 -> x3, other arithmetic: 0.11 us -> 2.01 us  [the longest x1 1.08 us: body(): grad_rows = grad_rows.astype(BF16).reshape(members // CORES, -1, features)]
    dot_general x3 -> x2, matrix products: 1.28 us -> 2.79 us  [the longest x1 2.37 us: body(): lax.dot_general(in_slots, w_in, (((1,), (1,)), ((), ())), preferred_eleme...]
    all_to_all x2 -> x3, starting transfers between devices: 26.5 us -> 26.9 us  [exchange(): return lax.all_to_all(x, axis, 0, 0, tiled=True, axis_index_groups=groups)]
  transfers between devices with their start and end apart: 3 -> 5, of which waited for: 3 -> 4; matrix products, arithmetic and copies ran while one was open for 4% -> 5% of each run, Pallas kernels for 0% -> 0%
where the time goes in v4:
time: 126 us; the launch traced here: 124 us
  waiting for transfers between devices  45.7 us (36%)
  starting transfers between devices  38.7 us (31%)
  blocking collectives  18.1 us (14%)
  local copies, waits for them, and re-layouts  10.1 us (8%)
  matrix products  5.45 us (4%)
  other arithmetic  4.41 us (4%)
  between operations  1.7 us (1%)
    all_to_all x3, waiting for transfers between devices, exchange(): return lax.all_to_all(x, axis, 0, 0, tiled=True, axis_index_groups=groups)  43.9 us
    all_to_all x3, starting transfers between devices, exchange(): return lax.all_to_all(x, axis, 0, 0, tiled=True, axis_index_groups=groups)  26.9 us
    all_to_all x1, blocking collectives, exchange(): return lax.all_to_all(x, axis, 0, 0, tiled=True, axis_index_groups=groups)  18.1 us
    ppermute x1, starting transfers between devices, body(): other = lax.ppermute(mine, 'dp', [(i, i ^ 1) for i in range(members)])  6.01 us
    ppermute x1, starting transfers between devices, body(): lax.ppermute(grad_rows[half:], 'dp', [(i, i ^ 1) for i in range(members)])  5.72 us
  transfers between devices with their start and end apart: 5, of which 4 were waited for; matrix products, arithmetic and copies ran while one was open for 5% of the time, Pallas kernels for 0%

profile of v4, /device:TPU:1, one launch (start us, length us, event | category | flops | bytes accessed | tf_op | source)
XLA Modules:
  0.0 124.1 jit_solution(8746108966947341603)
XLA Ops:
  0.6 0.8 pad_maximum_fusion.2
  1.5 1.1 broadcast_in_dim.61
  2.6 16.5 %all-to-all-start = ((bf16[32,120,128]{2,1,0:T(8,128)(2,1)}), bf16[32,120,128]{2,1,0:T(8,128)(2,1)S(1)}, u32[]{:S(2)}, u32[]{:S(2)}) async-start(bf16[32,120,128]{2,1,0:T(8,128)(2,1)} %broadcast_in_dim.61), calls=%async_computation | async-start | bytes 1966080 | tf_op jit(solution)/shard_map/gather_chips/all_to_all | solution.py:18
  19.5 0.6 compare_select_fusion
  20.5 23.9 %all-to-all-done = bf16[32,120,128]{2,1,0:T(8,128)(2,1)S(1)} async-done(((bf16[32,120,128]{2,1,0:T(8,128)(2,1)}), bf16[32,120,128]{2,1,0:T(8,128)(2,1)S(1)}, u32[]{:S(2)}, u32[]{:S(2)}) %all-to-all-start) | async-done | bytes 983072 | tf_op jit(solution)/shard_map/gather_chips/all_to_all | solution.py:18
  44.6 0.7 copy.44
  45.3 0.6 convolution_convert_fusion
  45.9 6.0 %collective-permute-start = (bf16[288,1280]{1,0:T(8,128)(2,1)S(1)}, bf16[288,1280]{1,0:T(8,128)(2,1)S(1)}, u32[]{:S(2)}, u32[]{:S(2)}) collective-permute-start(bf16[288,1280]{1,0:T(8,128)(2,1)S(1)} %convolution_convert_fusion), channel_id=1, source_target_pairs={{0,8},{8,0},{16,24},{24,16},{32,40},{40,32},{48,56},{56,48},{64,72... | collective-permute-start | bytes 2211848 | tf_op jit(solution)/shard_map/gather_core/ppermute | solution.py:88
  52.0 1.8 %collective-permute-done = bf16[288,1280]{1,0:T(8,128)(2,1)S(1)} collective-permute-done((bf16[288,1280]{1,0:T(8,128)(2,1)S(1)}, bf16[288,1280]{1,0:T(8,128)(2,1)S(1)}, u32[]{:S(2)}, u32[]{:S(2)}) %collective-permute-start) | collective-permute-done | bytes 737312 | tf_op jit(solution)/shard_map/gather_core/ppermute | solution.py:88
  54.0 0.4 convolution_convert_fusion.3
  54.4 0.6 convolution_convert_fusion.2
  55.4 18.1 %all_to_all.20 = bf16[8,432,128]{2,1,0:T(8,128)(2,1)S(1)} all-to-all(bf16[8,432,128]{2,1,0:T(8,128)(2,1)S(1)} %bitcast.34), channel_id=1, replica_groups=mesh['dp'=64,'fsdp'=8] {'fsdp'}, dimensions={0} | all-to-all | bytes 1769472 | tf_op jit(solution)/shard_map/sum_features/all_to_all | solution.py:18
  73.8 1.0 broadcast_in_dim.62
  74.8 3.5 %all-to-all-start.2 = ((bf16[8,432,128]{2,1,0:T(8,128)(2,1)}), bf16[8,432,128]{2,1,0:T(8,128)(2,1)S(1)}, u32[]{:S(2)}, u32[]{:S(2)}) async-start(bf16[8,432,128]{2,1,0:T(8,128)(2,1)} %broadcast_in_dim.62), calls=%async_computation.2 | async-start | bytes 1769472 | tf_op jit(solution)/shard_map/gather_hidden/all_to_all | solution.py:18
  79.8 8.6 %all-to-all-done.2 = bf16[8,432,128]{2,1,0:T(8,128)(2,1)S(1)} async-done(((bf16[8,432,128]{2,1,0:T(8,128)(2,1)}), bf16[8,432,128]{2,1,0:T(8,128)(2,1)S(1)}, u32[]{:S(2)}, u32[]{:S(2)}) %all-to-all-start.2) | async-done | bytes 884768 | tf_op jit(solution)/shard_map/gather_hidden/all_to_all | solution.py:18
  88.4 0.5 copy.46
  88.9 0.3 reshape.267
  89.2 2.4 %fusion.3 = f32[384,640]{1,0:T(8,128)S(1)} fusion(bf16[288,1536]{1,0:T(8,128)(2,1)S(1)} %reshape.267, bf16[640,432]{0,1:T(8,128)(2,1)S(1)} %copy-done.5, bf16[640,432]{0,1:T(8,128)(2,1)} %param.9, s32[384]{0:T(512)S(1)} %add.160), kind=kOutput, calls=%fused_computation.10 | convolution fusion | flops 735555584 | bytes 2680832 | tf_op jit(solution)/shard_map/grad_rows/dot_general | solution.py:124
  91.6 0.9 slice.57
  92.5 5.7 %collective-permute-start.1 = (f32[192,640]{1,0:T(8,128)}, f32[192,640]{1,0:T(8,128)}, u32[]{:S(2)}, u32[]{:S(2)}) collective-permute-start(f32[192,640]{1,0:T(8,128)} %slice.57), channel_id=1, source_target_pairs={{0,8},{8,0},{16,24},{24,16},{32,40},{40,32},{48,56},{56,48},{64,72... | collective-permute-start | bytes 1474568 | tf_op jit(solution)/shard_map/grad_rows/ppermute | solution.py:128
  98.2 0.9 multiply_convert_fusion
  99.2 1.1 copy.49
  100.3 1.1 copy.50
  101.3 0.2 copy-done.1
  101.5 1.1 fusion.11
  102.6 0.3 reshape.268
  103.1 0.7 pad.19.clone
  103.8 6.9 %all-to-all-start.3 = ((bf16[32,32,128]{2,1,0:T(8,128)(2,1)}), bf16[32,32,128]{2,1,0:T(8,128)(2,1)S(1)}, u32[]{:S(2)}, u32[]{:S(2)}) async-start(bf16[32,32,128]{2,1,0:T(8,128)(2,1)} %pad.19.clone), calls=%async_computation.3 | async-start | bytes 524288 | tf_op jit(solution)/shard_map/grad_rows/all_to_all | solution.py:18
  110.7 0.6 fusion.14
  111.3 0.9 fusion.4
  112.2 11.3 %all-to-all-done.3 = bf16[32,32,128]{2,1,0:T(8,128)(2,1)S(1)} async-done(((bf16[32,32,128]{2,1,0:T(8,128)(2,1)}), bf16[32,32,128]{2,1,0:T(8,128)(2,1)S(1)}, u32[]{:S(2)}, u32[]{:S(2)}) %all-to-all-start.3) | async-done | bytes 262176 | tf_op jit(solution)/shard_map/grad_rows/all_to_all | solution.py:18
  123.5 0.6 reshape.270
  (53 shorter events, 2.7 us)
Async XLA Ops:
  1.5 17.7 %copy-start.3 = (s32[64]{0:T(128)S(1)}, s32[64]{0:T(128)}, u32[]{:S(2)}) copy-start(s32[64]{0:T(128)} %param.12) | copy-start | bytes 772
  1.5 18.0 %copy-start.2 = (s32[64,3]{0,1:T(4,128)S(1)}, s32[64,3]{0,1:T(4,128)}, u32[]{:S(2)}) copy-start(s32[64,3]{0,1:T(4,128)} %param.13) | copy-start | bytes 2308
  2.6 41.8 %all-to-all-start = ((bf16[32,120,128]{2,1,0:T(8,128)(2,1)}), bf16[32,120,128]{2,1,0:T(8,128)(2,1)S(1)}, u32[]{:S(2)}, u32[]{:S(2)}) async-start(bf16[32,120,128]{2,1,0:T(8,128)(2,1)} %broadcast_in_dim.61), calls=%async_computation | async-start | bytes 1966080 | tf_op jit(solution)/shard_map/gather_chips/all_to_all | solution.py:18
  45.9 8.1 %copy-start.4 = (bf16[432,640]{1,0:T(8,128)(2,1)S(1)}, bf16[432,640]{1,0:T(8,128)(2,1)}, u32[]{:S(2)}) copy-start(bf16[432,640]{1,0:T(8,128)(2,1)} %param.11) | copy-start | bytes 1658884
  45.9 8.5 %copy-start.5 = (bf16[640,432]{0,1:T(8,128)(2,1)S(1)}, bf16[640,432]{0,1:T(8,128)(2,1)}, u32[]{:S(2)}) copy-start(bf16[640,432]{0,1:T(8,128)(2,1)} %param.10) | copy-start | bytes 1658884
  45.9 8.5 %copy-start.6 = (bf16[640,432]{0,1:T(8,128)(2,1)S(1)}, bf16[640,432]{0,1:T(8,128)(2,1)}, u32[]{:S(2)}) copy-start(bf16[640,432]{0,1:T(8,128)(2,1)} %param.9) | copy-start | bytes 1658884
  45.9 7.8 %collective-permute-start = (bf16[288,1280]{1,0:T(8,128)(2,1)S(1)}, bf16[288,1280]{1,0:T(8,128)(2,1)S(1)}, u32[]{:S(2)}, u32[]{:S(2)}) collective-permute-start(bf16[288,1280]{1,0:T(8,128)(2,1)S(1)} %convolution_convert_fusion), channel_id=1, source_target_pairs={{0,8},{8,0},{16,24},{24,16},{32,40},{40,32},{48,56},{56,48},{64,72... | collective-permute-start | bytes 2211848 | tf_op jit(solution)/shard_map/gather_core/ppermute | solution.py:88
  74.8 13.6 %all-to-all-start.2 = ((bf16[8,432,128]{2,1,0:T(8,128)(2,1)}), bf16[8,432,128]{2,1,0:T(8,128)(2,1)S(1)}, u32[]{:S(2)}, u32[]{:S(2)}) async-start(bf16[8,432,128]{2,1,0:T(8,128)(2,1)} %broadcast_in_dim.62), calls=%async_computation.2 | async-start | bytes 1769472 | tf_op jit(solution)/shard_map/gather_hidden/all_to_all | solution.py:18
  91.6 6.6 %copy-start = (f32[384,640]{1,0:T(8,128)}, f32[384,640]{1,0:T(8,128)S(1)}, u32[]{:S(2)}) copy-start(f32[384,640]{1,0:T(8,128)S(1)} %fusion.3) | copy-start | bytes 2949124
  92.5 8.8 %collective-permute-start.1 = (f32[192,640]{1,0:T(8,128)}, f32[192,640]{1,0:T(8,128)}, u32[]{:S(2)}, u32[]{:S(2)}) collective-permute-start(f32[192,640]{1,0:T(8,128)} %slice.57), channel_id=1, source_target_pairs={{0,8},{8,0},{16,24},{24,16},{32,40},{40,32},{48,56},{56,48},{64,72... | collective-permute-start | bytes 1474568 | tf_op jit(solution)/shard_map/grad_rows/ppermute | solution.py:128
  100.3 1.3 %copy-start.1 = (f32[384,640]{1,0:T(8,128)S(1)}, f32[384,640]{1,0:T(8,128)}, u32[]{:S(2)}) copy-start(f32[384,640]{1,0:T(8,128)} %copy-done) | copy-start | bytes 2949124
  103.8 19.6 %all-to-all-start.3 = ((bf16[32,32,128]{2,1,0:T(8,128)(2,1)}), bf16[32,32,128]{2,1,0:T(8,128)(2,1)S(1)}, u32[]{:S(2)}, u32[]{:S(2)}) async-start(bf16[32,32,128]{2,1,0:T(8,128)(2,1)} %pad.19.clone), calls=%async_computation.3 | async-start | bytes 524288 | tf_op jit(solution)/shard_map/grad_rows/all_to_all | solution.py:18

commit v5 on v4

v5 whole, which is shorter than its diff:
```python
import jax
import jax.numpy as jnp
from jax import lax
from jax.experimental import pallas as pl
from jax.experimental.pallas import tpu as pltpu
from jax.sharding import PartitionSpec as P

LANES = 128
CORES = 2
BF16 = jnp.bfloat16
F32 = jnp.float32
CORE_GROUPS = [[chip * CORES + core for chip in range(32)] for core in range(CORES)]


def exchange(x, axis, groups=None):
    return lax.all_to_all(x, axis, 0, 0, tiled=True, axis_index_groups=groups)


def copies(x, count):
    return jnp.broadcast_to(x[None], (count,) + x.shape)


def dense(x):
    n, rows, columns = x.shape
    tiles = columns // LANES
    return x.reshape(n, rows, tiles, LANES).transpose(0, 2, 1, 3).reshape(n, tiles * rows, LANES)


def undense(x, rows):
    n, flat, _ = x.shape
    tiles = flat // rows
    x = x.reshape(n, tiles, rows, LANES).transpose(0, 2, 1, 3)
    return x.reshape(n, rows, tiles * LANES)


def pad_hidden(weights):
    return jnp.pad(weights, ((0, -weights.shape[0] % (4 * LANES)), (0, 0)))


def call(kernel, outs, flops, *operands):
    whole = pl.BlockSpec(memory_space=pltpu.VMEM)
    moved = sum(x.size * x.dtype.itemsize for x in (*operands, *outs))
    return pl.pallas_call(
        kernel,
        out_shape=outs,
        in_specs=[whole] * len(operands),
        out_specs=[whole] * len(outs),
        cost_estimate=pl.CostEstimate(flops=flops, bytes_accessed=moved, transcendentals=0),
        compiler_params=pltpu.CompilerParams(vmem_limit_bytes=24 * 2**20),
    )(*operands)


def sums_kernel(mine_ref, other_ref, weights_ref, kept_ref, sums_ref):
    features = weights_ref.shape[1]
    padded = weights_ref.shape[0] // 3
    half = mine_ref.shape[0] // 2
    kept_ref[...] = mine_ref[...] + other_ref[...]
    step = 2 * LANES
    for which in range(3):
        first = 0 if which < 2 else features
        for at in range(0, padded, step):
            value = lax.dot_general(
                kept_ref[:, first : first + features],
                weights_ref[which * padded + at : which * padded + at + step, :],
                (((1,), (1,)), ((), ())),
                preferred_element_type=F32,
            ).astype(BF16)
            for tile in range(step // LANES):
                for part in range(2):
                    sums_ref[
                        2 * (at // LANES + tile) + part, which * half : (which + 1) * half, :
                    ] = value[part * half : (part + 1) * half, tile * LANES : (tile + 1) * LANES]


def rows_kernel(gathered_ref, weights_ref, order_ref, hidden_ref, rows_ref):
    shards, high, _ = gathered_ref.shape
    half = high // 3
    padded = shards // 2 * LANES
    for shard in range(shards):
        tile, part = divmod(shard, 2)
        for which in range(3):
            at = which * padded + tile * LANES
            hidden_ref[part * half : (part + 1) * half, at : at + LANES] = gathered_ref[
                shard, which * half : (which + 1) * half, :
            ]
    features = weights_ref.shape[1]
    for at in range(0, features, 2 * LANES):
        to = min(at + 2 * LANES, features)
        value = jnp.dot(
            hidden_ref[:, : 2 * padded],
            weights_ref[: 2 * padded, at:to],
            preferred_element_type=F32,
        ).astype(BF16)
        rows_ref[:, at:to] = jnp.dot(
            order_ref[...], value, preferred_element_type=F32
        ).astype(BF16)


def body(inputs, upstream, w_gate, w_up, w_down, lengths, move_dest):
    members = lax.axis_size("dp")
    shards = lax.axis_size("fsdp")
    core = lax.axis_index("dp") & 1
    capacity, features = inputs.shape
    hidden_units = w_gate.shape[1]
    heavy = members // 4
    rows = members * 4 + heavy * 2

    is_full = lengths == capacity
    full_rank = jnp.cumsum(is_full.astype(jnp.int32)) - is_full
    learner = jnp.arange(members, dtype=jnp.int32)[:, None]
    row = jnp.arange(capacity, dtype=jnp.int32)[None, :]
    target = jnp.repeat(move_dest, 2, axis=1)
    target = jnp.concatenate([jnp.zeros_like(target), target], axis=1)
    place = jnp.where(
        row < 2,
        learner * 4 + row,
        jnp.where(
            row < 4,
            members * 4 + full_rank[:, None] * 2 + row - 2,
            jnp.where(row < 6, learner * 4 + row - 2, target * 4 + 2 + row % 2),
        ),
    )
    place = jnp.where(row < lengths[:, None], place, -1)
    place = place.reshape(-1, CORES, capacity).transpose(1, 0, 2)
    place = jnp.where(core == 0, place[0], place[1]).reshape(-1)
    kept_row = jnp.arange(rows, dtype=jnp.int32)[None, :]
    pick = (kept_row.T == place[None, :]).astype(BF16)
    middle = jnp.where(is_full, members * 4 + full_rank * 2, -2)[:, None]
    pair = jnp.arange(2, dtype=jnp.int32)[None, :]
    none = jnp.full((members, 2), -1, jnp.int32)
    source = [learner * 4 + pair, middle + pair, learner * 4 + 2 + pair, none]
    source = jnp.concatenate(source, axis=1).reshape(-1)
    order = (source[:, None] == kept_row).astype(BF16)
    grad_scale = lax.rsqrt(jnp.sum(lengths).astype(F32))
    weights = jnp.concatenate([pad_hidden(w) for w in (w_gate.T, w_up.T, w_down)], axis=0)
    padded = weights.shape[0] // 3

    with jax.named_scope("gather_chips"):
        both = jnp.concatenate([inputs, upstream], axis=1)[None]
        got = exchange(copies(dense(both)[0], members // CORES), "dp", CORE_GROUPS)
        got, weights, order = lax.optimization_barrier((got, weights, order))
        got = undense(got, capacity).reshape(-1, 2 * features)
    with jax.named_scope("gather_core"):
        mine = jnp.dot(pick, got, preferred_element_type=F32).astype(BF16)
        other = lax.ppermute(mine, "dp", [(i, i ^ 1) for i in range(members)])
    with jax.named_scope("partial_sums"):
        kept, partial = call(
            sums_kernel,
            [
                jax.ShapeDtypeStruct(mine.shape, BF16),
                jax.ShapeDtypeStruct((shards, 3 * rows // 2, LANES), BF16),
            ],
            2 * rows * features * 3 * padded,
            mine,
            other,
            weights,
        )
    with jax.named_scope("sum_features"):
        parts = exchange(partial, "fsdp").reshape(shards, 3, rows // 2, LANES)
        gate_value, up_value, back_hidden = jnp.sum(parts.astype(F32), axis=0)
    with jax.named_scope("activation"):
        sigmoid_gate = jax.nn.sigmoid(gate_value)
        activated = gate_value * sigmoid_gate
        hidden = (activated * up_value).astype(BF16)
        grad_gate_hidden = (
            back_hidden * up_value * sigmoid_gate * (1.0 + gate_value * (1.0 - sigmoid_gate))
        ).astype(BF16)
        grad_up_hidden = (back_hidden * activated).astype(BF16)
        shard = jnp.concatenate([grad_gate_hidden, grad_up_hidden, hidden], axis=0)
    with jax.named_scope("gather_hidden"):
        gathered = exchange(copies(shard, shards), "fsdp")

    with jax.named_scope("grad_rows"):
        all_hidden, grad_rows = call(
            rows_kernel,
            [
                jax.ShapeDtypeStruct((rows, 3 * padded), BF16),
                jax.ShapeDtypeStruct((order.shape[0], features), BF16),
            ],
            2 * rows * features * (2 * padded + order.shape[0]),
            gathered,
            weights,
            order,
        )
        arrived = exchange(grad_rows.reshape(members, -1, features), "dp")
        grad_inputs = jnp.sum(arrived.astype(F32), axis=0)[: capacity // 2].astype(BF16)

    contract_rows = (((0,), (0,)), ((), ()))
    with jax.named_scope("grad_weights"):
        in_total = lax.dot_general(
            all_hidden[:, : 2 * padded],
            kept[:, :features],
            contract_rows,
            preferred_element_type=F32,
        )
        grad_in = (in_total * grad_scale).astype(BF16)
        down_total = lax.dot_general(
            all_hidden[:, 2 * padded :],
            kept[:, features:],
            contract_rows,
            preferred_element_type=F32,
        )
        grad_down = (down_total * grad_scale).astype(BF16)
    return (
        grad_inputs,
        grad_in[:hidden_units].T,
        grad_in[padded : padded + hidden_units].T,
        grad_down[:hidden_units],
    )


def solution(mesh):
    in_specs = (
        P("dp", "fsdp"),
        P("dp", "fsdp"),
        P("fsdp", "dp"),
        P("fsdp", "dp"),
        P("dp", "fsdp"),
        P(),
        P(),
    )
    out_specs = (P("dp", "fsdp"), P("fsdp", "dp"), P("fsdp", "dp"), P("dp", "fsdp"))
    return jax.shard_map(body, mesh=mesh, in_specs=in_specs, out_specs=out_specs, check_vma=False)
```

time: 126 us -> 126 us (level)
  blocking collectives: 18.1 us -> 33.1 us
  starting transfers between devices: 38.7 us -> 32.7 us
  waiting for transfers between devices: 45.7 us -> 39.8 us
  local copies, waits for them, and re-layouts: 10.1 us -> 4.72 us
  Pallas kernels: 0 us -> 3.89 us
  matrix products: 5.45 us -> 3.08 us
  other arithmetic: 4.41 us -> 6.41 us
    all_to_all x1 -> x2, blocking collectives: 18.1 us -> 33.1 us  [exchange(): return lax.all_to_all(x, axis, 0, 0, tiled=True, axis_index_groups=groups)]
    all_to_all x3 -> x2, waiting for transfers between devices: 43.9 us -> 37.9 us  [exchange(): return lax.all_to_all(x, axis, 0, 0, tiled=True, axis_index_groups=groups)]
    ppermute x1 -> x0, starting transfers between devices: 5.72 us -> none  [body(): lax.ppermute(grad_rows[half:], 'dp', [(i, i ^ 1) for i in range(members)])]
    pallas_call x0 -> x2, Pallas kernels: none -> 3.89 us  [call(): pl.pallas_call(kernel, out_shape=outs, in_specs=[whole] * len(operands),...]
    dot_general x5 -> x2, matrix products: 4.87 us -> 2.5 us  [the longest x1 1.54 us: body(): lax.dot_general(all_hidden[:, 2 * padded:], kept[:, features:], contract_...]
    reduce_sum x1, other arithmetic: 0.05 us -> 1.82 us  [body(): jnp.sum(arrived.astype(F32), axis=0)[:capacity // 2].astype(BF16)]
    reshape x6 -> x0, local copies, waits for them, and re-layouts: 1.64 us -> none  [the longest x1 0.61 us: undense(): x = x[:, :tiles * rows].reshape(n, tiles, rows, LANES).transpose(0, 2, 1, 3)]
    concatenate x1 -> x2, other arithmetic: 0.06 us -> 1.62 us  [the longest x1 1.54 us: body(): jnp.concatenate([pad_hidden(w) for w in (w_gate.T, w_up.T, w_down)], axis=0)]
  transfers between devices with their start and end apart: 5 -> 3, of which waited for: 4 -> 3; matrix products, arithmetic and copies ran while one was open for 5% -> 6% of each run, Pallas kernels for 0% -> 0%
where the time goes in v5:
time: 126 us; the launch traced here: 125 us
  waiting for transfers between devices  39.8 us (32%)
  blocking collectives  33.1 us (26%)
  starting transfers between devices  32.7 us (26%)
  other arithmetic  6.41 us (5%)
  local copies, waits for them, and re-layouts  4.72 us (4%)
  Pallas kernels  3.89 us (3%)
  matrix products  3.08 us (2%)
  between operations  1.62 us (1%)
    all_to_all x2, waiting for transfers between devices, exchange(): return lax.all_to_all(x, axis, 0, 0, tiled=True, axis_index_groups=groups)  37.9 us
    all_to_all x2, blocking collectives, exchange(): return lax.all_to_all(x, axis, 0, 0, tiled=True, axis_index_groups=groups)  33.1 us
    all_to_all x2, starting transfers between devices, exchange(): return lax.all_to_all(x, axis, 0, 0, tiled=True, axis_index_groups=groups)  26.8 us
    ppermute x1, starting transfers between devices, body(): other = lax.ppermute(mine, 'dp', [(i, i ^ 1) for i in range(members)])  5.88 us
    pallas_call x2, Pallas kernels, call(): pl.pallas_call(kernel, out_shape=outs, in_specs=[whole] * len(operands),...  3.89 us
  transfers between devices with their start and end apart: 3, of which 3 were waited for; matrix products, arithmetic and copies ran while one was open for 6% of the time, Pallas kernels for 0%

profile of v5, /device:TPU:1, one launch (start us, length us, event | category | flops | bytes accessed | tf_op | source)
XLA Modules:
  0.0 125.3 jit_solution(612493645922143792)
XLA Ops:
  0.7 0.8 pad_maximum_fusion.1
  1.5 1.1 broadcast_in_dim.63
  2.6 16.5 %all-to-all-start = ((bf16[32,120,128]{2,1,0:T(8,128)(2,1)}), bf16[32,120,128]{2,1,0:T(8,128)(2,1)S(1)}, u32[]{:S(2)}, u32[]{:S(2)}) async-start(bf16[32,120,128]{2,1,0:T(8,128)(2,1)} %broadcast_in_dim.63), calls=%async_computation | async-start | bytes 1966080 | tf_op jit(solution)/shard_map/gather_chips/all_to_all | solution.py:16
  19.2 0.1 copy.17
  19.3 0.1 reduce-window.9
  19.3 0.1 reduce.2
  19.5 0.6 multiply_add_fusion
  20.3 0.1 copy.18
  20.4 0.1 select_n.52
  20.7 0.1 eq.45
  20.8 0.1 fusion.9.order_ref
  21.0 1.5 %fusion.5.weights_ref = bf16[1536,640]{1,0:T(8,128)(2,1)S(1)} fusion(bf16[432,640]{1,0:T(8,128)(2,1)} %param.11, bf16[432,640]{1,0:T(8,128)(2,1)} %bitcast.26, bf16[432,640]{1,0:T(8,128)(2,1)} %bitcast.27), kind=kLoop, calls=%fused_computation.11 | loop fusion | flops 13762560 | bytes 3624960 | tf_op jit(solution)/shard_map/concatenate | solution.py:135
  22.5 21.9 %all-to-all-done = bf16[32,120,128]{2,1,0:T(8,128)(2,1)S(1)} async-done(((bf16[32,120,128]{2,1,0:T(8,128)(2,1)}), bf16[32,120,128]{2,1,0:T(8,128)(2,1)S(1)}, u32[]{:S(2)}, u32[]{:S(2)}) %all-to-all-start) | async-done | bytes 983072 | tf_op jit(solution)/shard_map/gather_chips/all_to_all | solution.py:16
  44.4 0.2 copy.21
  44.6 0.7 copy.22
  45.3 0.6 convolution_convert_fusion.mine_ref
  45.9 5.9 %collective-permute-start = (bf16[288,1280]{1,0:T(8,128)(2,1)S(1)}, bf16[288,1280]{1,0:T(8,128)(2,1)S(1)}, u32[]{:S(2)}, u32[]{:S(2)}) collective-permute-start(bf16[288,1280]{1,0:T(8,128)(2,1)S(1)} %convolution_convert_fusion.mine_ref), channel_id=1, source_target_pairs={{0,8},{8,0},{16,24},{24,16},{32,40},{40,32},{48,56},{56,48},{64,72... | collective-permute-start | bytes 2211848 | tf_op jit(solution)/shard_map/gather_core/ppermute | solution.py:145
  51.8 1.8 %collective-permute-done.other_ref = bf16[288,1280]{1,0:T(8,128)(2,1)S(1)} collective-permute-done((bf16[288,1280]{1,0:T(8,128)(2,1)S(1)}, bf16[288,1280]{1,0:T(8,128)(2,1)S(1)}, u32[]{:S(2)}, u32[]{:S(2)}) %collective-permute-start) | collective-permute-done | bytes 737312 | tf_op jit(solution)/shard_map/gather_core/ppermute | solution.py:145
  53.6 0.9 partial_sums.1
  54.5 18.1 %all_to_all.20 = bf16[8,432,128]{2,1,0:T(8,128)(2,1)S(1)} all-to-all(bf16[8,432,128]{2,1,0:T(8,128)(2,1)S(1)} %get-tuple-element.13), channel_id=1, replica_groups=mesh['dp'=64,'fsdp'=8] {'fsdp'}, dimensions={0} | all-to-all | bytes 1769472 | tf_op jit(solution)/shard_map/sum_features/all_to_all | solution.py:16
  72.6 0.1 convert_reduce_fusion
  72.8 0.1 broadcast_in_dim.66
  72.9 15.0 %all_to_all.21.gathered_ref = bf16[8,432,128]{2,1,0:T(8,128)(2,1)S(1)} all-to-all(bf16[8,432,128]{2,1,0:T(8,128)(2,1)S(1)} %broadcast_in_dim.66), channel_id=1, replica_groups=mesh['dp'=64,'fsdp'=8] {'fsdp'}, dimensions={0} | all-to-all | bytes 1769472 | tf_op jit(solution)/shard_map/gather_hidden/all_to_all | solution.py:16
  87.9 3.0 %grad_rows.1 = (bf16[288,1536]{1,0:T(8,128)(2,1)S(1)}, bf16[512,640]{1,0:T(8,128)(2,1)}) custom-call(bf16[8,432,128]{2,1,0:T(8,128)(2,1)S(1)} %all_to_all.21.gathered_ref, bf16[1536,640]{1,0:T(8,128)(2,1)S(1)} %fusion.5.weights_ref, bf16[512,288]{1,0:T(8,128)(2,1)S(1)} %fusion.9.order_ref), custom_call_target="tpu_custom_call" | custom-call | flops 566231040 | bytes 4685824 | tf_op jit(solution)/shard_map/grad_rows/pallas_call | solution.py:43
  90.9 0.9 copy-done
  91.9 10.3 %all-to-all-start.3 = ((bf16[64,8,640]{2,1,0:T(8,128)(2,1)}), bf16[64,8,640]{2,1,0:T(8,128)(2,1)}, u32[]{:S(2)}, u32[]{:S(2)}) async-start(bf16[64,8,640]{2,1,0:T(8,128)(2,1)} %bitcast.9), calls=%async_computation.3 | async-start | bytes 1310720 | tf_op jit(solution)/shard_map/grad_rows/all_to_all | solution.py:16
  103.0 1.5 %fusion.11 = f32[512,640]{1,0:T(8,128)S(1)} fusion(bf16[288,1280]{1,0:T(8,128)(2,1)S(1)} %get-tuple-element.17, bf16[288,1536]{1,0:T(8,128)(2,1)} %copy-done), kind=kOutput, calls=%fused_computation.23 | convolution fusion | flops 188743680 | bytes 1974272 | tf_op jit(solution)/shard_map/grad_weights/dot_general | solution.py:197
  104.5 0.9 fusion.6
  105.4 1.0 multiply_convert_fusion
  106.4 1.1 slice_bitcast_fusion
  107.4 16.1 %all-to-all-done.3 = bf16[64,8,640]{2,1,0:T(8,128)(2,1)} async-done(((bf16[64,8,640]{2,1,0:T(8,128)(2,1)}), bf16[64,8,640]{2,1,0:T(8,128)(2,1)}, u32[]{:S(2)}, u32[]{:S(2)}) %all-to-all-start.3) | async-done | bytes 655392 | tf_op jit(solution)/shard_map/grad_rows/all_to_all | solution.py:16
  123.5 1.8 %reduce.1 = bf16[8,640]{1,0:T(8,128)(2,1)} reduce(bf16[64,8,640]{2,1,0:T(8,128)(2,1)} %all-to-all-done.3, bf16[]{:T(256)} %constant.53.clone.1), dimensions={0}, to_apply=%region_2.3.clone | reduce | flops 322560 | bytes 665602 | tf_op jit(solution)/shard_map/grad_rows/reduce_sum | solution.py:186
  (28 shorter events, 0.6 us)
Async XLA Ops:
  0.6 18.5 %copy-start.2 = (s32[64]{0:T(128)S(1)}, s32[64]{0:T(128)}, u32[]{:S(2)}) copy-start(s32[64]{0:T(128)} %param.12) | copy-start | bytes 772
  0.6 19.5 %copy-start.3 = (s32[64,3]{0,1:T(4,128)S(1)}, s32[64,3]{0,1:T(4,128)}, u32[]{:S(2)}) copy-start(s32[64,3]{0,1:T(4,128)} %param.13) | copy-start | bytes 2308
  2.6 41.8 %all-to-all-start = ((bf16[32,120,128]{2,1,0:T(8,128)(2,1)}), bf16[32,120,128]{2,1,0:T(8,128)(2,1)S(1)}, u32[]{:S(2)}, u32[]{:S(2)}) async-start(bf16[32,120,128]{2,1,0:T(8,128)(2,1)} %broadcast_in_dim.63), calls=%async_computation | async-start | bytes 1966080 | tf_op jit(solution)/shard_map/gather_chips/all_to_all | solution.py:16
  45.9 7.7 %collective-permute-start = (bf16[288,1280]{1,0:T(8,128)(2,1)S(1)}, bf16[288,1280]{1,0:T(8,128)(2,1)S(1)}, u32[]{:S(2)}, u32[]{:S(2)}) collective-permute-start(bf16[288,1280]{1,0:T(8,128)(2,1)S(1)} %convolution_convert_fusion.mine_ref), channel_id=1, source_target_pairs={{0,8},{8,0},{16,24},{24,16},{32,40},{40,32},{48,56},{56,48},{64,72... | collective-permute-start | bytes 2211848 | tf_op jit(solution)/shard_map/gather_core/ppermute | solution.py:145
  90.9 0.9 copy-start
  91.9 31.6 %all-to-all-start.3 = ((bf16[64,8,640]{2,1,0:T(8,128)(2,1)}), bf16[64,8,640]{2,1,0:T(8,128)(2,1)}, u32[]{:S(2)}, u32[]{:S(2)}) async-start(bf16[64,8,640]{2,1,0:T(8,128)(2,1)} %bitcast.9), calls=%async_computation.3 | async-start | bytes 1310720 | tf_op jit(solution)/shard_map/grad_rows/all_to_all | solution.py:16
  102.2 3.2 %copy-start.1 = (bf16[288,1536]{1,0:T(8,128)(2,1)S(1)}, bf16[288,1536]{1,0:T(8,128)(2,1)}, u32[]{:S(2)}) copy-start(bf16[288,1536]{1,0:T(8,128)(2,1)} %copy-done) | copy-start | bytes 2654212

commit v6 on v5

--- a/solution.py
+++ b/solution.py
@@ -72,7 +72,7 @@
                     ] = value[part * half : (part + 1) * half, tile * LANES : (tile + 1) * LANES]
 
 
-def rows_kernel(gathered_ref, weights_ref, order_ref, hidden_ref, rows_ref):
+def rows_kernel(gathered_ref, weights_ref, hidden_ref, rows_ref):
     shards, high, _ = gathered_ref.shape
     half = high // 3
     padded = shards // 2 * LANES
@@ -86,13 +86,10 @@
     features = weights_ref.shape[1]
     for at in range(0, features, 2 * LANES):
         to = min(at + 2 * LANES, features)
-        value = jnp.dot(
+        rows_ref[:, at:to] = jnp.dot(
             hidden_ref[:, : 2 * padded],
             weights_ref[: 2 * padded, at:to],
             preferred_element_type=F32,
-        ).astype(BF16)
-        rows_ref[:, at:to] = jnp.dot(
-            order_ref[...], value, preferred_element_type=F32
         ).astype(BF16)
 
 
@@ -104,6 +101,14 @@
     hidden_units = w_gate.shape[1]
     heavy = members // 4
     rows = members * 4 + heavy * 2
+
+    with jax.named_scope("gather_chips"):
+        both = jnp.concatenate([inputs, upstream], axis=1)[None]
+        got = exchange(copies(dense(both)[0], members // CORES), "dp", CORE_GROUPS)
+        got, lengths, move_dest, w_gate, w_up, w_down = lax.optimization_barrier(
+            (got, lengths, move_dest, w_gate, w_up, w_down)
+        )
+        theirs = lax.ppermute(got, "dp", [(i, i ^ 1) for i in range(members)])
 
     is_full = lengths == capacity
     full_rank = jnp.cumsum(is_full.astype(jnp.int32)) - is_full
@@ -121,28 +126,25 @@
         ),
     )
     place = jnp.where(row < lengths[:, None], place, -1)
-    place = place.reshape(-1, CORES, capacity).transpose(1, 0, 2)
-    place = jnp.where(core == 0, place[0], place[1]).reshape(-1)
-    kept_row = jnp.arange(rows, dtype=jnp.int32)[None, :]
-    pick = (kept_row.T == place[None, :]).astype(BF16)
-    middle = jnp.where(is_full, members * 4 + full_rank * 2, -2)[:, None]
-    pair = jnp.arange(2, dtype=jnp.int32)[None, :]
-    none = jnp.full((members, 2), -1, jnp.int32)
-    source = [learner * 4 + pair, middle + pair, learner * 4 + 2 + pair, none]
-    source = jnp.concatenate(source, axis=1).reshape(-1)
-    order = (source[:, None] == kept_row).astype(BF16)
+    place = place.reshape(-1, CORES, capacity).transpose(1, 0, 2).reshape(CORES, -1)
+    place = jnp.where(core == 0, place, place[::-1])
+    kept_row = jnp.arange(rows, dtype=jnp.int32)
+    pick = (kept_row[None, :, None] == place[:, None, :]).astype(BF16)
+    full = jnp.where(is_full, full_rank, -1)
+    spread = (full[:, None] == jnp.arange(heavy, dtype=jnp.int32)[None, :]).astype(BF16)
     grad_scale = lax.rsqrt(jnp.sum(lengths).astype(F32))
     weights = jnp.concatenate([pad_hidden(w) for w in (w_gate.T, w_up.T, w_down)], axis=0)
     padded = weights.shape[0] // 3
 
-    with jax.named_scope("gather_chips"):
-        both = jnp.concatenate([inputs, upstream], axis=1)[None]
-        got = exchange(copies(dense(both)[0], members // CORES), "dp", CORE_GROUPS)
-        got, weights, order = lax.optimization_barrier((got, weights, order))
-        got = undense(got, capacity).reshape(-1, 2 * features)
     with jax.named_scope("gather_core"):
-        mine = jnp.dot(pick, got, preferred_element_type=F32).astype(BF16)
-        other = lax.ppermute(mine, "dp", [(i, i ^ 1) for i in range(members)])
+        mine, other = [
+            jnp.dot(
+                pick[which],
+                undense(part, capacity).reshape(-1, 2 * features),
+                preferred_element_type=F32,
+            ).astype(BF16)
+            for which, part in enumerate((got, theirs))
+        ]
     with jax.named_scope("partial_sums"):
         kept, partial = call(
             sums_kernel,
@@ -175,15 +177,24 @@
             rows_kernel,
             [
                 jax.ShapeDtypeStruct((rows, 3 * padded), BF16),
-                jax.ShapeDtypeStruct((order.shape[0], features), BF16),
+                jax.ShapeDtypeStruct((rows, features), BF16),
             ],
-            2 * rows * features * (2 * padded + order.shape[0]),
+            2 * rows * features * 2 * padded,
             gathered,
             weights,
-            order,
-        )
-        arrived = exchange(grad_rows.reshape(members, -1, features), "dp")
-        grad_inputs = jnp.sum(arrived.astype(F32), axis=0)[: capacity // 2].astype(BF16)
+        )
+        outer = grad_rows[: members * 4].reshape(members, 2, 2, features)
+        middle = jnp.einsum(
+            "lh,htf->ltf",
+            spread,
+            grad_rows[members * 4 :].reshape(heavy, 2, features),
+            preferred_element_type=F32,
+        ).astype(BF16)
+        slots = jnp.stack([outer[:, 0], middle, outer[:, 1]], axis=1).reshape(members, 6, features)
+        message = jnp.pad(dense(slots), ((0, 0), (0, 2), (0, 0)))
+        arrived = exchange(message, "dp")
+        grad_inputs = jnp.sum(arrived.astype(F32), axis=0, keepdims=True)[:, :-2].astype(BF16)
+        grad_inputs = undense(grad_inputs, 6)[0]
 
     contract_rows = (((0,), (0,)), ((), ()))
     with jax.named_scope("grad_weights"):

time: 126 us -> 125 us (level)
  blocking collectives: 33.1 us -> 18.1 us
  waiting for transfers between devices: 39.8 us -> 50.3 us
  local copies, waits for them, and re-layouts: 4.72 us -> 9.18 us
  starting transfers between devices: 32.7 us -> 37.1 us
  other arithmetic: 6.41 us -> 3.23 us
  Pallas kernels: 3.89 us -> 1.61 us
    all_to_all x2 -> x1, blocking collectives: 33.1 us -> 18.1 us  [exchange(): return lax.all_to_all(x, axis, 0, 0, tiled=True, axis_index_groups=groups)]
    all_to_all x2 -> x3, waiting for transfers between devices: 37.9 us -> 49.9 us  [exchange(): return lax.all_to_all(x, axis, 0, 0, tiled=True, axis_index_groups=groups)]
    all_to_all x2 -> x3, starting transfers between devices: 26.8 us -> 31.2 us  [exchange(): return lax.all_to_all(x, axis, 0, 0, tiled=True, axis_index_groups=groups)]
    pallas_call x2, Pallas kernels: 3.89 us -> 1.61 us  [call(): pl.pallas_call(kernel, out_shape=outs, in_specs=[whole] * len(operands),...]
    reduce_sum x1, other arithmetic: 1.82 us -> 0.1 us  [body(): jnp.sum(arrived.astype(F32), axis=0, keepdims=True)[:, :-2].astype(BF16)]
    reshape x0 -> x5, local copies, waits for them, and re-layouts: none -> 1.42 us  [the longest x1 0.61 us: undense(): x = x.reshape(n, tiles, rows, LANES).transpose(0, 2, 1, 3)]
    concatenate x1, other arithmetic: 1.54 us -> 0.16 us  [body(): jnp.concatenate([pad_hidden(w) for w in (w_gate.T, w_up.T, w_down)], axis=0)]
    ppermute x1, waiting for transfers between devices: 1.82 us -> 0.46 us  [body(): theirs = lax.ppermute(got, 'dp', [(i, i ^ 1) for i in range(members)])]
  transfers between devices with their start and end apart: 3 -> 4, of which waited for: 3 -> 4; matrix products, arithmetic and copies ran while one was open for 6% -> 4% of each run, Pallas kernels for 0% -> 0%
where the time goes in v6:
time: 125 us; the launch traced here: 124 us
  waiting for transfers between devices  50.3 us (40%)
  starting transfers between devices  37.1 us (30%)
  blocking collectives  18.1 us (14%)
  local copies, waits for them, and re-layouts  9.18 us (7%)
  other arithmetic  3.23 us (3%)
  matrix products  2.99 us (2%)
  between operations  1.73 us (1%)
  Pallas kernels  1.61 us (1%)
    all_to_all x3, waiting for transfers between devices, exchange(): return lax.all_to_all(x, axis, 0, 0, tiled=True, axis_index_groups=groups)  49.9 us
    all_to_all x3, starting transfers between devices, exchange(): return lax.all_to_all(x, axis, 0, 0, tiled=True, axis_index_groups=groups)  31.2 us
    all_to_all x1, blocking collectives, exchange(): return lax.all_to_all(x, axis, 0, 0, tiled=True, axis_index_groups=groups)  18.1 us
    ppermute x1, starting transfers between devices, body(): theirs = lax.ppermute(got, 'dp', [(i, i ^ 1) for i in range(members)])  5.88 us
  transfers between devices with their start and end apart: 4, of which 4 were waited for; matrix products, arithmetic and copies ran while one was open for 4% of the time, Pallas kernels for 0%

profile of v6, /device:TPU:1, one launch (start us, length us, event | category | flops | bytes accessed | tf_op | source)
XLA Modules:
  0.0 124.2 jit_solution(14160622790865947549)
XLA Ops:
  0.7 0.8 pad_maximum_fusion.2
  1.5 1.1 broadcast_in_dim.60
  2.6 16.5 %all-to-all-start = ((bf16[32,120,128]{2,1,0:T(8,128)(2,1)}), bf16[32,120,128]{2,1,0:T(8,128)(2,1)S(1)}, u32[]{:S(2)}, u32[]{:S(2)}) async-start(bf16[32,120,128]{2,1,0:T(8,128)(2,1)} %broadcast_in_dim.60), calls=%async_computation | async-start | bytes 1966080 | tf_op jit(solution)/shard_map/gather_chips/all_to_all | solution.py:16
  19.1 25.3 %all-to-all-done = bf16[32,120,128]{2,1,0:T(8,128)(2,1)S(1)} async-done(((bf16[32,120,128]{2,1,0:T(8,128)(2,1)}), bf16[32,120,128]{2,1,0:T(8,128)(2,1)S(1)}, u32[]{:S(2)}, u32[]{:S(2)}) %all-to-all-start) | async-done | bytes 983072 | tf_op jit(solution)/shard_map/gather_chips/all_to_all | solution.py:16
  44.7 0.6 compare_select_fusion
  45.8 0.2 copy.30
  46.0 5.9 %collective-permute-start = (bf16[32,120,128]{2,0,1:T(8,128)(2,1)S(1)}, bf16[32,120,128]{2,0,1:T(8,128)(2,1)S(1)}, u32[]{:S(2)}, u32[]{:S(2)}) collective-permute-start(bf16[32,120,128]{2,0,1:T(8,128)(2,1)S(1)} %copy.30), channel_id=1, source_target_pairs={{0,8},{8,0},{16,24},{24,16},{32,40},{40,32},{48,56},{56,48},{64,72... | collective-permute-start | bytes 2949128 | tf_op jit(solution)/shard_map/gather_chips/ppermute | solution.py:111
  51.9 0.7 copy.31
  52.8 0.6 convolution_convert_fusion.1.mine_ref
  53.4 0.2 fusion.5.weights_ref
  53.6 0.5 collective-permute-done
  54.0 0.7 copy.33
  54.7 0.6 convolution_convert_fusion.other_ref
  55.3 0.9 partial_sums.1
  56.3 18.1 %all_to_all.20 = bf16[8,432,128]{2,1,0:T(8,128)(2,1)S(1)} all-to-all(bf16[8,432,128]{2,1,0:T(8,128)(2,1)S(1)} %get-tuple-element.20), channel_id=1, replica_groups=mesh['dp'=64,'fsdp'=8] {'fsdp'}, dimensions={0} | all-to-all | bytes 1769472 | tf_op jit(solution)/shard_map/sum_features/all_to_all | solution.py:16
  74.6 1.1 broadcast_in_dim.66
  75.7 3.5 %all-to-all-start.2 = ((bf16[8,432,128]{2,1,0:T(8,128)(2,1)}), bf16[8,432,128]{2,1,0:T(8,128)(2,1)S(1)}, u32[]{:S(2)}, u32[]{:S(2)}) async-start(bf16[8,432,128]{2,1,0:T(8,128)(2,1)} %broadcast_in_dim.66), calls=%async_computation.2 | async-start | bytes 1769472 | tf_op jit(solution)/shard_map/gather_hidden/all_to_all | solution.py:16
  79.9 9.4 %all-to-all-done.2.gathered_ref = bf16[8,432,128]{2,1,0:T(8,128)(2,1)S(1)} async-done(((bf16[8,432,128]{2,1,0:T(8,128)(2,1)}), bf16[8,432,128]{2,1,0:T(8,128)(2,1)S(1)}, u32[]{:S(2)}, u32[]{:S(2)}) %all-to-all-start.2) | async-done | bytes 884768 | tf_op jit(solution)/shard_map/gather_hidden/all_to_all | solution.py:16
  89.3 0.7 grad_rows.1
  90.0 0.9 copy-done.2
  91.1 0.2 fusion.24
  91.4 0.3 fusion.6
  91.8 0.6 reshape.136
  92.5 0.3 copy.41
  92.8 0.9 pad.18.clone
  93.7 11.1 %all-to-all-start.3 = ((bf16[64,32,128]{2,1,0:T(8,128)(2,1)}), bf16[64,32,128]{2,1,0:T(8,128)(2,1)S(1)}, u32[]{:S(2)}, u32[]{:S(2)}) async-start(bf16[64,32,128]{2,1,0:T(8,128)(2,1)} %pad.18.clone), calls=%async_computation.3 | async-start | bytes 1048576 | tf_op jit(solution)/shard_map/grad_rows/all_to_all | solution.py:16
  104.8 0.6 fusion.13
  105.4 0.9 fusion.7
  106.3 1.0 multiply_convert_fusion
  107.2 1.1 slice_bitcast_fusion
  108.3 15.2 %all-to-all-done.3 = bf16[64,32,128]{2,1,0:T(8,128)(2,1)S(1)} async-done(((bf16[64,32,128]{2,1,0:T(8,128)(2,1)}), bf16[64,32,128]{2,1,0:T(8,128)(2,1)S(1)}, u32[]{:S(2)}, u32[]{:S(2)}) %all-to-all-start.3) | async-done | bytes 524320 | tf_op jit(solution)/shard_map/grad_rows/all_to_all | solution.py:16
  123.6 0.6 reshape.138
  (49 shorter events, 1.7 us)
Async XLA Ops:
  0.6 43.8 %copy-start.8 = (s32[64,3]{0,1:T(4,128)S(1)}, s32[64,3]{0,1:T(4,128)}, u32[]{:S(2)}) copy-start(s32[64,3]{0,1:T(4,128)} %param.13) | copy-start | bytes 2308
  0.6 43.8 %copy-start.7 = (s32[64]{0:T(128)S(1)}, s32[64]{0:T(128)}, u32[]{:S(2)}) copy-start(s32[64]{0:T(128)} %param.12) | copy-start | bytes 772
  2.6 41.8 %all-to-all-start = ((bf16[32,120,128]{2,1,0:T(8,128)(2,1)}), bf16[32,120,128]{2,1,0:T(8,128)(2,1)S(1)}, u32[]{:S(2)}, u32[]{:S(2)}) async-start(bf16[32,120,128]{2,1,0:T(8,128)(2,1)} %broadcast_in_dim.60), calls=%async_computation | async-start | bytes 1966080 | tf_op jit(solution)/shard_map/gather_chips/all_to_all | solution.py:16
  46.0 8.1 %collective-permute-start = (bf16[32,120,128]{2,0,1:T(8,128)(2,1)S(1)}, bf16[32,120,128]{2,0,1:T(8,128)(2,1)S(1)}, u32[]{:S(2)}, u32[]{:S(2)}) collective-permute-start(bf16[32,120,128]{2,0,1:T(8,128)(2,1)S(1)} %copy.30), channel_id=1, source_target_pairs={{0,8},{8,0},{16,24},{24,16},{32,40},{40,32},{48,56},{56,48},{64,72... | collective-permute-start | bytes 2949128 | tf_op jit(solution)/shard_map/gather_chips/ppermute | solution.py:111
  51.8 1.5 %copy-start.4 = (bf16[432,640]{1,0:T(8,128)(2,1)S(1)}, bf16[432,640]{1,0:T(8,128)(2,1)}, u32[]{:S(2)}) copy-start(bf16[432,640]{1,0:T(8,128)(2,1)} %param.11) | copy-start | bytes 1658884
  51.9 1.5 %copy-start.5 = (bf16[640,432]{0,1:T(8,128)(2,1)S(1)}, bf16[640,432]{0,1:T(8,128)(2,1)}, u32[]{:S(2)}) copy-start(bf16[640,432]{0,1:T(8,128)(2,1)} %param.10) | copy-start | bytes 1658884
  51.9 1.5 %copy-start.6 = (bf16[640,432]{0,1:T(8,128)(2,1)S(1)}, bf16[640,432]{0,1:T(8,128)(2,1)}, u32[]{:S(2)}) copy-start(bf16[640,432]{0,1:T(8,128)(2,1)} %param.9) | copy-start | bytes 1658884
  56.3 18.1 %copy-start = (bf16[288,1280]{1,0:T(8,128)(2,1)}, bf16[288,1280]{1,0:T(8,128)(2,1)S(1)}, u32[]{:S(2)}) copy-start(bf16[288,1280]{1,0:T(8,128)(2,1)S(1)} %get-tuple-element.23) | copy-start | bytes 2211844
  75.7 13.6 %all-to-all-start.2 = ((bf16[8,432,128]{2,1,0:T(8,128)(2,1)}), bf16[8,432,128]{2,1,0:T(8,128)(2,1)S(1)}, u32[]{:S(2)}, u32[]{:S(2)}) async-start(bf16[8,432,128]{2,1,0:T(8,128)(2,1)} %broadcast_in_dim.66), calls=%async_computation.2 | async-start | bytes 1769472 | tf_op jit(solution)/shard_map/gather_hidden/all_to_all | solution.py:16
  90.0 0.9 copy-start.2
  92.3 12.5 %copy-start.1 = (bf16[288,1280]{1,0:T(8,128)(2,1)S(1)}, bf16[288,1280]{1,0:T(8,128)(2,1)}, u32[]{:S(2)}) copy-start(bf16[288,1280]{1,0:T(8,128)(2,1)} %copy-done) | copy-start | bytes 2211844
  92.3 12.5 %copy-start.3 = (bf16[288,1536]{1,0:T(8,128)(2,1)S(1)}, bf16[288,1536]{1,0:T(8,128)(2,1)}, u32[]{:S(2)}) copy-start(bf16[288,1536]{1,0:T(8,128)(2,1)} %copy-done.2) | copy-start | bytes 2654212
  93.7 29.9 %all-to-all-start.3 = ((bf16[64,32,128]{2,1,0:T(8,128)(2,1)}), bf16[64,32,128]{2,1,0:T(8,128)(2,1)S(1)}, u32[]{:S(2)}, u32[]{:S(2)}) async-start(bf16[64,32,128]{2,1,0:T(8,128)(2,1)} %pad.18.clone), calls=%async_computation.3 | async-start | bytes 1048576 | tf_op jit(solution)/shard_map/grad_rows/all_to_all | solution.py:16

commit v7 on v6

--- a/solution.py
+++ b/solution.py
@@ -37,7 +37,7 @@
     return jnp.pad(weights, ((0, -weights.shape[0] % (4 * LANES)), (0, 0)))
 
 
-def call(kernel, outs, flops, *operands):
+def call(kernel, outs, flops, *operands, scratch=()):
     whole = pl.BlockSpec(memory_space=pltpu.VMEM)
     moved = sum(x.size * x.dtype.itemsize for x in (*operands, *outs))
     return pl.pallas_call(
@@ -45,6 +45,7 @@
         out_shape=outs,
         in_specs=[whole] * len(operands),
         out_specs=[whole] * len(outs),
+        scratch_shapes=scratch,
         cost_estimate=pl.CostEstimate(flops=flops, bytes_accessed=moved, transcendentals=0),
         compiler_params=pltpu.CompilerParams(vmem_limit_bytes=24 * 2**20),
     )(*operands)
@@ -72,13 +73,13 @@
                     ] = value[part * half : (part + 1) * half, tile * LANES : (tile + 1) * LANES]
 
 
-def rows_kernel(gathered_ref, weights_ref, hidden_ref, rows_ref):
+def rows_kernel(gathered_ref, weights_ref, rows_ref, hidden_ref):
     shards, high, _ = gathered_ref.shape
     half = high // 3
     padded = shards // 2 * LANES
     for shard in range(shards):
         tile, part = divmod(shard, 2)
-        for which in range(3):
+        for which in range(2):
             at = which * padded + tile * LANES
             hidden_ref[part * half : (part + 1) * half, at : at + LANES] = gathered_ref[
                 shard, which * half : (which + 1) * half, :
@@ -87,7 +88,7 @@
     for at in range(0, features, 2 * LANES):
         to = min(at + 2 * LANES, features)
         rows_ref[:, at:to] = jnp.dot(
-            hidden_ref[:, : 2 * padded],
+            hidden_ref[...],
             weights_ref[: 2 * padded, at:to],
             preferred_element_type=F32,
         ).astype(BF16)
@@ -101,14 +102,6 @@
     hidden_units = w_gate.shape[1]
     heavy = members // 4
     rows = members * 4 + heavy * 2
-
-    with jax.named_scope("gather_chips"):
-        both = jnp.concatenate([inputs, upstream], axis=1)[None]
-        got = exchange(copies(dense(both)[0], members // CORES), "dp", CORE_GROUPS)
-        got, lengths, move_dest, w_gate, w_up, w_down = lax.optimization_barrier(
-            (got, lengths, move_dest, w_gate, w_up, w_down)
-        )
-        theirs = lax.ppermute(got, "dp", [(i, i ^ 1) for i in range(members)])
 
     is_full = lengths == capacity
     full_rank = jnp.cumsum(is_full.astype(jnp.int32)) - is_full
@@ -126,25 +119,25 @@
         ),
     )
     place = jnp.where(row < lengths[:, None], place, -1)
-    place = place.reshape(-1, CORES, capacity).transpose(1, 0, 2).reshape(CORES, -1)
-    place = jnp.where(core == 0, place, place[::-1])
-    kept_row = jnp.arange(rows, dtype=jnp.int32)
-    pick = (kept_row[None, :, None] == place[:, None, :]).astype(BF16)
+    place = place.reshape(-1, CORES, capacity).transpose(1, 0, 2)
+    place = jnp.where(core == 0, place[0], place[1]).reshape(-1)
+    pick = (jnp.arange(rows, dtype=jnp.int32)[:, None] == place[None, :]).astype(BF16)
     full = jnp.where(is_full, full_rank, -1)
     spread = (full[:, None] == jnp.arange(heavy, dtype=jnp.int32)[None, :]).astype(BF16)
     grad_scale = lax.rsqrt(jnp.sum(lengths).astype(F32))
     weights = jnp.concatenate([pad_hidden(w) for w in (w_gate.T, w_up.T, w_down)], axis=0)
     padded = weights.shape[0] // 3
 
+    with jax.named_scope("gather_chips"):
+        both = jnp.concatenate([inputs, upstream], axis=1)[None]
+        got = exchange(copies(dense(both)[0], members // CORES), "dp", CORE_GROUPS)
+        got, pick, weights, spread, grad_scale = lax.optimization_barrier(
+            (got, pick, weights, spread, grad_scale)
+        )
+        got = undense(got, capacity).reshape(-1, 2 * features)
     with jax.named_scope("gather_core"):
-        mine, other = [
-            jnp.dot(
-                pick[which],
-                undense(part, capacity).reshape(-1, 2 * features),
-                preferred_element_type=F32,
-            ).astype(BF16)
-            for which, part in enumerate((got, theirs))
-        ]
+        mine = jnp.dot(pick, got, preferred_element_type=F32).astype(BF16)
+        other = lax.ppermute(mine, "dp", [(i, i ^ 1) for i in range(members)])
     with jax.named_scope("partial_sums"):
         kept, partial = call(
             sums_kernel,
@@ -173,15 +166,13 @@
         gathered = exchange(copies(shard, shards), "fsdp")
 
     with jax.named_scope("grad_rows"):
-        all_hidden, grad_rows = call(
+        (grad_rows,) = call(
             rows_kernel,
-            [
-                jax.ShapeDtypeStruct((rows, 3 * padded), BF16),
-                jax.ShapeDtypeStruct((rows, features), BF16),
-            ],
+            [jax.ShapeDtypeStruct((rows, features), BF16)],
             2 * rows * features * 2 * padded,
             gathered,
             weights,
+            scratch=[pltpu.VMEM((rows, 2 * padded), BF16)],
         )
         outer = grad_rows[: members * 4].reshape(members, 2, 2, features)
         middle = jnp.einsum(
@@ -191,13 +182,14 @@
             preferred_element_type=F32,
         ).astype(BF16)
         slots = jnp.stack([outer[:, 0], middle, outer[:, 1]], axis=1).reshape(members, 6, features)
-        message = jnp.pad(dense(slots), ((0, 0), (0, 2), (0, 0)))
-        arrived = exchange(message, "dp")
-        grad_inputs = jnp.sum(arrived.astype(F32), axis=0, keepdims=True)[:, :-2].astype(BF16)
+        arrived = exchange(dense(slots), "dp")
+        grad_inputs = jnp.sum(arrived.astype(F32), axis=0, keepdims=True).astype(BF16)
         grad_inputs = undense(grad_inputs, 6)[0]
 
     contract_rows = (((0,), (0,)), ((), ()))
     with jax.named_scope("grad_weights"):
+        all_hidden = gathered.reshape(padded // LANES, 2, 3, rows // 2, LANES)
+        all_hidden = all_hidden.transpose(1, 3, 2, 0, 4).reshape(rows, 3 * padded)
         in_total = lax.dot_general(
             all_hidden[:, : 2 * padded],
             kept[:, :features],

time: 125 us -> 122 us (0.976)
  blocking collectives: 18.1 us -> 33.1 us
  waiting for transfers between devices: 50.3 us -> 38 us
  starting transfers between devices: 37.1 us -> 32.5 us
  local copies, waits for them, and re-layouts: 9.18 us -> 7.18 us
  other arithmetic: 3.23 us -> 5.18 us
    all_to_all x1 -> x2, blocking collectives: 18.1 us -> 33.1 us  [exchange(): return lax.all_to_all(x, axis, 0, 0, tiled=True, axis_index_groups=groups)]
    all_to_all x3 -> x2, waiting for transfers between devices: 49.9 us -> 36.2 us  [exchange(): return lax.all_to_all(x, axis, 0, 0, tiled=True, axis_index_groups=groups)]
    all_to_all x3 -> x2, starting transfers between devices: 31.2 us -> 26.6 us  [exchange(): return lax.all_to_all(x, axis, 0, 0, tiled=True, axis_index_groups=groups)]
    ppermute x1, waiting for transfers between devices: 0.46 us -> 1.82 us  [body(): other = lax.ppermute(mine, 'dp', [(i, i ^ 1) for i in range(members)])]
    unnamed x21 -> x10, local copies, waits for them, and re-layouts: 1.34 us -> 0.06 us
  transfers between devices with their start and end apart: 4 -> 3, of which waited for: 4 -> 3; matrix products, arithmetic and copies ran while one was open for 4% -> 6% of each run, Pallas kernels for 0% -> 0%
where the time goes in v7:
time: 122 us
  waiting for transfers between devices  38 us (31%)
  blocking collectives  33.1 us (27%)
  starting transfers between devices  32.5 us (27%)
  local copies, waits for them, and re-layouts  7.18 us (6%)
  other arithmetic  5.18 us (4%)
  matrix products  2.31 us (2%)
  between operations  1.67 us (1%)
  Pallas kernels  1.58 us (1%)
    all_to_all x2, waiting for transfers between devices, exchange(): return lax.all_to_all(x, axis, 0, 0, tiled=True, axis_index_groups=groups)  36.2 us
    all_to_all x2, blocking collectives, exchange(): return lax.all_to_all(x, axis, 0, 0, tiled=True, axis_index_groups=groups)  33.1 us
    all_to_all x2, starting transfers between devices, exchange(): return lax.all_to_all(x, axis, 0, 0, tiled=True, axis_index_groups=groups)  26.6 us
    ppermute x1, starting transfers between devices, body(): other = lax.ppermute(mine, 'dp', [(i, i ^ 1) for i in range(members)])  5.88 us
  transfers between devices with their start and end apart: 3, of which 3 were waited for; matrix products, arithmetic and copies ran while one was open for 6% of the time, Pallas kernels for 0%

profile of v7, /device:TPU:1, one launch (start us, length us, event | category | flops | bytes accessed | tf_op | source)
XLA Modules:
  0.0 121.6 jit_solution(16221334946858216940)
XLA Ops:
  0.7 0.8 pad_maximum_fusion.2
  1.6 1.1 broadcast_in_dim.56
  2.6 16.5 %all-to-all-start = ((bf16[32,120,128]{2,1,0:T(8,128)(2,1)}), bf16[32,120,128]{2,1,0:T(8,128)(2,1)S(1)}, u32[]{:S(2)}, u32[]{:S(2)}) async-start(bf16[32,120,128]{2,1,0:T(8,128)(2,1)} %broadcast_in_dim.56), calls=%async_computation | async-start | bytes 1966080 | tf_op jit(solution)/shard_map/gather_chips/all_to_all | solution.py:16
  19.5 0.6 compare_select_fusion
  21.2 0.7 fusion.11
  22.0 1.4 %fusion.5.weights_ref = bf16[1536,640]{1,0:T(8,128)(2,1)S(1)} fusion(bf16[432,640]{1,0:T(8,128)(2,1)S(1)} %copy-done, bf16[432,640]{1,0:T(8,128)(2,1)} %bitcast.47, bf16[432,640]{1,0:T(8,128)(2,1)} %bitcast.48), kind=kLoop, calls=%fused_computation.11 | loop fusion | flops 13762560 | bytes 3624960 | tf_op jit(solution)/shard_map/concatenate | solution.py:128
  23.4 21.1 %all-to-all-done = bf16[32,120,128]{2,1,0:T(8,128)(2,1)S(1)} async-done(((bf16[32,120,128]{2,1,0:T(8,128)(2,1)}), bf16[32,120,128]{2,1,0:T(8,128)(2,1)S(1)}, u32[]{:S(2)}, u32[]{:S(2)}) %all-to-all-start) | async-done | bytes 983072 | tf_op jit(solution)/shard_map/gather_chips/all_to_all | solution.py:16
  44.5 0.2 copy.28
  44.6 0.7 copy.29
  45.4 0.6 convolution_convert_fusion.mine_ref
  45.9 5.9 %collective-permute-start = (bf16[288,1280]{1,0:T(8,128)(2,1)S(1)}, bf16[288,1280]{1,0:T(8,128)(2,1)S(1)}, u32[]{:S(2)}, u32[]{:S(2)}) collective-permute-start(bf16[288,1280]{1,0:T(8,128)(2,1)S(1)} %convolution_convert_fusion.mine_ref), channel_id=1, source_target_pairs={{0,8},{8,0},{16,24},{24,16},{32,40},{40,32},{48,56},{56,48},{64,72... | collective-permute-start | bytes 2211848 | tf_op jit(solution)/shard_map/gather_core/ppermute | solution.py:140
  51.8 1.8 %collective-permute-done.other_ref = bf16[288,1280]{1,0:T(8,128)(2,1)S(1)} collective-permute-done((bf16[288,1280]{1,0:T(8,128)(2,1)S(1)}, bf16[288,1280]{1,0:T(8,128)(2,1)S(1)}, u32[]{:S(2)}, u32[]{:S(2)}) %collective-permute-start) | collective-permute-done | bytes 737312 | tf_op jit(solution)/shard_map/gather_core/ppermute | solution.py:140
  53.6 0.9 partial_sums.1
  54.6 18.1 %all_to_all.20 = bf16[8,432,128]{2,1,0:T(8,128)(2,1)S(1)} all-to-all(bf16[8,432,128]{2,1,0:T(8,128)(2,1)S(1)} %get-tuple-element.14), channel_id=1, replica_groups=mesh['dp'=64,'fsdp'=8] {'fsdp'}, dimensions={0} | all-to-all | bytes 1769472 | tf_op jit(solution)/shard_map/sum_features/all_to_all | solution.py:16
  72.7 0.1 convert_reduce_fusion
  73.0 15.0 %all_to_all.21.gathered_ref = bf16[8,432,128]{2,1,0:T(8,128)(2,1)S(1)} all-to-all(bf16[8,432,128]{2,1,0:T(8,128)(2,1)S(1)} %broadcast_in_dim.63), channel_id=1, replica_groups=mesh['dp'=64,'fsdp'=8] {'fsdp'}, dimensions={0} | all-to-all | bytes 1769472 | tf_op jit(solution)/shard_map/gather_hidden/all_to_all | solution.py:16
  88.0 0.7 grad_rows.1
  88.8 0.5 copy.46
  89.2 0.3 reshape.155
  89.6 0.1 reshape.149
  89.7 0.2 fusion.23
  90.0 0.2 fusion.6
  90.3 0.6 reshape.151
  91.0 1.1 copy.34
  92.1 10.1 %all-to-all-start.3 = ((bf16[64,30,128]{2,1,0:T(8,128)(2,1)}), bf16[64,30,128]{2,1,0:T(8,128)(2,1)S(1)}, u32[]{:S(2)}, u32[]{:S(2)}) async-start(bf16[64,30,128]{2,1,0:T(8,128)(2,1)} %copy.34), calls=%async_computation.3 | async-start | bytes 1048576 | tf_op jit(solution)/shard_map/grad_rows/all_to_all | solution.py:16
  102.2 0.6 fusion.12
  102.8 0.9 fusion.7
  103.7 1.0 multiply_convert_fusion
  104.7 1.1 slice_bitcast_fusion
  105.8 15.1 %all-to-all-done.3 = bf16[64,30,128]{2,1,0:T(8,128)(2,1)S(1)} async-done(((bf16[64,30,128]{2,1,0:T(8,128)(2,1)}), bf16[64,30,128]{2,1,0:T(8,128)(2,1)S(1)}, u32[]{:S(2)}, u32[]{:S(2)}) %all-to-all-start.3) | async-done | bytes 491552 | tf_op jit(solution)/shard_map/grad_rows/all_to_all | solution.py:16
  120.9 0.1 reduce_sum.32
  121.0 0.6 convert_element_type.66
  (35 shorter events, 1.2 us)
Async XLA Ops:
  0.6 18.5 %copy-start.3 = (s32[64]{0:T(128)S(1)}, s32[64]{0:T(128)}, u32[]{:S(2)}) copy-start(s32[64]{0:T(128)} %param.12) | copy-start | bytes 772
  0.6 18.5 %copy-start.2 = (s32[64,3]{0,1:T(4,128)S(1)}, s32[64,3]{0,1:T(4,128)}, u32[]{:S(2)}) copy-start(s32[64,3]{0,1:T(4,128)} %param.13) | copy-start | bytes 2308
  0.7 21.3 %copy-start = (bf16[432,640]{1,0:T(8,128)(2,1)S(1)}, bf16[432,640]{1,0:T(8,128)(2,1)}, u32[]{:S(2)}) copy-start(bf16[432,640]{1,0:T(8,128)(2,1)} %param.11) | copy-start | bytes 1658884
  2.6 41.8 %all-to-all-start = ((bf16[32,120,128]{2,1,0:T(8,128)(2,1)}), bf16[32,120,128]{2,1,0:T(8,128)(2,1)S(1)}, u32[]{:S(2)}, u32[]{:S(2)}) async-start(bf16[32,120,128]{2,1,0:T(8,128)(2,1)} %broadcast_in_dim.56), calls=%async_computation | async-start | bytes 1966080 | tf_op jit(solution)/shard_map/gather_chips/all_to_all | solution.py:16
  23.4 22.0 %copy-start.1 = (bf16[288,384]{1,0:T(8,128)(2,1)S(1)}, bf16[288,384]{1,0:T(8,128)(2,1)}, u32[]{:S(2)}) copy-start(bf16[288,384]{1,0:T(8,128)(2,1)} %fusion.11) | copy-start | bytes 663556
  45.9 7.7 %collective-permute-start = (bf16[288,1280]{1,0:T(8,128)(2,1)S(1)}, bf16[288,1280]{1,0:T(8,128)(2,1)S(1)}, u32[]{:S(2)}, u32[]{:S(2)}) collective-permute-start(bf16[288,1280]{1,0:T(8,128)(2,1)S(1)} %convolution_convert_fusion.mine_ref), channel_id=1, source_target_pairs={{0,8},{8,0},{16,24},{24,16},{32,40},{40,32},{48,56},{56,48},{64,72... | collective-permute-start | bytes 2211848 | tf_op jit(solution)/shard_map/gather_core/ppermute | solution.py:140
  92.1 28.8 %all-to-all-start.3 = ((bf16[64,30,128]{2,1,0:T(8,128)(2,1)}), bf16[64,30,128]{2,1,0:T(8,128)(2,1)S(1)}, u32[]{:S(2)}, u32[]{:S(2)}) async-start(bf16[64,30,128]{2,1,0:T(8,128)(2,1)} %copy.34), calls=%async_computation.3 | async-start | bytes 1048576 | tf_op jit(solution)/shard_map/grad_rows/all_to_all | solution.py:16

commit v8 on v7

--- a/solution.py
+++ b/solution.py
@@ -1,3 +1,5 @@
+import functools
+
 import jax
 import jax.numpy as jnp
 from jax import lax
@@ -39,11 +41,12 @@
 
 def call(kernel, outs, flops, *operands, scratch=()):
     whole = pl.BlockSpec(memory_space=pltpu.VMEM)
+    scalars = pl.BlockSpec(memory_space=pltpu.SMEM)
     moved = sum(x.size * x.dtype.itemsize for x in (*operands, *outs))
     return pl.pallas_call(
         kernel,
         out_shape=outs,
-        in_specs=[whole] * len(operands),
+        in_specs=[scalars if x.ndim == 1 else whole for x in operands],
         out_specs=[whole] * len(outs),
         scratch_shapes=scratch,
         cost_estimate=pl.CostEstimate(flops=flops, bytes_accessed=moved, transcendentals=0),
@@ -73,7 +76,7 @@
                     ] = value[part * half : (part + 1) * half, tile * LANES : (tile + 1) * LANES]
 
 
-def rows_kernel(gathered_ref, weights_ref, rows_ref, hidden_ref):
+def rows_kernel(shared, core_ref, gathered_ref, weights_ref, own_ref, send_ref, hidden_ref, all_ref):
     shards, high, _ = gathered_ref.shape
     half = high // 3
     padded = shards // 2 * LANES
@@ -87,17 +90,22 @@
     features = weights_ref.shape[1]
     for at in range(0, features, 2 * LANES):
         to = min(at + 2 * LANES, features)
-        rows_ref[:, at:to] = jnp.dot(
+        all_ref[:, at:to] = jnp.dot(
             hidden_ref[...],
             weights_ref[: 2 * padded, at:to],
             preferred_element_type=F32,
-        ).astype(BF16)
+        )
+    owned = (all_ref.shape[0] - shared) // CORES
+    core = core_ref[0]
+    for out_ref, which in ((own_ref, core), (send_ref, 1 - core)):
+        out_ref[:owned, :] = all_ref[pl.ds(pl.multiple_of(which * owned, owned), owned), :]
+        out_ref[owned:, :] = all_ref[CORES * owned :, :]
 
 
 def body(inputs, upstream, w_gate, w_up, w_down, lengths, move_dest):
     members = lax.axis_size("dp")
     shards = lax.axis_size("fsdp")
-    core = lax.axis_index("dp") & 1
+    core = (lax.axis_index("dp") & 1).astype(jnp.int32)
     capacity, features = inputs.shape
     hidden_units = w_gate.shape[1]
     heavy = members // 4
@@ -107,22 +115,25 @@
     full_rank = jnp.cumsum(is_full.astype(jnp.int32)) - is_full
     learner = jnp.arange(members, dtype=jnp.int32)[:, None]
     row = jnp.arange(capacity, dtype=jnp.int32)[None, :]
-    target = jnp.repeat(move_dest, 2, axis=1)
+    chips = members // CORES
+    first = ((learner & 1) * chips + (learner >> 1)) * 4
+    target = jnp.repeat(((move_dest & 1) * chips + (move_dest >> 1)) * 4, 2, axis=1)
     target = jnp.concatenate([jnp.zeros_like(target), target], axis=1)
     place = jnp.where(
         row < 2,
-        learner * 4 + row,
+        first + row,
         jnp.where(
             row < 4,
             members * 4 + full_rank[:, None] * 2 + row - 2,
-            jnp.where(row < 6, learner * 4 + row - 2, target * 4 + 2 + row % 2),
+            jnp.where(row < 6, first + row - 2, target + 2 + row % 2),
         ),
     )
     place = jnp.where(row < lengths[:, None], place, -1)
     place = place.reshape(-1, CORES, capacity).transpose(1, 0, 2)
     place = jnp.where(core == 0, place[0], place[1]).reshape(-1)
     pick = (jnp.arange(rows, dtype=jnp.int32)[:, None] == place[None, :]).astype(BF16)
-    full = jnp.where(is_full, full_rank, -1)
+    full = jnp.where(is_full, full_rank, -1).reshape(-1, CORES)
+    full = jnp.where(core == 0, full[:, 0], full[:, 1])
     spread = (full[:, None] == jnp.arange(heavy, dtype=jnp.int32)[None, :]).astype(BF16)
     grad_scale = lax.rsqrt(jnp.sum(lengths).astype(F32))
     weights = jnp.concatenate([pad_hidden(w) for w in (w_gate.T, w_up.T, w_down)], axis=0)
@@ -166,23 +177,27 @@
         gathered = exchange(copies(shard, shards), "fsdp")
 
     with jax.named_scope("grad_rows"):
-        (grad_rows,) = call(
-            rows_kernel,
-            [jax.ShapeDtypeStruct((rows, features), BF16)],
+        own, send = call(
+            functools.partial(rows_kernel, 2 * heavy),
+            [jax.ShapeDtypeStruct((2 * members + 2 * heavy, features), F32)] * 2,
             2 * rows * features * 2 * padded,
+            core[None],
             gathered,
             weights,
-            scratch=[pltpu.VMEM((rows, 2 * padded), BF16)],
-        )
-        outer = grad_rows[: members * 4].reshape(members, 2, 2, features)
+            scratch=[pltpu.VMEM((rows, 2 * padded), BF16), pltpu.VMEM((rows, features), F32)],
+        )
+        own, send, gathered = lax.optimization_barrier((own, send, gathered))
+        grad_rows = own + lax.ppermute(send, "dp", [(i, i ^ 1) for i in range(members)])
+        grad_rows = grad_rows.astype(BF16)
+        outer = grad_rows[: 2 * members].reshape(chips, 2, 2, features)
         middle = jnp.einsum(
             "lh,htf->ltf",
             spread,
-            grad_rows[members * 4 :].reshape(heavy, 2, features),
+            grad_rows[2 * members :].reshape(heavy, 2, features),
             preferred_element_type=F32,
         ).astype(BF16)
-        slots = jnp.stack([outer[:, 0], middle, outer[:, 1]], axis=1).reshape(members, 6, features)
-        arrived = exchange(dense(slots), "dp")
+        slots = jnp.stack([outer[:, 0], middle, outer[:, 1]], axis=1).reshape(chips, 6, features)
+        arrived = exchange(dense(slots), "dp", CORE_GROUPS)
         grad_inputs = jnp.sum(arrived.astype(F32), axis=0, keepdims=True).astype(BF16)
         grad_inputs = undense(grad_inputs, 6)[0]
 

time: 122 us -> 123 us (level); the launches traced: 122 us -> 121 us
  waiting for transfers between devices: 38 us -> 33.4 us
  matrix products: 2.31 us -> 4.4 us
  starting transfers between devices: 32.5 us -> 34 us
    ppermute x0 -> x1, starting transfers between devices: none -> 4.74 us  [body(): lax.ppermute(send, 'dp', [(i, i ^ 1) for i in range(members)])]
    all_to_all x2, waiting for transfers between devices: 36.2 us -> 31.6 us  [exchange(): return lax.all_to_all(x, axis, 0, 0, tiled=True, axis_index_groups=groups)]
    all_to_all x2, starting transfers between devices: 26.6 us -> 23.4 us  [exchange(): return lax.all_to_all(x, axis, 0, 0, tiled=True, axis_index_groups=groups)]
  transfers between devices with their start and end apart: 3 -> 4, of which waited for: 3 -> 3; matrix products, arithmetic and copies ran while one was open for 6% -> 9% of each run, Pallas kernels for 0% -> 0%
where the time goes in v8:
time: 123 us; the launch traced here: 121 us
  starting transfers between devices  34 us (28%)
  waiting for transfers between devices  33.4 us (27%)
  blocking collectives  33.1 us (27%)
  local copies, waits for them, and re-layouts  7.36 us (6%)
  other arithmetic  5.33 us (4%)
  matrix products  4.4 us (4%)
  between operations  1.68 us (1%)
  Pallas kernels  1.58 us (1%)
    all_to_all x2, blocking collectives, exchange(): return lax.all_to_all(x, axis, 0, 0, tiled=True, axis_index_groups=groups)  33.1 us
    all_to_all x2, waiting for transfers between devices, exchange(): return lax.all_to_all(x, axis, 0, 0, tiled=True, axis_index_groups=groups)  31.6 us
    all_to_all x2, starting transfers between devices, exchange(): return lax.all_to_all(x, axis, 0, 0, tiled=True, axis_index_groups=groups)  23.4 us
    ppermute x1, starting transfers between devices, body(): other = lax.ppermute(mine, 'dp', [(i, i ^ 1) for i in range(members)])  5.88 us
    ppermute x1, starting transfers between devices, body(): lax.ppermute(send, 'dp', [(i, i ^ 1) for i in range(members)])  4.74 us
  transfers between devices with their start and end apart: 4, of which 3 were waited for; matrix products, arithmetic and copies ran while one was open for 9% of the time, Pallas kernels for 0%

profile of v8, /device:TPU:1, one launch (start us, length us, event | category | flops | bytes accessed | tf_op | source)
XLA Modules:
  0.0 120.9 jit_solution(1214390265530822554)
XLA Ops:
  0.7 0.8 pad_maximum_fusion.2
  1.6 1.1 broadcast_in_dim.60
  2.6 16.5 %all-to-all-start = ((bf16[32,120,128]{2,1,0:T(8,128)(2,1)}), bf16[32,120,128]{2,1,0:T(8,128)(2,1)S(1)}, u32[]{:S(2)}, u32[]{:S(2)}) async-start(bf16[32,120,128]{2,1,0:T(8,128)(2,1)} %broadcast_in_dim.60), calls=%async_computation | async-start | bytes 1966080 | tf_op jit(solution)/shard_map/gather_chips/all_to_all | solution.py:18
  19.5 0.6 compare_select_fusion
  21.3 0.2 fusion.19
  21.5 0.7 fusion.11
  22.3 1.4 %fusion.5.weights_ref = bf16[1536,640]{1,0:T(8,128)(2,1)S(1)} fusion(bf16[432,640]{1,0:T(8,128)(2,1)S(1)} %copy-done.2, bf16[432,640]{1,0:T(8,128)(2,1)} %bitcast.48, bf16[432,640]{1,0:T(8,128)(2,1)} %bitcast.49), kind=kLoop, calls=%fused_computation.11 | loop fusion | flops 13762560 | bytes 3624960 | tf_op jit(solution)/shard_map/concatenate | solution.py:139
  23.7 20.8 %all-to-all-done = bf16[32,120,128]{2,1,0:T(8,128)(2,1)S(1)} async-done(((bf16[32,120,128]{2,1,0:T(8,128)(2,1)}), bf16[32,120,128]{2,1,0:T(8,128)(2,1)S(1)}, u32[]{:S(2)}, u32[]{:S(2)}) %all-to-all-start) | async-done | bytes 983072 | tf_op jit(solution)/shard_map/gather_chips/all_to_all | solution.py:18
  44.5 0.2 copy.28
  44.6 0.7 copy.29
  45.4 0.6 convolution_convert_fusion.mine_ref
  45.9 5.9 %collective-permute-start = (bf16[288,1280]{1,0:T(8,128)(2,1)S(1)}, bf16[288,1280]{1,0:T(8,128)(2,1)S(1)}, u32[]{:S(2)}, u32[]{:S(2)}) collective-permute-start(bf16[288,1280]{1,0:T(8,128)(2,1)S(1)} %convolution_convert_fusion.mine_ref), channel_id=1, source_target_pairs={{0,8},{8,0},{16,24},{24,16},{32,40},{40,32},{48,56},{56,48},{64,72... | collective-permute-start | bytes 2211848 | tf_op jit(solution)/shard_map/gather_core/ppermute | solution.py:151
  51.8 1.8 %collective-permute-done.other_ref = bf16[288,1280]{1,0:T(8,128)(2,1)S(1)} collective-permute-done((bf16[288,1280]{1,0:T(8,128)(2,1)S(1)}, bf16[288,1280]{1,0:T(8,128)(2,1)S(1)}, u32[]{:S(2)}, u32[]{:S(2)}) %collective-permute-start) | collective-permute-done | bytes 737312 | tf_op jit(solution)/shard_map/gather_core/ppermute | solution.py:151
  53.6 0.9 partial_sums.1
  54.5 18.1 %all_to_all.20 = bf16[8,432,128]{2,1,0:T(8,128)(2,1)S(1)} all-to-all(bf16[8,432,128]{2,1,0:T(8,128)(2,1)S(1)} %get-tuple-element.19), channel_id=1, replica_groups=mesh['dp'=64,'fsdp'=8] {'fsdp'}, dimensions={0} | all-to-all | bytes 1769472 | tf_op jit(solution)/shard_map/sum_features/all_to_all | solution.py:18
  72.7 0.1 convert_reduce_fusion
  72.9 0.1 broadcast_in_dim.67
  73.0 15.0 %all_to_all.21.gathered_ref = bf16[8,432,128]{2,1,0:T(8,128)(2,1)S(1)} all-to-all(bf16[8,432,128]{2,1,0:T(8,128)(2,1)S(1)} %broadcast_in_dim.67), channel_id=1, replica_groups=mesh['dp'=64,'fsdp'=8] {'fsdp'}, dimensions={0} | all-to-all | bytes 1769472 | tf_op jit(solution)/shard_map/gather_hidden/all_to_all | solution.py:18
  88.0 0.7 grad_rows.1
  88.7 4.7 %collective-permute-start.1 = (f32[160,640]{1,0:T(8,128)S(1)}, f32[160,640]{1,0:T(8,128)S(1)}, u32[]{:S(2)}, u32[]{:S(2)}) collective-permute-start(f32[160,640]{1,0:T(8,128)S(1)} %get-tuple-element.23), channel_id=1, source_target_pairs={{0,8},{8,0},{16,24},{24,16},{32,40},{40,32},{48,56},{56,48},{64,72... | collective-permute-start | bytes 1228808 | tf_op jit(solution)/shard_map/grad_rows/ppermute | solution.py:190
  93.5 0.5 copy.46
  93.9 1.3 %reshape.168 = bf16[288,1536]{1,0:T(8,128)(2,1)} reshape(bf16[2,144,3,4,128]{4,3,2,1,0:T(4,128)(2,1)S(1)} %bitcast.44) | data formatting | bytes 1769472 | tf_op jit(solution)/shard_map/grad_weights/reshape | solution.py:207
  95.2 1.6 %fusion.12 = f32[512,640]{1,0:T(8,128)S(1)} fusion(bf16[288,1280]{1,0:T(8,128)(2,1)S(1)} %get-tuple-element.26, bf16[288,1536]{1,0:T(8,128)(2,1)} %reshape.168), kind=kOutput, calls=%fused_computation.26 | convolution fusion | flops 188743680 | bytes 1974272 | tf_op jit(solution)/shard_map/grad_weights/dot_general | solution.py:215
  96.8 2.0 %multiply_convert_fusion = bf16[1024,640]{1,0:T(8,128)(2,1)} fusion(f32[]{:T(128)S(6)} %rsqrt.3, bf16[288,1536]{1,0:T(8,128)(2,1)S(1)} %copy-done, bf16[288,1280]{1,0:T(8,128)(2,1)S(1)} %get-tuple-element.26), kind=kOutput, calls=%fused_computation.9 | convolution fusion | flops 378798080 | bytes 2269188 | tf_op jit(solution)/shard_map/grad_weights/dot_general | solution.py:208
  99.2 0.2 fusion.6
  99.4 0.3 reshape.164
  99.8 0.8 copy.34
  100.6 6.9 %all-to-all-start.3 = ((bf16[32,30,128]{2,1,0:T(8,128)(2,1)}), bf16[32,30,128]{2,1,0:T(8,128)(2,1)S(1)}, u32[]{:S(2)}, u32[]{:S(2)}) async-start(bf16[32,30,128]{2,1,0:T(8,128)(2,1)} %copy.34), calls=%async_computation.3 | async-start | bytes 524288 | tf_op jit(solution)/shard_map/grad_rows/all_to_all | solution.py:18
  107.5 0.9 fusion.7
  108.3 1.1 slice_bitcast_fusion
  109.4 10.8 %all-to-all-done.3 = bf16[32,30,128]{2,1,0:T(8,128)(2,1)S(1)} async-done(((bf16[32,30,128]{2,1,0:T(8,128)(2,1)}), bf16[32,30,128]{2,1,0:T(8,128)(2,1)S(1)}, u32[]{:S(2)}, u32[]{:S(2)}) %all-to-all-start.3) | async-done | bytes 245792 | tf_op jit(solution)/shard_map/grad_rows/all_to_all | solution.py:18
  120.3 0.6 convert_element_type.70
  (45 shorter events, 1.4 us)
Async XLA Ops:
  0.6 18.5 %copy-start.5 = (s32[64]{0:T(128)S(1)}, s32[64]{0:T(128)}, u32[]{:S(2)}) copy-start(s32[64]{0:T(128)} %param.12) | copy-start | bytes 772
  0.6 18.5 %copy-start.4 = (s32[64,3]{0,1:T(4,128)S(1)}, s32[64,3]{0,1:T(4,128)}, u32[]{:S(2)}) copy-start(s32[64,3]{0,1:T(4,128)} %param.13) | copy-start | bytes 2308
  0.7 21.6 %copy-start.2 = (bf16[432,640]{1,0:T(8,128)(2,1)S(1)}, bf16[432,640]{1,0:T(8,128)(2,1)}, u32[]{:S(2)}) copy-start(bf16[432,640]{1,0:T(8,128)(2,1)} %param.11) | copy-start | bytes 1658884
  2.6 41.8 %all-to-all-start = ((bf16[32,120,128]{2,1,0:T(8,128)(2,1)}), bf16[32,120,128]{2,1,0:T(8,128)(2,1)S(1)}, u32[]{:S(2)}, u32[]{:S(2)}) async-start(bf16[32,120,128]{2,1,0:T(8,128)(2,1)} %broadcast_in_dim.60), calls=%async_computation | async-start | bytes 1966080 | tf_op jit(solution)/shard_map/gather_chips/all_to_all | solution.py:18
  23.7 21.7 %copy-start.3 = (bf16[288,384]{1,0:T(8,128)(2,1)S(1)}, bf16[288,384]{1,0:T(8,128)(2,1)}, u32[]{:S(2)}) copy-start(bf16[288,384]{1,0:T(8,128)(2,1)} %fusion.11) | copy-start | bytes 663556
  45.9 7.7 %collective-permute-start = (bf16[288,1280]{1,0:T(8,128)(2,1)S(1)}, bf16[288,1280]{1,0:T(8,128)(2,1)S(1)}, u32[]{:S(2)}, u32[]{:S(2)}) collective-permute-start(bf16[288,1280]{1,0:T(8,128)(2,1)S(1)} %convolution_convert_fusion.mine_ref), channel_id=1, source_target_pairs={{0,8},{8,0},{16,24},{24,16},{32,40},{40,32},{48,56},{56,48},{64,72... | collective-permute-start | bytes 2211848 | tf_op jit(solution)/shard_map/gather_core/ppermute | solution.py:151
  88.7 10.1 %collective-permute-start.1 = (f32[160,640]{1,0:T(8,128)S(1)}, f32[160,640]{1,0:T(8,128)S(1)}, u32[]{:S(2)}, u32[]{:S(2)}) collective-permute-start(f32[160,640]{1,0:T(8,128)S(1)} %get-tuple-element.23), channel_id=1, source_target_pairs={{0,8},{8,0},{16,24},{24,16},{32,40},{40,32},{48,56},{56,48},{64,72... | collective-permute-start | bytes 1228808 | tf_op jit(solution)/shard_map/grad_rows/ppermute | solution.py:190
  95.2 1.6 %copy-start = (bf16[288,1536]{1,0:T(8,128)(2,1)S(1)}, bf16[288,1536]{1,0:T(8,128)(2,1)}, u32[]{:S(2)}) copy-start(bf16[288,1536]{1,0:T(8,128)(2,1)} %reshape.168) | copy-start | bytes 2654212
  99.4 8.9 %copy-start.1 = (bf16[1024,640]{1,0:T(8,128)(2,1)S(1)}, bf16[1024,640]{1,0:T(8,128)(2,1)}, u32[]{:S(2)}) copy-start(bf16[1024,640]{1,0:T(8,128)(2,1)} %multiply_convert_fusion) | copy-start | bytes 3932164
  100.6 19.6 %all-to-all-start.3 = ((bf16[32,30,128]{2,1,0:T(8,128)(2,1)}), bf16[32,30,128]{2,1,0:T(8,128)(2,1)S(1)}, u32[]{:S(2)}, u32[]{:S(2)}) async-start(bf16[32,30,128]{2,1,0:T(8,128)(2,1)} %copy.34), calls=%async_computation.3 | async-start | bytes 524288 | tf_op jit(solution)/shard_map/grad_rows/all_to_all | solution.py:18

commit v9 on v8

--- a/solution.py
+++ b/solution.py
@@ -188,6 +188,8 @@
         )
         own, send, gathered = lax.optimization_barrier((own, send, gathered))
         grad_rows = own + lax.ppermute(send, "dp", [(i, i ^ 1) for i in range(members)])
+        all_hidden = gathered.reshape(padded // LANES, 2, 3, rows // 2, LANES)
+        all_hidden = all_hidden.transpose(1, 3, 2, 0, 4).reshape(rows, 3 * padded)
         grad_rows = grad_rows.astype(BF16)
         outer = grad_rows[: 2 * members].reshape(chips, 2, 2, features)
         middle = jnp.einsum(
@@ -197,14 +199,13 @@
             preferred_element_type=F32,
         ).astype(BF16)
         slots = jnp.stack([outer[:, 0], middle, outer[:, 1]], axis=1).reshape(chips, 6, features)
-        arrived = exchange(dense(slots), "dp", CORE_GROUPS)
+        message, all_hidden, kept = lax.optimization_barrier((dense(slots), all_hidden, kept))
+        arrived = exchange(message, "dp", CORE_GROUPS)
         grad_inputs = jnp.sum(arrived.astype(F32), axis=0, keepdims=True).astype(BF16)
         grad_inputs = undense(grad_inputs, 6)[0]
 
     contract_rows = (((0,), (0,)), ((), ()))
     with jax.named_scope("grad_weights"):
-        all_hidden = gathered.reshape(padded // LANES, 2, 3, rows // 2, LANES)
-        all_hidden = all_hidden.transpose(1, 3, 2, 0, 4).reshape(rows, 3 * padded)
         in_total = lax.dot_general(
             all_hidden[:, : 2 * padded],
             kept[:, :features],

time: 123 us -> 120 us (0.976)
  the two profiles are of different devices: /device:TPU:1 before, /device:TPU:8 now
where the time goes in v9:
time: 120 us
  waiting for transfers between devices  40.1 us (33%)
  blocking collectives  35.3 us (29%)
  starting transfers between devices  25.9 us (22%)
  local copies, waits for them, and re-layouts  6.4 us (5%)
  other arithmetic  6.32 us (5%)
  matrix products  2.29 us (2%)
  between operations  1.69 us (1%)
  Pallas kernels  1.59 us (1%)
    all_to_all x2, waiting for transfers between devices, exchange(): return lax.all_to_all(x, axis, 0, 0, tiled=True, axis_index_groups=groups)  36.9 us
    all_to_all x2, blocking collectives, exchange(): return lax.all_to_all(x, axis, 0, 0, tiled=True, axis_index_groups=groups)  35.3 us
    all_to_all x2, starting transfers between devices, exchange(): return lax.all_to_all(x, axis, 0, 0, tiled=True, axis_index_groups=groups)  22.1 us
  transfers between devices with their start and end apart: 4, of which 4 were waited for; matrix products, arithmetic and copies ran while one was open for 7% of the time, Pallas kernels for 0%

profile of v9, /device:TPU:8, one launch (start us, length us, event | category | flops | bytes accessed | tf_op | source)
XLA Modules:
  0.0 119.6 jit_solution(5456371185056483621)
XLA Ops:
  0.7 0.8 pad_maximum_fusion.2
  1.6 1.1 broadcast_in_dim.60
  2.6 16.2 %all-to-all-start = ((bf16[32,120,128]{2,1,0:T(8,128)(2,1)}), bf16[32,120,128]{2,1,0:T(8,128)(2,1)S(1)}, u32[]{:S(2)}, u32[]{:S(2)}) async-start(bf16[32,120,128]{2,1,0:T(8,128)(2,1)} %broadcast_in_dim.60), calls=%async_computation | async-start | bytes 1966080 | tf_op jit(solution)/shard_map/gather_chips/all_to_all | solution.py:18
  19.2 0.6 compare_select_fusion
  21.0 0.2 fusion.19
  21.2 0.7 fusion.11
  21.9 1.4 %fusion.5.weights_ref = bf16[1536,640]{1,0:T(8,128)(2,1)S(1)} fusion(bf16[432,640]{1,0:T(8,128)(2,1)S(1)} %copy-done, bf16[432,640]{1,0:T(8,128)(2,1)} %bitcast.48, bf16[432,640]{1,0:T(8,128)(2,1)} %bitcast.49), kind=kLoop, calls=%fused_computation.11 | loop fusion | flops 13762560 | bytes 3624960 | tf_op jit(solution)/shard_map/concatenate | solution.py:139
  23.3 25.3 %all-to-all-done = bf16[32,120,128]{2,1,0:T(8,128)(2,1)S(1)} async-done(((bf16[32,120,128]{2,1,0:T(8,128)(2,1)}), bf16[32,120,128]{2,1,0:T(8,128)(2,1)S(1)}, u32[]{:S(2)}, u32[]{:S(2)}) %all-to-all-start) | async-done | bytes 983072 | tf_op jit(solution)/shard_map/gather_chips/all_to_all | solution.py:18
  48.7 0.2 copy.28
  48.8 0.7 copy.29
  49.6 0.6 convolution_convert_fusion.mine_ref
  50.1 1.9 %collective-permute-start = (bf16[288,1280]{1,0:T(8,128)(2,1)S(1)}, bf16[288,1280]{1,0:T(8,128)(2,1)S(1)}, u32[]{:S(2)}, u32[]{:S(2)}) collective-permute-start(bf16[288,1280]{1,0:T(8,128)(2,1)S(1)} %convolution_convert_fusion.mine_ref), channel_id=1, source_target_pairs={{0,8},{8,0},{16,24},{24,16},{32,40},{40,32},{48,56},{56,48},{64,72... | collective-permute-start | bytes 2211848 | tf_op jit(solution)/shard_map/gather_core/ppermute | solution.py:151
  52.1 2.2 %collective-permute-done.other_ref = bf16[288,1280]{1,0:T(8,128)(2,1)S(1)} collective-permute-done((bf16[288,1280]{1,0:T(8,128)(2,1)S(1)}, bf16[288,1280]{1,0:T(8,128)(2,1)S(1)}, u32[]{:S(2)}, u32[]{:S(2)}) %collective-permute-start) | collective-permute-done | bytes 737312 | tf_op jit(solution)/shard_map/gather_core/ppermute | solution.py:151
  54.2 0.9 partial_sums.1
  55.1 19.2 %all_to_all.20 = bf16[8,432,128]{2,1,0:T(8,128)(2,1)S(1)} all-to-all(bf16[8,432,128]{2,1,0:T(8,128)(2,1)S(1)} %get-tuple-element.22), channel_id=1, replica_groups=mesh['dp'=64,'fsdp'=8] {'fsdp'}, dimensions={0} | all-to-all | bytes 1769472 | tf_op jit(solution)/shard_map/sum_features/all_to_all | solution.py:18
  74.7 16.1 %all_to_all.21.gathered_ref = bf16[8,432,128]{2,1,0:T(8,128)(2,1)S(1)} all-to-all(bf16[8,432,128]{2,1,0:T(8,128)(2,1)S(1)} %broadcast_in_dim.67), channel_id=1, replica_groups=mesh['dp'=64,'fsdp'=8] {'fsdp'}, dimensions={0} | all-to-all | bytes 1769472 | tf_op jit(solution)/shard_map/gather_hidden/all_to_all | solution.py:18
  90.8 0.7 grad_rows.1
  91.5 1.9 %collective-permute-start.1 = (f32[160,640]{1,0:T(8,128)S(1)}, f32[160,640]{1,0:T(8,128)}, u32[]{:S(2)}, u32[]{:S(2)}) collective-permute-start(f32[160,640]{1,0:T(8,128)S(1)} %get-tuple-element.26), channel_id=1, source_target_pairs={{0,8},{8,0},{16,24},{24,16},{32,40},{40,32},{48,56},{56,48},{64,72... | collective-permute-start | bytes 1228808 | tf_op jit(solution)/shard_map/grad_rows/ppermute | solution.py:190
  93.4 0.5 copy.46
  93.9 0.3 reshape.167
  94.2 1.0 collective-permute-done.1
  95.2 1.0 add_convert_fusion
  96.6 0.2 fusion.6
  96.8 0.3 reshape.164
  97.2 0.8 copy.35
  98.0 5.9 %all-to-all-start.3 = ((bf16[32,30,128]{2,1,0:T(8,128)(2,1)}), bf16[32,30,128]{2,1,0:T(8,128)(2,1)S(1)}, u32[]{:S(2)}, u32[]{:S(2)}) async-start(bf16[32,30,128]{2,1,0:T(8,128)(2,1)} %copy.35), calls=%async_computation.3 | async-start | bytes 524288 | tf_op jit(solution)/shard_map/grad_rows/all_to_all | solution.py:18
  103.9 0.6 fusion.12
  104.5 1.0 multiply_convert_fusion
  105.4 0.9 fusion.7
  106.3 1.1 slice_bitcast_fusion
  107.4 11.6 %all-to-all-done.3 = bf16[32,30,128]{2,1,0:T(8,128)(2,1)S(1)} async-done(((bf16[32,30,128]{2,1,0:T(8,128)(2,1)}), bf16[32,30,128]{2,1,0:T(8,128)(2,1)S(1)}, u32[]{:S(2)}, u32[]{:S(2)}) %all-to-all-start.3) | async-done | bytes 245792 | tf_op jit(solution)/shard_map/grad_rows/all_to_all | solution.py:18
  119.0 0.6 convert_element_type.70
  (41 shorter events, 1.5 us)
Async XLA Ops:
  0.6 18.2 %copy-start.3 = (s32[64]{0:T(128)S(1)}, s32[64]{0:T(128)}, u32[]{:S(2)}) copy-start(s32[64]{0:T(128)} %param.12) | copy-start | bytes 772
  0.6 18.2 %copy-start.2 = (s32[64,3]{0,1:T(4,128)S(1)}, s32[64,3]{0,1:T(4,128)}, u32[]{:S(2)}) copy-start(s32[64,3]{0,1:T(4,128)} %param.13) | copy-start | bytes 2308
  0.7 21.3 %copy-start = (bf16[432,640]{1,0:T(8,128)(2,1)S(1)}, bf16[432,640]{1,0:T(8,128)(2,1)}, u32[]{:S(2)}) copy-start(bf16[432,640]{1,0:T(8,128)(2,1)} %param.11) | copy-start | bytes 1658884
  2.6 46.0 %all-to-all-start = ((bf16[32,120,128]{2,1,0:T(8,128)(2,1)}), bf16[32,120,128]{2,1,0:T(8,128)(2,1)S(1)}, u32[]{:S(2)}, u32[]{:S(2)}) async-start(bf16[32,120,128]{2,1,0:T(8,128)(2,1)} %broadcast_in_dim.60), calls=%async_computation | async-start | bytes 1966080 | tf_op jit(solution)/shard_map/gather_chips/all_to_all | solution.py:18
  23.3 26.2 %copy-start.1 = (bf16[288,384]{1,0:T(8,128)(2,1)S(1)}, bf16[288,384]{1,0:T(8,128)(2,1)}, u32[]{:S(2)}) copy-start(bf16[288,384]{1,0:T(8,128)(2,1)} %fusion.11) | copy-start | bytes 663556
  50.1 4.1 %collective-permute-start = (bf16[288,1280]{1,0:T(8,128)(2,1)S(1)}, bf16[288,1280]{1,0:T(8,128)(2,1)S(1)}, u32[]{:S(2)}, u32[]{:S(2)}) collective-permute-start(bf16[288,1280]{1,0:T(8,128)(2,1)S(1)} %convolution_convert_fusion.mine_ref), channel_id=1, source_target_pairs={{0,8},{8,0},{16,24},{24,16},{32,40},{40,32},{48,56},{56,48},{64,72... | collective-permute-start | bytes 2211848 | tf_op jit(solution)/shard_map/gather_core/ppermute | solution.py:151
  91.5 3.8 %collective-permute-start.1 = (f32[160,640]{1,0:T(8,128)S(1)}, f32[160,640]{1,0:T(8,128)}, u32[]{:S(2)}, u32[]{:S(2)}) collective-permute-start(f32[160,640]{1,0:T(8,128)S(1)} %get-tuple-element.26), channel_id=1, source_target_pairs={{0,8},{8,0},{16,24},{24,16},{32,40},{40,32},{48,56},{56,48},{64,72... | collective-permute-start | bytes 1228808 | tf_op jit(solution)/shard_map/grad_rows/ppermute | solution.py:190
  98.0 21.0 %all-to-all-start.3 = ((bf16[32,30,128]{2,1,0:T(8,128)(2,1)}), bf16[32,30,128]{2,1,0:T(8,128)(2,1)S(1)}, u32[]{:S(2)}, u32[]{:S(2)}) async-start(bf16[32,30,128]{2,1,0:T(8,128)(2,1)} %copy.35), calls=%async_computation.3 | async-start | bytes 524288 | tf_op jit(solution)/shard_map/grad_rows/all_to_all | solution.py:18

commit v10 on v9

--- a/solution.py
+++ b/solution.py
@@ -11,7 +11,25 @@
 CORES = 2
 BF16 = jnp.bfloat16
 F32 = jnp.float32
+Y_CHIPS = 8
+Z_CHIPS = 4
 CORE_GROUPS = [[chip * CORES + core for chip in range(32)] for core in range(CORES)]
+
+
+def dp_index(z, y, core):
+    return (z * Y_CHIPS + y) * CORES + core
+
+
+Z_GROUPS = [
+    [dp_index(z, y, core) for z in range(Z_CHIPS)]
+    for y in range(Y_CHIPS)
+    for core in range(CORES)
+]
+Y_GROUPS = [
+    [dp_index(z, y, core) for y in range(Y_CHIPS)]
+    for z in range(Z_CHIPS)
+    for core in range(CORES)
+]
 
 
 def exchange(x, axis, groups=None):
@@ -129,7 +147,7 @@
         ),
     )
     place = jnp.where(row < lengths[:, None], place, -1)
-    place = place.reshape(-1, CORES, capacity).transpose(1, 0, 2)
+    place = place.reshape(Z_CHIPS, Y_CHIPS, CORES, capacity).transpose(2, 1, 0, 3)
     place = jnp.where(core == 0, place[0], place[1]).reshape(-1)
     pick = (jnp.arange(rows, dtype=jnp.int32)[:, None] == place[None, :]).astype(BF16)
     full = jnp.where(is_full, full_rank, -1).reshape(-1, CORES)
@@ -141,11 +159,14 @@
 
     with jax.named_scope("gather_chips"):
         both = jnp.concatenate([inputs, upstream], axis=1)[None]
-        got = exchange(copies(dense(both)[0], members // CORES), "dp", CORE_GROUPS)
+        got = exchange(copies(dense(both)[0], Z_CHIPS), "dp", Z_GROUPS)
+        got = undense(got, capacity).reshape(1, Z_CHIPS * capacity, 2 * features)
+        got = dense(got)[0]
         got, pick, weights, spread, grad_scale = lax.optimization_barrier(
             (got, pick, weights, spread, grad_scale)
         )
-        got = undense(got, capacity).reshape(-1, 2 * features)
+        got = exchange(copies(got, Y_CHIPS), "dp", Y_GROUPS)
+        got = undense(got, Z_CHIPS * capacity).reshape(-1, 2 * features)
     with jax.named_scope("gather_core"):
         mine = jnp.dot(pick, got, preferred_element_type=F32).astype(BF16)
         other = lax.ppermute(mine, "dp", [(i, i ^ 1) for i in range(members)])

time: 120 us -> 126 us (1.050)
  blocking collectives: 35.3 us -> 66.6 us
  waiting for transfers between devices: 40.1 us -> 17.3 us
  starting transfers between devices: 25.9 us -> 21.8 us
  other arithmetic: 6.32 us -> 8.36 us
    all_to_all x2 -> x3, blocking collectives: 35.3 us -> 66.6 us  [exchange(): return lax.all_to_all(x, axis, 0, 0, tiled=True, axis_index_groups=groups)]
    all_to_all x2, waiting for transfers between devices: 36.9 us -> 14.1 us  [exchange(): return lax.all_to_all(x, axis, 0, 0, tiled=True, axis_index_groups=groups)]
    all_to_all x2, starting transfers between devices: 22.1 us -> 18 us  [exchange(): return lax.all_to_all(x, axis, 0, 0, tiled=True, axis_index_groups=groups)]
  transfers between devices with their start and end apart: 4 -> 4, of which waited for: 4 -> 4; matrix products, arithmetic and copies ran while one was open for 7% -> 8% of each run, Pallas kernels for 0% -> 0%
where the time goes in v10:
time: 126 us; the launch traced here: 125 us
  blocking collectives  66.6 us (53%)
  starting transfers between devices  21.8 us (17%)
  waiting for transfers between devices  17.3 us (14%)
  other arithmetic  8.36 us (7%)
  local copies, waits for them, and re-layouts  5.7 us (5%)
  matrix products  2.29 us (2%)
  between operations  1.62 us (1%)
  Pallas kernels  1.58 us (1%)
    all_to_all x3, blocking collectives, exchange(): return lax.all_to_all(x, axis, 0, 0, tiled=True, axis_index_groups=groups)  66.6 us
    all_to_all x2, starting transfers between devices, exchange(): return lax.all_to_all(x, axis, 0, 0, tiled=True, axis_index_groups=groups)  18 us
    all_to_all x2, waiting for transfers between devices, exchange(): return lax.all_to_all(x, axis, 0, 0, tiled=True, axis_index_groups=groups)  14.1 us
  transfers between devices with their start and end apart: 4, of which 4 were waited for; matrix products, arithmetic and copies ran while one was open for 8% of the time, Pallas kernels for 0%

profile of v10, /device:TPU:8, one launch (start us, length us, event | category | flops | bytes accessed | tf_op | source)
XLA Modules:
  0.0 125.3 jit_solution(8559833796500700555)
XLA Ops:
  0.6 0.8 pad_maximum_fusion.2
  1.5 0.7 broadcast_in_dim.66
  2.1 10.3 %all-to-all-start = ((bf16[4,120,128]{2,1,0:T(8,128)(2,1)}), bf16[4,120,128]{2,1,0:T(8,128)(2,1)S(1)}, u32[]{:S(2)}, u32[]{:S(2)}) async-start(bf16[4,120,128]{2,1,0:T(8,128)(2,1)} %broadcast_in_dim.66), calls=%async_computation | async-start | bytes 245760 | tf_op jit(solution)/shard_map/gather_chips/all_to_all | solution.py:36
  12.5 0.7 fusion.25
  13.1 0.7 add_multiply_fusion
  14.1 1.3 %compare_select_fusion = (s32[64]{0:T(128)S(1)}, s32[64]{0:T(128)S(1)}, s32[]{:T(128)}, s32[64]{0:T(128)S(1)}) fusion(s32[64]{0:T(128)} %param.12, s32[64]{0:T(128)S(1)} %reduce.2), kind=kLoop, calls=%fused_computation.49 | loop fusion | flops 767 | bytes 1284 | tf_op jit(solution)/shard_map/jit(_where)/select_n | solution.py:153
  16.2 0.7 select_select_fusion
  17.5 1.5 %fusion.5.weights_ref = bf16[1536,640]{1,0:T(8,128)(2,1)S(1)} fusion(bf16[432,640]{1,0:T(8,128)(2,1)} %param.11, bf16[432,640]{1,0:T(8,128)(2,1)} %bitcast.56, bf16[432,640]{1,0:T(8,128)(2,1)} %bitcast.57), kind=kLoop, calls=%fused_computation.11 | loop fusion | flops 13762560 | bytes 3624960 | tf_op jit(solution)/shard_map/concatenate | solution.py:157
  19.0 2.5 %all-to-all-done = bf16[4,120,128]{2,1,0:T(8,128)(2,1)S(1)} async-done(((bf16[4,120,128]{2,1,0:T(8,128)(2,1)}), bf16[4,120,128]{2,1,0:T(8,128)(2,1)S(1)}, u32[]{:S(2)}, u32[]{:S(2)}) %all-to-all-start) | async-done | bytes 122912 | tf_op jit(solution)/shard_map/gather_chips/all_to_all | solution.py:36
  21.8 31.3 %all_to_all.25 = bf16[8,480,128]{2,1,0:T(8,128)(2,1)S(1)} all-to-all(bf16[8,480,128]{2,1,0:T(8,128)(2,1)S(1)} %broadcast_in_dim.73), channel_id=1, replica_groups={{0,16,32,48,64,80,96,112},{8,24,40,56,72,88,104,120},{128,144,160,176,1..., dimensions={0} | all-to-all | bytes 1966080 | tf_op jit(solution)/shard_map/gather_chips/all_to_all | solution.py:36
  53.1 0.4 copy.42
  53.5 0.6 convolution_convert_fusion.mine_ref
  54.1 1.9 %collective-permute-start = (bf16[288,1280]{1,0:T(8,128)(2,1)S(1)}, bf16[288,1280]{1,0:T(8,128)(2,1)S(1)}, u32[]{:S(2)}, u32[]{:S(2)}) collective-permute-start(bf16[288,1280]{1,0:T(8,128)(2,1)S(1)} %convolution_convert_fusion.mine_ref), channel_id=1, source_target_pairs={{0,8},{8,0},{16,24},{24,16},{32,40},{40,32},{48,56},{56,48},{64,72... | collective-permute-start | bytes 2211848 | tf_op jit(solution)/shard_map/gather_core/ppermute | solution.py:172
  56.0 2.2 %collective-permute-done.other_ref = bf16[288,1280]{1,0:T(8,128)(2,1)S(1)} collective-permute-done((bf16[288,1280]{1,0:T(8,128)(2,1)S(1)}, bf16[288,1280]{1,0:T(8,128)(2,1)S(1)}, u32[]{:S(2)}, u32[]{:S(2)}) %collective-permute-start) | collective-permute-done | bytes 737312 | tf_op jit(solution)/shard_map/gather_core/ppermute | solution.py:172
  58.2 0.9 partial_sums.1
  59.1 19.3 %all_to_all.26 = bf16[8,432,128]{2,1,0:T(8,128)(2,1)S(1)} all-to-all(bf16[8,432,128]{2,1,0:T(8,128)(2,1)S(1)} %get-tuple-element.22), channel_id=1, replica_groups=mesh['dp'=64,'fsdp'=8] {'fsdp'}, dimensions={0} | all-to-all | bytes 1769472 | tf_op jit(solution)/shard_map/sum_features/all_to_all | solution.py:36
  78.6 16.1 %all_to_all.27.gathered_ref = bf16[8,432,128]{2,1,0:T(8,128)(2,1)S(1)} all-to-all(bf16[8,432,128]{2,1,0:T(8,128)(2,1)S(1)} %broadcast_in_dim.74), channel_id=1, replica_groups=mesh['dp'=64,'fsdp'=8] {'fsdp'}, dimensions={0} | all-to-all | bytes 1769472 | tf_op jit(solution)/shard_map/gather_hidden/all_to_all | solution.py:36
  94.7 0.7 grad_rows.1
  95.4 1.9 %collective-permute-start.1 = (f32[160,640]{1,0:T(8,128)S(1)}, f32[160,640]{1,0:T(8,128)}, u32[]{:S(2)}, u32[]{:S(2)}) collective-permute-start(f32[160,640]{1,0:T(8,128)S(1)} %get-tuple-element.26), channel_id=1, source_target_pairs={{0,8},{8,0},{16,24},{24,16},{32,40},{40,32},{48,56},{56,48},{64,72... | collective-permute-start | bytes 1228808 | tf_op jit(solution)/shard_map/grad_rows/ppermute | solution.py:211
  97.3 0.5 copy.59
  97.8 0.3 reshape.180
  98.1 1.0 collective-permute-done.1
  99.2 1.0 add_convert_fusion
  100.8 0.3 reshape.177
  101.1 0.8 copy.48
  101.9 7.7 %all-to-all-start.4 = ((bf16[32,30,128]{2,1,0:T(8,128)(2,1)}), bf16[32,30,128]{2,1,0:T(8,128)(2,1)S(1)}, u32[]{:S(2)}, u32[]{:S(2)}) async-start(bf16[32,30,128]{2,1,0:T(8,128)(2,1)} %copy.48), calls=%async_computation.4 | async-start | bytes 524288 | tf_op jit(solution)/shard_map/grad_rows/all_to_all | solution.py:36
  109.6 0.6 fusion.12
  110.2 1.0 multiply_convert_fusion
  111.1 0.9 fusion.7
  112.0 1.1 slice_bitcast_fusion
  113.1 11.6 %all-to-all-done.4 = bf16[32,30,128]{2,1,0:T(8,128)(2,1)S(1)} async-done(((bf16[32,30,128]{2,1,0:T(8,128)(2,1)}), bf16[32,30,128]{2,1,0:T(8,128)(2,1)S(1)}, u32[]{:S(2)}, u32[]{:S(2)}) %all-to-all-start.4) | async-done | bytes 245792 | tf_op jit(solution)/shard_map/grad_rows/all_to_all | solution.py:36
  124.7 0.6 convert_element_type.70
  (38 shorter events, 2.1 us)
Async XLA Ops:
  2.1 19.4 %all-to-all-start = ((bf16[4,120,128]{2,1,0:T(8,128)(2,1)}), bf16[4,120,128]{2,1,0:T(8,128)(2,1)S(1)}, u32[]{:S(2)}, u32[]{:S(2)}) async-start(bf16[4,120,128]{2,1,0:T(8,128)(2,1)} %broadcast_in_dim.66), calls=%async_computation | async-start | bytes 245760 | tf_op jit(solution)/shard_map/gather_chips/all_to_all | solution.py:36
  54.1 4.1 %collective-permute-start = (bf16[288,1280]{1,0:T(8,128)(2,1)S(1)}, bf16[288,1280]{1,0:T(8,128)(2,1)S(1)}, u32[]{:S(2)}, u32[]{:S(2)}) collective-permute-start(bf16[288,1280]{1,0:T(8,128)(2,1)S(1)} %convolution_convert_fusion.mine_ref), channel_id=1, source_target_pairs={{0,8},{8,0},{16,24},{24,16},{32,40},{40,32},{48,56},{56,48},{64,72... | collective-permute-start | bytes 2211848 | tf_op jit(solution)/shard_map/gather_core/ppermute | solution.py:172
  95.4 3.8 %collective-permute-start.1 = (f32[160,640]{1,0:T(8,128)S(1)}, f32[160,640]{1,0:T(8,128)}, u32[]{:S(2)}, u32[]{:S(2)}) collective-permute-start(f32[160,640]{1,0:T(8,128)S(1)} %get-tuple-element.26), channel_id=1, source_target_pairs={{0,8},{8,0},{16,24},{24,16},{32,40},{40,32},{48,56},{56,48},{64,72... | collective-permute-start | bytes 1228808 | tf_op jit(solution)/shard_map/grad_rows/ppermute | solution.py:211
  101.9 22.7 %all-to-all-start.4 = ((bf16[32,30,128]{2,1,0:T(8,128)(2,1)}), bf16[32,30,128]{2,1,0:T(8,128)(2,1)S(1)}, u32[]{:S(2)}, u32[]{:S(2)}) async-start(bf16[32,30,128]{2,1,0:T(8,128)(2,1)} %copy.48), calls=%async_computation.4 | async-start | bytes 524288 | tf_op jit(solution)/shard_map/grad_rows/all_to_all | solution.py:36

commit v11 on v8

--- a/solution.py
+++ b/solution.py
@@ -187,22 +187,9 @@
             scratch=[pltpu.VMEM((rows, 2 * padded), BF16), pltpu.VMEM((rows, features), F32)],
         )
         own, send, gathered = lax.optimization_barrier((own, send, gathered))
-        grad_rows = own + lax.ppermute(send, "dp", [(i, i ^ 1) for i in range(members)])
-        grad_rows = grad_rows.astype(BF16)
-        outer = grad_rows[: 2 * members].reshape(chips, 2, 2, features)
-        middle = jnp.einsum(
-            "lh,htf->ltf",
-            spread,
-            grad_rows[2 * members :].reshape(heavy, 2, features),
-            preferred_element_type=F32,
-        ).astype(BF16)
-        slots = jnp.stack([outer[:, 0], middle, outer[:, 1]], axis=1).reshape(chips, 6, features)
-        arrived = exchange(dense(slots), "dp", CORE_GROUPS)
-        grad_inputs = jnp.sum(arrived.astype(F32), axis=0, keepdims=True).astype(BF16)
-        grad_inputs = undense(grad_inputs, 6)[0]
-
-    contract_rows = (((0,), (0,)), ((), ()))
+        received = lax.ppermute(send, "dp", [(i, i ^ 1) for i in range(members)])
     with jax.named_scope("grad_weights"):
+        contract_rows = (((0,), (0,)), ((), ()))
         all_hidden = gathered.reshape(padded // LANES, 2, 3, rows // 2, LANES)
         all_hidden = all_hidden.transpose(1, 3, 2, 0, 4).reshape(rows, 3 * padded)
         in_total = lax.dot_general(
@@ -219,12 +206,27 @@
             preferred_element_type=F32,
         )
         grad_down = (down_total * grad_scale).astype(BF16)
-    return (
-        grad_inputs,
-        grad_in[:hidden_units].T,
-        grad_in[padded : padded + hidden_units].T,
-        grad_down[:hidden_units],
-    )
+        grads = (
+            grad_in[:hidden_units].T,
+            grad_in[padded : padded + hidden_units].T,
+            grad_down[:hidden_units],
+        )
+        own, grads = lax.optimization_barrier((own, grads))
+    with jax.named_scope("grad_rows"):
+        grad_rows = (own + received).astype(BF16)
+        outer = grad_rows[: 2 * members].reshape(chips, 2, 2, features)
+        middle = jnp.einsum(
+            "lh,htf->ltf",
+            spread,
+            grad_rows[2 * members :].reshape(heavy, 2, features),
+            preferred_element_type=F32,
+        ).astype(BF16)
+        slots = jnp.stack([outer[:, 0], middle, outer[:, 1]], axis=1).reshape(chips, 6, features)
+        arrived = exchange(dense(slots), "dp", CORE_GROUPS)
+        grad_inputs = jnp.sum(arrived.astype(F32), axis=0, keepdims=True).astype(BF16)
+        grad_inputs = undense(grad_inputs, 6)[0]
+
+    return (grad_inputs, *grads)
 
 
 def solution(mesh):

time: 123 us -> 121 us (0.984)
  blocking collectives: 33.1 us -> 52.5 us
  waiting for transfers between devices: 33.4 us -> 22.6 us
  starting transfers between devices: 34 us -> 27.1 us
  matrix products: 4.4 us -> 2.29 us
  local copies, waits for them, and re-layouts: 7.36 us -> 5.71 us
    all_to_all x2 -> x3, blocking collectives: 33.1 us -> 52.5 us  [exchange(): return lax.all_to_all(x, axis, 0, 0, tiled=True, axis_index_groups=groups)]
    all_to_all x2 -> x1, waiting for transfers between devices: 31.6 us -> 20.8 us  [exchange(): return lax.all_to_all(x, axis, 0, 0, tiled=True, axis_index_groups=groups)]
    all_to_all x2 -> x1, starting transfers between devices: 23.4 us -> 16.5 us  [exchange(): return lax.all_to_all(x, axis, 0, 0, tiled=True, axis_index_groups=groups)]
  transfers between devices with their start and end apart: 4 -> 3, of which waited for: 3 -> 2; matrix products, arithmetic and copies ran while one was open for 9% -> 6% of each run, Pallas kernels for 0% -> 0%
where the time goes in v11:
time: 121 us; the launch traced here: 119 us
  blocking collectives  52.5 us (43%)
  starting transfers between devices  27.1 us (22%)
  waiting for transfers between devices  22.6 us (19%)
  local copies, waits for them, and re-layouts  5.71 us (5%)
  other arithmetic  5.32 us (4%)
  matrix products  2.29 us (2%)
  between operations  1.68 us (1%)
  Pallas kernels  1.58 us (1%)
    all_to_all x3, blocking collectives, exchange(): return lax.all_to_all(x, axis, 0, 0, tiled=True, axis_index_groups=groups)  52.5 us
    all_to_all x1, waiting for transfers between devices, exchange(): return lax.all_to_all(x, axis, 0, 0, tiled=True, axis_index_groups=groups)  20.8 us
    all_to_all x1, starting transfers between devices, exchange(): return lax.all_to_all(x, axis, 0, 0, tiled=True, axis_index_groups=groups)  16.5 us
    ppermute x1, starting transfers between devices, body(): other = lax.ppermute(mine, 'dp', [(i, i ^ 1) for i in range(members)])  5.88 us
    ppermute x1, starting transfers between devices, body(): received = lax.ppermute(send, 'dp', [(i, i ^ 1) for i in range(members)])  4.74 us
  transfers between devices with their start and end apart: 3, of which 2 were waited for; matrix products, arithmetic and copies ran while one was open for 6% of the time, Pallas kernels for 0%

profile of v11, /device:TPU:1, one launch (start us, length us, event | category | flops | bytes accessed | tf_op | source)
XLA Modules:
  0.0 118.9 jit_solution(4433489449921869368)
XLA Ops:
  0.7 0.8 pad_maximum_fusion.2
  1.6 1.1 broadcast_in_dim.60
  2.6 16.5 %all-to-all-start = ((bf16[32,120,128]{2,1,0:T(8,128)(2,1)}), bf16[32,120,128]{2,1,0:T(8,128)(2,1)S(1)}, u32[]{:S(2)}, u32[]{:S(2)}) async-start(bf16[32,120,128]{2,1,0:T(8,128)(2,1)} %broadcast_in_dim.60), calls=%async_computation | async-start | bytes 1966080 | tf_op jit(solution)/shard_map/gather_chips/all_to_all | solution.py:18
  19.4 0.1 reduce.2
  19.5 0.6 compare_select_fusion
  21.3 0.2 fusion.19
  21.5 0.7 fusion.11
  22.3 1.4 %fusion.5.weights_ref = bf16[1536,640]{1,0:T(8,128)(2,1)S(1)} fusion(bf16[432,640]{1,0:T(8,128)(2,1)S(1)} %copy-done, bf16[432,640]{1,0:T(8,128)(2,1)} %bitcast.48, bf16[432,640]{1,0:T(8,128)(2,1)} %bitcast.49), kind=kLoop, calls=%fused_computation.11 | loop fusion | flops 13762560 | bytes 3624960 | tf_op jit(solution)/shard_map/concatenate | solution.py:139
  23.7 20.8 %all-to-all-done = bf16[32,120,128]{2,1,0:T(8,128)(2,1)S(1)} async-done(((bf16[32,120,128]{2,1,0:T(8,128)(2,1)}), bf16[32,120,128]{2,1,0:T(8,128)(2,1)S(1)}, u32[]{:S(2)}, u32[]{:S(2)}) %all-to-all-start) | async-done | bytes 983072 | tf_op jit(solution)/shard_map/gather_chips/all_to_all | solution.py:18
  44.5 0.2 copy.28
  44.6 0.7 copy.29
  45.4 0.6 convolution_convert_fusion.mine_ref
  45.9 5.9 %collective-permute-start = (bf16[288,1280]{1,0:T(8,128)(2,1)S(1)}, bf16[288,1280]{1,0:T(8,128)(2,1)S(1)}, u32[]{:S(2)}, u32[]{:S(2)}) collective-permute-start(bf16[288,1280]{1,0:T(8,128)(2,1)S(1)} %convolution_convert_fusion.mine_ref), channel_id=1, source_target_pairs={{0,8},{8,0},{16,24},{24,16},{32,40},{40,32},{48,56},{56,48},{64,72... | collective-permute-start | bytes 2211848 | tf_op jit(solution)/shard_map/gather_core/ppermute | solution.py:151
  51.8 1.8 %collective-permute-done.other_ref = bf16[288,1280]{1,0:T(8,128)(2,1)S(1)} collective-permute-done((bf16[288,1280]{1,0:T(8,128)(2,1)S(1)}, bf16[288,1280]{1,0:T(8,128)(2,1)S(1)}, u32[]{:S(2)}, u32[]{:S(2)}) %collective-permute-start) | collective-permute-done | bytes 737312 | tf_op jit(solution)/shard_map/gather_core/ppermute | solution.py:151
  53.6 0.9 partial_sums.1
  54.5 18.1 %all_to_all.20 = bf16[8,432,128]{2,1,0:T(8,128)(2,1)S(1)} all-to-all(bf16[8,432,128]{2,1,0:T(8,128)(2,1)S(1)} %get-tuple-element.23), channel_id=1, replica_groups=mesh['dp'=64,'fsdp'=8] {'fsdp'}, dimensions={0} | all-to-all | bytes 1769472 | tf_op jit(solution)/shard_map/sum_features/all_to_all | solution.py:18
  72.7 0.1 convert_reduce_fusion
  72.9 0.1 broadcast_in_dim.67
  73.0 15.0 %all_to_all.21.gathered_ref = bf16[8,432,128]{2,1,0:T(8,128)(2,1)S(1)} all-to-all(bf16[8,432,128]{2,1,0:T(8,128)(2,1)S(1)} %broadcast_in_dim.67), channel_id=1, replica_groups=mesh['dp'=64,'fsdp'=8] {'fsdp'}, dimensions={0} | all-to-all | bytes 1769472 | tf_op jit(solution)/shard_map/gather_hidden/all_to_all | solution.py:18
  88.0 0.7 grad_rows.1
  88.7 0.5 copy.46
  89.2 0.3 reshape.163
  89.5 4.7 %collective-permute-start.1 = (f32[160,640]{1,0:T(8,128)S(1)}, f32[160,640]{1,0:T(8,128)S(1)}, u32[]{:S(2)}, u32[]{:S(2)}) collective-permute-start(f32[160,640]{1,0:T(8,128)S(1)} %get-tuple-element.31), channel_id=1, source_target_pairs={{0,8},{8,0},{16,24},{24,16},{32,40},{40,32},{48,56},{56,48},{64,72... | collective-permute-start | bytes 1228808 | tf_op jit(solution)/shard_map/grad_rows/ppermute | solution.py:190
  94.3 0.6 fusion.12
  94.8 1.0 multiply_convert_fusion
  95.8 0.9 fusion.7
  96.7 1.1 slice_bitcast_fusion
  98.0 0.1 fusion.27
  98.1 0.2 fusion.6
  98.4 0.3 reshape.166
  98.8 19.4 %all_to_all.22 = bf16[32,30,128]{2,1,0:T(8,128)(2,1)S(1)} all-to-all(bf16[32,30,128]{2,1,0:T(8,128)(2,1)S(1)} %copy.35), channel_id=1, replica_groups={{0,16,32,48,64,80,96,112,128,144,160,176,192,208,224,240,256,272,288,30..., dimensions={0} | all-to-all | bytes 491520 | tf_op jit(solution)/shard_map/grad_rows/all_to_all | solution.py:18
  118.3 0.6 convert_element_type.72
  (40 shorter events, 1.2 us)
Async XLA Ops:
  0.6 18.5 %copy-start.3 = (s32[64]{0:T(128)S(1)}, s32[64]{0:T(128)}, u32[]{:S(2)}) copy-start(s32[64]{0:T(128)} %param.12) | copy-start | bytes 772
  0.6 18.5 %copy-start.2 = (s32[64,3]{0,1:T(4,128)S(1)}, s32[64,3]{0,1:T(4,128)}, u32[]{:S(2)}) copy-start(s32[64,3]{0,1:T(4,128)} %param.13) | copy-start | bytes 2308
  0.7 21.6 %copy-start = (bf16[432,640]{1,0:T(8,128)(2,1)S(1)}, bf16[432,640]{1,0:T(8,128)(2,1)}, u32[]{:S(2)}) copy-start(bf16[432,640]{1,0:T(8,128)(2,1)} %param.11) | copy-start | bytes 1658884
  2.6 41.8 %all-to-all-start = ((bf16[32,120,128]{2,1,0:T(8,128)(2,1)}), bf16[32,120,128]{2,1,0:T(8,128)(2,1)S(1)}, u32[]{:S(2)}, u32[]{:S(2)}) async-start(bf16[32,120,128]{2,1,0:T(8,128)(2,1)} %broadcast_in_dim.60), calls=%async_computation | async-start | bytes 1966080 | tf_op jit(solution)/shard_map/gather_chips/all_to_all | solution.py:18
  23.7 21.7 %copy-start.1 = (bf16[288,384]{1,0:T(8,128)(2,1)S(1)}, bf16[288,384]{1,0:T(8,128)(2,1)}, u32[]{:S(2)}) copy-start(bf16[288,384]{1,0:T(8,128)(2,1)} %fusion.11) | copy-start | bytes 663556
  45.9 7.7 %collective-permute-start = (bf16[288,1280]{1,0:T(8,128)(2,1)S(1)}, bf16[288,1280]{1,0:T(8,128)(2,1)S(1)}, u32[]{:S(2)}, u32[]{:S(2)}) collective-permute-start(bf16[288,1280]{1,0:T(8,128)(2,1)S(1)} %convolution_convert_fusion.mine_ref), channel_id=1, source_target_pairs={{0,8},{8,0},{16,24},{24,16},{32,40},{40,32},{48,56},{56,48},{64,72... | collective-permute-start | bytes 2211848 | tf_op jit(solution)/shard_map/gather_core/ppermute | solution.py:151
  89.5 8.3 %collective-permute-start.1 = (f32[160,640]{1,0:T(8,128)S(1)}, f32[160,640]{1,0:T(8,128)S(1)}, u32[]{:S(2)}, u32[]{:S(2)}) collective-permute-start(f32[160,640]{1,0:T(8,128)S(1)} %get-tuple-element.31), channel_id=1, source_target_pairs={{0,8},{8,0},{16,24},{24,16},{32,40},{40,32},{48,56},{56,48},{64,72... | collective-permute-start | bytes 1228808 | tf_op jit(solution)/shard_map/grad_rows/ppermute | solution.py:190

commit v12 on v8

--- a/solution.py
+++ b/solution.py
@@ -186,7 +186,6 @@
             weights,
             scratch=[pltpu.VMEM((rows, 2 * padded), BF16), pltpu.VMEM((rows, features), F32)],
         )
-        own, send, gathered = lax.optimization_barrier((own, send, gathered))
         grad_rows = own + lax.ppermute(send, "dp", [(i, i ^ 1) for i in range(members)])
         grad_rows = grad_rows.astype(BF16)
         outer = grad_rows[: 2 * members].reshape(chips, 2, 2, features)
@@ -197,7 +196,8 @@
             preferred_element_type=F32,
         ).astype(BF16)
         slots = jnp.stack([outer[:, 0], middle, outer[:, 1]], axis=1).reshape(chips, 6, features)
-        arrived = exchange(dense(slots), "dp", CORE_GROUPS)
+        message, gathered, kept = lax.optimization_barrier((dense(slots), gathered, kept))
+        arrived = exchange(message, "dp", CORE_GROUPS)
         grad_inputs = jnp.sum(arrived.astype(F32), axis=0, keepdims=True).astype(BF16)
         grad_inputs = undense(grad_inputs, 6)[0]
 

time: 123 us -> 120 us (0.976)
  the two profiles are of different devices: /device:TPU:1 before, /device:TPU:8 now
where the time goes in v12:
time: 120 us; the launch traced here: 119 us
  waiting for transfers between devices  40.8 us (34%)
  blocking collectives  35.3 us (29%)
  starting transfers between devices  25.9 us (22%)
  local copies, waits for them, and re-layouts  6.41 us (5%)
  other arithmetic  5.32 us (4%)
  matrix products  2.29 us (2%)
  between operations  1.72 us (1%)
  Pallas kernels  1.63 us (1%)
    all_to_all x2, waiting for transfers between devices, exchange(): return lax.all_to_all(x, axis, 0, 0, tiled=True, axis_index_groups=groups)  36.9 us
    all_to_all x2, blocking collectives, exchange(): return lax.all_to_all(x, axis, 0, 0, tiled=True, axis_index_groups=groups)  35.3 us
    all_to_all x2, starting transfers between devices, exchange(): return lax.all_to_all(x, axis, 0, 0, tiled=True, axis_index_groups=groups)  22.1 us
  transfers between devices with their start and end apart: 4, of which 4 were waited for; matrix products, arithmetic and copies ran while one was open for 6% of the time, Pallas kernels for 0%

profile of v12, /device:TPU:8, one launch (start us, length us, event | category | flops | bytes accessed | tf_op | source)
XLA Modules:
  0.0 119.4 jit_solution(5757713504004637435)
XLA Ops:
  0.7 0.8 pad_maximum_fusion.2
  1.6 1.1 broadcast_in_dim.60
  2.6 16.2 %all-to-all-start = ((bf16[32,120,128]{2,1,0:T(8,128)(2,1)}), bf16[32,120,128]{2,1,0:T(8,128)(2,1)S(1)}, u32[]{:S(2)}, u32[]{:S(2)}) async-start(bf16[32,120,128]{2,1,0:T(8,128)(2,1)} %broadcast_in_dim.60), calls=%async_computation | async-start | bytes 1966080 | tf_op jit(solution)/shard_map/gather_chips/all_to_all | solution.py:18
  19.2 0.6 compare_select_fusion
  21.0 0.2 fusion.19
  21.2 0.7 fusion.11
  21.9 1.4 %fusion.5.weights_ref = bf16[1536,640]{1,0:T(8,128)(2,1)S(1)} fusion(bf16[432,640]{1,0:T(8,128)(2,1)S(1)} %copy-done.2, bf16[432,640]{1,0:T(8,128)(2,1)} %bitcast.48, bf16[432,640]{1,0:T(8,128)(2,1)} %bitcast.49), kind=kLoop, calls=%fused_computation.11 | loop fusion | flops 13762560 | bytes 3624960 | tf_op jit(solution)/shard_map/concatenate | solution.py:139
  23.3 25.3 %all-to-all-done = bf16[32,120,128]{2,1,0:T(8,128)(2,1)S(1)} async-done(((bf16[32,120,128]{2,1,0:T(8,128)(2,1)}), bf16[32,120,128]{2,1,0:T(8,128)(2,1)S(1)}, u32[]{:S(2)}, u32[]{:S(2)}) %all-to-all-start) | async-done | bytes 983072 | tf_op jit(solution)/shard_map/gather_chips/all_to_all | solution.py:18
  48.7 0.2 copy.28
  48.8 0.7 copy.29
  49.6 0.6 convolution_convert_fusion.mine_ref
  50.1 1.9 %collective-permute-start = (bf16[288,1280]{1,0:T(8,128)(2,1)S(1)}, bf16[288,1280]{1,0:T(8,128)(2,1)S(1)}, u32[]{:S(2)}, u32[]{:S(2)}) collective-permute-start(bf16[288,1280]{1,0:T(8,128)(2,1)S(1)} %convolution_convert_fusion.mine_ref), channel_id=1, source_target_pairs={{0,8},{8,0},{16,24},{24,16},{32,40},{40,32},{48,56},{56,48},{64,72... | collective-permute-start | bytes 2211848 | tf_op jit(solution)/shard_map/gather_core/ppermute | solution.py:151
  52.1 2.2 %collective-permute-done.other_ref = bf16[288,1280]{1,0:T(8,128)(2,1)S(1)} collective-permute-done((bf16[288,1280]{1,0:T(8,128)(2,1)S(1)}, bf16[288,1280]{1,0:T(8,128)(2,1)S(1)}, u32[]{:S(2)}, u32[]{:S(2)}) %collective-permute-start) | collective-permute-done | bytes 737312 | tf_op jit(solution)/shard_map/gather_core/ppermute | solution.py:151
  54.2 0.9 partial_sums.1
  55.2 19.2 %all_to_all.20 = bf16[8,432,128]{2,1,0:T(8,128)(2,1)S(1)} all-to-all(bf16[8,432,128]{2,1,0:T(8,128)(2,1)S(1)} %get-tuple-element.19), channel_id=1, replica_groups=mesh['dp'=64,'fsdp'=8] {'fsdp'}, dimensions={0} | all-to-all | bytes 1769472 | tf_op jit(solution)/shard_map/sum_features/all_to_all | solution.py:18
  74.4 0.1 convert_reduce_fusion
  74.8 16.1 %all_to_all.21.gathered_ref = bf16[8,432,128]{2,1,0:T(8,128)(2,1)S(1)} all-to-all(bf16[8,432,128]{2,1,0:T(8,128)(2,1)S(1)} %broadcast_in_dim.67), channel_id=1, replica_groups=mesh['dp'=64,'fsdp'=8] {'fsdp'}, dimensions={0} | all-to-all | bytes 1769472 | tf_op jit(solution)/shard_map/gather_hidden/all_to_all | solution.py:18
  90.8 0.7 grad_rows.1
  91.5 1.9 %collective-permute-start.1 = (f32[160,640]{1,0:T(8,128)S(1)}, f32[160,640]{1,0:T(8,128)S(1)}, u32[]{:S(2)}, u32[]{:S(2)}) collective-permute-start(f32[160,640]{1,0:T(8,128)S(1)} %get-tuple-element.21), channel_id=1, source_target_pairs={{0,8},{8,0},{16,24},{24,16},{32,40},{40,32},{48,56},{56,48},{64,72... | collective-permute-start | bytes 1228808 | tf_op jit(solution)/shard_map/grad_rows/ppermute | solution.py:189
  93.5 1.7 %collective-permute-done.1 = f32[160,640]{1,0:T(8,128)S(1)} collective-permute-done((f32[160,640]{1,0:T(8,128)S(1)}, f32[160,640]{1,0:T(8,128)S(1)}, u32[]{:S(2)}, u32[]{:S(2)}) %collective-permute-start.1) | collective-permute-done | bytes 409632 | tf_op jit(solution)/shard_map/grad_rows/ppermute | solution.py:189
  95.5 0.2 fusion.6
  95.8 0.3 reshape.164
  96.1 0.5 copy.46
  96.6 0.3 reshape.168
  96.9 0.8 copy.34
  97.7 5.9 %all-to-all-start.3 = ((bf16[32,30,128]{2,1,0:T(8,128)(2,1)}), bf16[32,30,128]{2,1,0:T(8,128)(2,1)S(1)}, u32[]{:S(2)}, u32[]{:S(2)}) async-start(bf16[32,30,128]{2,1,0:T(8,128)(2,1)} %copy.34), calls=%async_computation.3 | async-start | bytes 524288 | tf_op jit(solution)/shard_map/grad_rows/all_to_all | solution.py:18
  103.6 0.6 fusion.12
  104.2 1.0 multiply_convert_fusion
  105.2 0.9 fusion.7
  106.1 1.1 slice_bitcast_fusion
  107.2 11.5 %all-to-all-done.3 = bf16[32,30,128]{2,1,0:T(8,128)(2,1)S(1)} async-done(((bf16[32,30,128]{2,1,0:T(8,128)(2,1)}), bf16[32,30,128]{2,1,0:T(8,128)(2,1)S(1)}, u32[]{:S(2)}, u32[]{:S(2)}) %all-to-all-start.3) | async-done | bytes 245792 | tf_op jit(solution)/shard_map/grad_rows/all_to_all | solution.py:18
  118.8 0.6 convert_element_type.70
  (45 shorter events, 1.5 us)
Async XLA Ops:
  0.6 18.2 %copy-start.5 = (s32[64]{0:T(128)S(1)}, s32[64]{0:T(128)}, u32[]{:S(2)}) copy-start(s32[64]{0:T(128)} %param.12) | copy-start | bytes 772
  0.6 18.2 %copy-start.4 = (s32[64,3]{0,1:T(4,128)S(1)}, s32[64,3]{0,1:T(4,128)}, u32[]{:S(2)}) copy-start(s32[64,3]{0,1:T(4,128)} %param.13) | copy-start | bytes 2308
  0.7 21.3 %copy-start.2 = (bf16[432,640]{1,0:T(8,128)(2,1)S(1)}, bf16[432,640]{1,0:T(8,128)(2,1)}, u32[]{:S(2)}) copy-start(bf16[432,640]{1,0:T(8,128)(2,1)} %param.11) | copy-start | bytes 1658884
  2.6 46.0 %all-to-all-start = ((bf16[32,120,128]{2,1,0:T(8,128)(2,1)}), bf16[32,120,128]{2,1,0:T(8,128)(2,1)S(1)}, u32[]{:S(2)}, u32[]{:S(2)}) async-start(bf16[32,120,128]{2,1,0:T(8,128)(2,1)} %broadcast_in_dim.60), calls=%async_computation | async-start | bytes 1966080 | tf_op jit(solution)/shard_map/gather_chips/all_to_all | solution.py:18
  23.3 26.2 %copy-start.3 = (bf16[288,384]{1,0:T(8,128)(2,1)S(1)}, bf16[288,384]{1,0:T(8,128)(2,1)}, u32[]{:S(2)}) copy-start(bf16[288,384]{1,0:T(8,128)(2,1)} %fusion.11) | copy-start | bytes 663556
  50.1 4.1 %collective-permute-start = (bf16[288,1280]{1,0:T(8,128)(2,1)S(1)}, bf16[288,1280]{1,0:T(8,128)(2,1)S(1)}, u32[]{:S(2)}, u32[]{:S(2)}) collective-permute-start(bf16[288,1280]{1,0:T(8,128)(2,1)S(1)} %convolution_convert_fusion.mine_ref), channel_id=1, source_target_pairs={{0,8},{8,0},{16,24},{24,16},{32,40},{40,32},{48,56},{56,48},{64,72... | collective-permute-start | bytes 2211848 | tf_op jit(solution)/shard_map/gather_core/ppermute | solution.py:151
  55.2 19.6 %copy-start = (bf16[288,1280]{1,0:T(8,128)(2,1)}, bf16[288,1280]{1,0:T(8,128)(2,1)S(1)}, u32[]{:S(2)}) copy-start(bf16[288,1280]{1,0:T(8,128)(2,1)S(1)} %get-tuple-element.26) | copy-start | bytes 2211844
  91.5 3.6 %collective-permute-start.1 = (f32[160,640]{1,0:T(8,128)S(1)}, f32[160,640]{1,0:T(8,128)S(1)}, u32[]{:S(2)}, u32[]{:S(2)}) collective-permute-start(f32[160,640]{1,0:T(8,128)S(1)} %get-tuple-element.21), channel_id=1, source_target_pairs={{0,8},{8,0},{16,24},{24,16},{32,40},{40,32},{48,56},{56,48},{64,72... | collective-permute-start | bytes 1228808 | tf_op jit(solution)/shard_map/grad_rows/ppermute | solution.py:189
  96.1 7.5 %copy-start.1 = (bf16[288,1280]{1,0:T(8,128)(2,1)S(1)}, bf16[288,1280]{1,0:T(8,128)(2,1)}, u32[]{:S(2)}) copy-start(bf16[288,1280]{1,0:T(8,128)(2,1)} %copy-done) | copy-start | bytes 2211844
  97.7 21.0 %all-to-all-start.3 = ((bf16[32,30,128]{2,1,0:T(8,128)(2,1)}), bf16[32,30,128]{2,1,0:T(8,128)(2,1)S(1)}, u32[]{:S(2)}, u32[]{:S(2)}) async-start(bf16[32,30,128]{2,1,0:T(8,128)(2,1)} %copy.34), calls=%async_computation.3 | async-start | bytes 524288 | tf_op jit(solution)/shard_map/grad_rows/all_to_all | solution.py:18

commit v13 on v9

--- a/solution.py
+++ b/solution.py
@@ -82,7 +82,7 @@
     padded = shards // 2 * LANES
     for shard in range(shards):
         tile, part = divmod(shard, 2)
-        for which in range(2):
+        for which in range(3):
             at = which * padded + tile * LANES
             hidden_ref[part * half : (part + 1) * half, at : at + LANES] = gathered_ref[
                 shard, which * half : (which + 1) * half, :
@@ -91,7 +91,7 @@
     for at in range(0, features, 2 * LANES):
         to = min(at + 2 * LANES, features)
         all_ref[:, at:to] = jnp.dot(
-            hidden_ref[...],
+            hidden_ref[:, : 2 * padded],
             weights_ref[: 2 * padded, at:to],
             preferred_element_type=F32,
         )
@@ -177,19 +177,17 @@
         gathered = exchange(copies(shard, shards), "fsdp")
 
     with jax.named_scope("grad_rows"):
-        own, send = call(
+        own, send, all_hidden = call(
             functools.partial(rows_kernel, 2 * heavy),
-            [jax.ShapeDtypeStruct((2 * members + 2 * heavy, features), F32)] * 2,
+            [jax.ShapeDtypeStruct((2 * members + 2 * heavy, features), F32)] * 2
+            + [jax.ShapeDtypeStruct((rows, 3 * padded), BF16)],
             2 * rows * features * 2 * padded,
             core[None],
             gathered,
             weights,
-            scratch=[pltpu.VMEM((rows, 2 * padded), BF16), pltpu.VMEM((rows, features), F32)],
-        )
-        own, send, gathered = lax.optimization_barrier((own, send, gathered))
+            scratch=[pltpu.VMEM((rows, features), F32)],
+        )
         grad_rows = own + lax.ppermute(send, "dp", [(i, i ^ 1) for i in range(members)])
-        all_hidden = gathered.reshape(padded // LANES, 2, 3, rows // 2, LANES)
-        all_hidden = all_hidden.transpose(1, 3, 2, 0, 4).reshape(rows, 3 * padded)
         grad_rows = grad_rows.astype(BF16)
         outer = grad_rows[: 2 * members].reshape(chips, 2, 2, features)
         middle = jnp.einsum(

time: 120 us -> 119 us (level)
  transfers between devices with their start and end apart: 4 -> 4, of which waited for: 4 -> 4; matrix products, arithmetic and copies ran while one was open for 7% -> 6% of each run, Pallas kernels for 0% -> 0%
where the time goes in v13:
time: 119 us
  waiting for transfers between devices  40.8 us (34%)
  blocking collectives  35.3 us (30%)
  starting transfers between devices  25.9 us (22%)
  local copies, waits for them, and re-layouts  5.63 us (5%)
  other arithmetic  5.32 us (4%)
  matrix products  2.29 us (2%)
  between operations  1.7 us (1%)
  Pallas kernels  1.68 us (1%)
    all_to_all x2, waiting for transfers between devices, exchange(): return lax.all_to_all(x, axis, 0, 0, tiled=True, axis_index_groups=groups)  36.9 us
    all_to_all x2, blocking collectives, exchange(): return lax.all_to_all(x, axis, 0, 0, tiled=True, axis_index_groups=groups)  35.3 us
    all_to_all x2, starting transfers between devices, exchange(): return lax.all_to_all(x, axis, 0, 0, tiled=True, axis_index_groups=groups)  22.1 us
  transfers between devices with their start and end apart: 4, of which 4 were waited for; matrix products, arithmetic and copies ran while one was open for 6% of the time, Pallas kernels for 0%

profile of v13, /device:TPU:8, one launch (start us, length us, event | category | flops | bytes accessed | tf_op | source)
XLA Modules:
  0.0 118.6 jit_solution(6067854572738032438)
XLA Ops:
  0.7 0.8 pad_maximum_fusion.2
  1.6 1.1 broadcast_in_dim.60
  2.6 16.2 %all-to-all-start = ((bf16[32,120,128]{2,1,0:T(8,128)(2,1)}), bf16[32,120,128]{2,1,0:T(8,128)(2,1)S(1)}, u32[]{:S(2)}, u32[]{:S(2)}) async-start(bf16[32,120,128]{2,1,0:T(8,128)(2,1)} %broadcast_in_dim.60), calls=%async_computation | async-start | bytes 1966080 | tf_op jit(solution)/shard_map/gather_chips/all_to_all | solution.py:18
  19.2 0.6 compare_select_fusion
  21.0 0.2 fusion.19
  21.2 0.7 fusion.11
  21.9 1.4 %fusion.5.weights_ref = bf16[1536,640]{1,0:T(8,128)(2,1)S(1)} fusion(bf16[432,640]{1,0:T(8,128)(2,1)S(1)} %copy-done.2, bf16[432,640]{1,0:T(8,128)(2,1)} %bitcast.42, bf16[432,640]{1,0:T(8,128)(2,1)} %bitcast.43), kind=kLoop, calls=%fused_computation.11 | loop fusion | flops 13762560 | bytes 3624960 | tf_op jit(solution)/shard_map/concatenate | solution.py:139
  23.3 25.3 %all-to-all-done = bf16[32,120,128]{2,1,0:T(8,128)(2,1)S(1)} async-done(((bf16[32,120,128]{2,1,0:T(8,128)(2,1)}), bf16[32,120,128]{2,1,0:T(8,128)(2,1)S(1)}, u32[]{:S(2)}, u32[]{:S(2)}) %all-to-all-start) | async-done | bytes 983072 | tf_op jit(solution)/shard_map/gather_chips/all_to_all | solution.py:18
  48.7 0.2 copy.27
  48.8 0.7 copy.28
  49.6 0.6 convolution_convert_fusion.mine_ref
  50.1 1.9 %collective-permute-start = (bf16[288,1280]{1,0:T(8,128)(2,1)S(1)}, bf16[288,1280]{1,0:T(8,128)(2,1)S(1)}, u32[]{:S(2)}, u32[]{:S(2)}) collective-permute-start(bf16[288,1280]{1,0:T(8,128)(2,1)S(1)} %convolution_convert_fusion.mine_ref), channel_id=1, source_target_pairs={{0,8},{8,0},{16,24},{24,16},{32,40},{40,32},{48,56},{56,48},{64,72... | collective-permute-start | bytes 2211848 | tf_op jit(solution)/shard_map/gather_core/ppermute | solution.py:151
  52.1 2.2 %collective-permute-done.other_ref = bf16[288,1280]{1,0:T(8,128)(2,1)S(1)} collective-permute-done((bf16[288,1280]{1,0:T(8,128)(2,1)S(1)}, bf16[288,1280]{1,0:T(8,128)(2,1)S(1)}, u32[]{:S(2)}, u32[]{:S(2)}) %collective-permute-start) | collective-permute-done | bytes 737312 | tf_op jit(solution)/shard_map/gather_core/ppermute | solution.py:151
  54.2 0.9 partial_sums.1
  55.2 19.2 %all_to_all.20 = bf16[8,432,128]{2,1,0:T(8,128)(2,1)S(1)} all-to-all(bf16[8,432,128]{2,1,0:T(8,128)(2,1)S(1)} %get-tuple-element.20), channel_id=1, replica_groups=mesh['dp'=64,'fsdp'=8] {'fsdp'}, dimensions={0} | all-to-all | bytes 1769472 | tf_op jit(solution)/shard_map/sum_features/all_to_all | solution.py:18
  74.4 0.1 convert_reduce_fusion
  74.6 0.1 broadcast_in_dim.67
  74.7 16.1 %all_to_all.21.gathered_ref = bf16[8,432,128]{2,1,0:T(8,128)(2,1)S(1)} all-to-all(bf16[8,432,128]{2,1,0:T(8,128)(2,1)S(1)} %broadcast_in_dim.67), channel_id=1, replica_groups=mesh['dp'=64,'fsdp'=8] {'fsdp'}, dimensions={0} | all-to-all | bytes 1769472 | tf_op jit(solution)/shard_map/gather_hidden/all_to_all | solution.py:18
  90.8 0.8 grad_rows.1
  91.6 1.9 %collective-permute-start.1 = (f32[160,640]{1,0:T(8,128)S(1)}, f32[160,640]{1,0:T(8,128)S(1)}, u32[]{:S(2)}, u32[]{:S(2)}) collective-permute-start(f32[160,640]{1,0:T(8,128)S(1)} %get-tuple-element.22), channel_id=1, source_target_pairs={{0,8},{8,0},{16,24},{24,16},{32,40},{40,32},{48,56},{56,48},{64,72... | collective-permute-start | bytes 1228808 | tf_op jit(solution)/shard_map/grad_rows/ppermute | solution.py:190
  93.5 1.7 %collective-permute-done.1 = f32[160,640]{1,0:T(8,128)S(1)} collective-permute-done((f32[160,640]{1,0:T(8,128)S(1)}, f32[160,640]{1,0:T(8,128)S(1)}, u32[]{:S(2)}, u32[]{:S(2)}) %collective-permute-start.1) | collective-permute-done | bytes 409632 | tf_op jit(solution)/shard_map/grad_rows/ppermute | solution.py:190
  95.4 0.1 fusion.27
  95.6 0.2 fusion.6
  95.8 0.3 reshape.158
  96.2 0.8 copy.33
  97.0 5.9 %all-to-all-start.3 = ((bf16[32,30,128]{2,1,0:T(8,128)(2,1)}), bf16[32,30,128]{2,1,0:T(8,128)(2,1)S(1)}, u32[]{:S(2)}, u32[]{:S(2)}) async-start(bf16[32,30,128]{2,1,0:T(8,128)(2,1)} %copy.33), calls=%async_computation.3 | async-start | bytes 524288 | tf_op jit(solution)/shard_map/grad_rows/all_to_all | solution.py:18
  102.9 0.6 fusion.12
  103.5 1.0 multiply_convert_fusion
  104.5 0.9 fusion.7
  105.3 1.1 slice_bitcast_fusion
  106.4 11.5 %all-to-all-done.3 = bf16[32,30,128]{2,1,0:T(8,128)(2,1)S(1)} async-done(((bf16[32,30,128]{2,1,0:T(8,128)(2,1)}), bf16[32,30,128]{2,1,0:T(8,128)(2,1)S(1)}, u32[]{:S(2)}, u32[]{:S(2)}) %all-to-all-start.3) | async-done | bytes 245792 | tf_op jit(solution)/shard_map/grad_rows/all_to_all | solution.py:18
  118.0 0.6 convert_element_type.70
  (43 shorter events, 1.2 us)
Async XLA Ops:
  0.6 18.2 %copy-start.5 = (s32[64]{0:T(128)S(1)}, s32[64]{0:T(128)}, u32[]{:S(2)}) copy-start(s32[64]{0:T(128)} %param.12) | copy-start | bytes 772
  0.6 18.2 %copy-start.4 = (s32[64,3]{0,1:T(4,128)S(1)}, s32[64,3]{0,1:T(4,128)}, u32[]{:S(2)}) copy-start(s32[64,3]{0,1:T(4,128)} %param.13) | copy-start | bytes 2308
  0.7 21.3 %copy-start.2 = (bf16[432,640]{1,0:T(8,128)(2,1)S(1)}, bf16[432,640]{1,0:T(8,128)(2,1)}, u32[]{:S(2)}) copy-start(bf16[432,640]{1,0:T(8,128)(2,1)} %param.11) | copy-start | bytes 1658884
  2.6 46.0 %all-to-all-start = ((bf16[32,120,128]{2,1,0:T(8,128)(2,1)}), bf16[32,120,128]{2,1,0:T(8,128)(2,1)S(1)}, u32[]{:S(2)}, u32[]{:S(2)}) async-start(bf16[32,120,128]{2,1,0:T(8,128)(2,1)} %broadcast_in_dim.60), calls=%async_computation | async-start | bytes 1966080 | tf_op jit(solution)/shard_map/gather_chips/all_to_all | solution.py:18
  23.3 26.2 %copy-start.3 = (bf16[288,384]{1,0:T(8,128)(2,1)S(1)}, bf16[288,384]{1,0:T(8,128)(2,1)}, u32[]{:S(2)}) copy-start(bf16[288,384]{1,0:T(8,128)(2,1)} %fusion.11) | copy-start | bytes 663556
  50.1 4.1 %collective-permute-start = (bf16[288,1280]{1,0:T(8,128)(2,1)S(1)}, bf16[288,1280]{1,0:T(8,128)(2,1)S(1)}, u32[]{:S(2)}, u32[]{:S(2)}) collective-permute-start(bf16[288,1280]{1,0:T(8,128)(2,1)S(1)} %convolution_convert_fusion.mine_ref), channel_id=1, source_target_pairs={{0,8},{8,0},{16,24},{24,16},{32,40},{40,32},{48,56},{56,48},{64,72... | collective-permute-start | bytes 2211848 | tf_op jit(solution)/shard_map/gather_core/ppermute | solution.py:151
  91.6 3.7 %copy-start = (bf16[288,1536]{1,0:T(8,128)(2,1)}, bf16[288,1536]{1,0:T(8,128)(2,1)S(1)}, u32[]{:S(2)}) copy-start(bf16[288,1536]{1,0:T(8,128)(2,1)S(1)} %get-tuple-element.27) | copy-start | bytes 2654212
  91.6 3.6 %collective-permute-start.1 = (f32[160,640]{1,0:T(8,128)S(1)}, f32[160,640]{1,0:T(8,128)S(1)}, u32[]{:S(2)}, u32[]{:S(2)}) collective-permute-start(f32[160,640]{1,0:T(8,128)S(1)} %get-tuple-element.22), channel_id=1, source_target_pairs={{0,8},{8,0},{16,24},{24,16},{32,40},{40,32},{48,56},{56,48},{64,72... | collective-permute-start | bytes 1228808 | tf_op jit(solution)/shard_map/grad_rows/ppermute | solution.py:190
  95.3 7.6 %copy-start.1 = (bf16[288,1536]{1,0:T(8,128)(2,1)S(1)}, bf16[288,1536]{1,0:T(8,128)(2,1)}, u32[]{:S(2)}) copy-start(bf16[288,1536]{1,0:T(8,128)(2,1)} %copy-done) | copy-start | bytes 2654212
  97.0 21.0 %all-to-all-start.3 = ((bf16[32,30,128]{2,1,0:T(8,128)(2,1)}), bf16[32,30,128]{2,1,0:T(8,128)(2,1)S(1)}, u32[]{:S(2)}, u32[]{:S(2)}) async-start(bf16[32,30,128]{2,1,0:T(8,128)(2,1)} %copy.33), calls=%async_computation.3 | async-start | bytes 524288 | tf_op jit(solution)/shard_map/grad_rows/all_to_all | solution.py:18

commit v14 on v13

--- a/solution.py
+++ b/solution.py
@@ -130,8 +130,16 @@
     )
     place = jnp.where(row < lengths[:, None], place, -1)
     place = place.reshape(-1, CORES, capacity).transpose(1, 0, 2)
-    place = jnp.where(core == 0, place[0], place[1]).reshape(-1)
-    pick = (jnp.arange(rows, dtype=jnp.int32)[:, None] == place[None, :]).astype(BF16)
+    place = jnp.where(core == 0, place[0], place[1])
+    none = jnp.full_like(place[:, 8:], -1)
+    places = jnp.stack(
+        [
+            place[:, :8],
+            jnp.concatenate([place[:, 8:], none], axis=1),
+            jnp.concatenate([none, place[:, 8:]], axis=1),
+        ]
+    ).reshape(3, -1)
+    pick = (jnp.arange(rows, dtype=jnp.int32)[None, :, None] == places[:, None, :]).astype(BF16)
     full = jnp.where(is_full, full_rank, -1).reshape(-1, CORES)
     full = jnp.where(core == 0, full[:, 0], full[:, 1])
     spread = (full[:, None] == jnp.arange(heavy, dtype=jnp.int32)[None, :]).astype(BF16)
@@ -140,14 +148,23 @@
     padded = weights.shape[0] // 3
 
     with jax.named_scope("gather_chips"):
-        both = jnp.concatenate([inputs, upstream], axis=1)[None]
-        got = exchange(copies(dense(both)[0], members // CORES), "dp", CORE_GROUPS)
+        tall = jnp.concatenate([inputs[:8], upstream[:8]], axis=1)
+        rest = jnp.concatenate([inputs[8:], upstream[8:]], axis=0)
+        both = jnp.concatenate([dense(tall[None])[0], dense(rest[None])[0]], axis=0)
+        got = exchange(copies(both, members // CORES), "dp", CORE_GROUPS)
         got, pick, weights, spread, grad_scale = lax.optimization_barrier(
             (got, pick, weights, spread, grad_scale)
         )
-        got = undense(got, capacity).reshape(-1, 2 * features)
+        cut = tall.size // LANES
+        tall = undense(got[:, :cut], 8).reshape(-1, 2 * features)
+        rest = undense(got[:, cut:], 8).reshape(-1, features)
     with jax.named_scope("gather_core"):
-        mine = jnp.dot(pick, got, preferred_element_type=F32).astype(BF16)
+        mine = jnp.dot(pick[0], tall, preferred_element_type=F32)
+        mine = mine + jnp.concatenate(
+            [jnp.dot(which, rest, preferred_element_type=F32) for which in (pick[1], pick[2])],
+            axis=1,
+        )
+        mine = mine.astype(BF16)
         other = lax.ppermute(mine, "dp", [(i, i ^ 1) for i in range(members)])
     with jax.named_scope("partial_sums"):
         kept, partial = call(

time: 119 us -> 121 us (1.017)
  local copies, waits for them, and re-layouts: 5.63 us -> 7.81 us
  other arithmetic: 5.32 us -> 4.06 us
    slice x0 -> x5, local copies, waits for them, and re-layouts: none -> 2.9 us  [the longest x2 1.42 us: body(): rest = jnp.concatenate([inputs[8:], upstream[8:]], axis=0)]
where the time goes in v14:
time: 121 us; the launch traced here: 120 us
  waiting for transfers between devices  40.9 us (34%)
  blocking collectives  35.3 us (29%)
  starting transfers between devices  25.9 us (21%)
  local copies, waits for them, and re-layouts  7.81 us (6%)
  other arithmetic  4.06 us (3%)
  matrix products  2.66 us (2%)
  between operations  1.67 us (1%)
  Pallas kernels  1.62 us (1%)
    all_to_all x2, waiting for transfers between devices, exchange(): return lax.all_to_all(x, axis, 0, 0, tiled=True, axis_index_groups=groups)  37 us
    all_to_all x2, blocking collectives, exchange(): return lax.all_to_all(x, axis, 0, 0, tiled=True, axis_index_groups=groups)  35.3 us
    all_to_all x2, starting transfers between devices, exchange(): return lax.all_to_all(x, axis, 0, 0, tiled=True, axis_index_groups=groups)  22.1 us
  transfers between devices with their start and end apart: 4, of which 4 were waited for; matrix products, arithmetic and copies ran while one was open for 6% of the time, Pallas kernels for 0%

profile of v14, /device:TPU:8, one launch (start us, length us, event | category | flops | bytes accessed | tf_op | source)
XLA Modules:
  0.0 120.0 jit_solution(12927583349458947259)
XLA Ops:
  0.7 0.7 slice.84
  1.4 0.7 slice.82
  2.1 0.7 slice.85
  2.8 0.7 slice.83
  3.5 1.1 broadcast_in_dim.63
  4.6 16.2 %all-to-all-start = ((bf16[32,120,128]{2,1,0:T(8,128)(2,1)}), bf16[32,120,128]{2,1,0:T(8,128)(2,1)S(1)}, u32[]{:S(2)}, u32[]{:S(2)}) async-start(bf16[32,120,128]{2,1,0:T(8,128)(2,1)} %broadcast_in_dim.63), calls=%async_computation | async-start | bytes 1966080 | tf_op jit(solution)/shard_map/gather_chips/all_to_all | solution.py:18
  21.1 0.6 compare_select_fusion
  23.2 0.2 fusion.31
  23.4 0.1 fusion.9
  23.6 1.5 %fusion.6.weights_ref = bf16[1536,640]{1,0:T(8,128)(2,1)S(1)} fusion(bf16[432,640]{1,0:T(8,128)(2,1)} %param.11, bf16[432,640]{1,0:T(8,128)(2,1)} %bitcast.72, bf16[432,640]{1,0:T(8,128)(2,1)} %bitcast.73), kind=kLoop, calls=%fused_computation.12 | loop fusion | flops 13762560 | bytes 3624960 | tf_op jit(solution)/shard_map/concatenate | solution.py:147
  25.1 25.5 %all-to-all-done = bf16[32,120,128]{2,1,0:T(8,128)(2,1)S(1)} async-done(((bf16[32,120,128]{2,1,0:T(8,128)(2,1)}), bf16[32,120,128]{2,1,0:T(8,128)(2,1)S(1)}, u32[]{:S(2)}, u32[]{:S(2)}) %all-to-all-start) | async-done | bytes 983072 | tf_op jit(solution)/shard_map/gather_chips/all_to_all | solution.py:18
  50.6 0.3 fusion.16
  50.9 0.3 fusion.18
  51.2 0.4 fusion.4.mine_ref
  51.6 1.9 %collective-permute-start = (bf16[288,1280]{1,0:T(8,128)(2,1)S(1)}, bf16[288,1280]{1,0:T(8,128)(2,1)S(1)}, u32[]{:S(2)}, u32[]{:S(2)}) collective-permute-start(bf16[288,1280]{1,0:T(8,128)(2,1)S(1)} %fusion.4.mine_ref), channel_id=1, source_target_pairs={{0,8},{8,0},{16,24},{24,16},{32,40},{40,32},{48,56},{56,48},{64,72... | collective-permute-start | bytes 2211848 | tf_op jit(solution)/shard_map/gather_core/ppermute | solution.py:168
  53.5 2.2 %collective-permute-done.other_ref = bf16[288,1280]{1,0:T(8,128)(2,1)S(1)} collective-permute-done((bf16[288,1280]{1,0:T(8,128)(2,1)S(1)}, bf16[288,1280]{1,0:T(8,128)(2,1)S(1)}, u32[]{:S(2)}, u32[]{:S(2)}) %collective-permute-start) | collective-permute-done | bytes 737312 | tf_op jit(solution)/shard_map/gather_core/ppermute | solution.py:168
  55.7 0.9 partial_sums.1
  56.6 19.2 %all_to_all.20 = bf16[8,432,128]{2,1,0:T(8,128)(2,1)S(1)} all-to-all(bf16[8,432,128]{2,1,0:T(8,128)(2,1)S(1)} %get-tuple-element.20), channel_id=1, replica_groups=mesh['dp'=64,'fsdp'=8] {'fsdp'}, dimensions={0} | all-to-all | bytes 1769472 | tf_op jit(solution)/shard_map/sum_features/all_to_all | solution.py:18
  76.1 16.1 %all_to_all.21.gathered_ref = bf16[8,432,128]{2,1,0:T(8,128)(2,1)S(1)} all-to-all(bf16[8,432,128]{2,1,0:T(8,128)(2,1)S(1)} %broadcast_in_dim.70), channel_id=1, replica_groups=mesh['dp'=64,'fsdp'=8] {'fsdp'}, dimensions={0} | all-to-all | bytes 1769472 | tf_op jit(solution)/shard_map/gather_hidden/all_to_all | solution.py:18
  92.2 0.7 grad_rows.1
  92.9 1.9 %collective-permute-start.1 = (f32[160,640]{1,0:T(8,128)S(1)}, f32[160,640]{1,0:T(8,128)S(1)}, u32[]{:S(2)}, u32[]{:S(2)}) collective-permute-start(f32[160,640]{1,0:T(8,128)S(1)} %get-tuple-element.22), channel_id=1, source_target_pairs={{0,8},{8,0},{16,24},{24,16},{32,40},{40,32},{48,56},{56,48},{64,72... | collective-permute-start | bytes 1228808 | tf_op jit(solution)/shard_map/grad_rows/ppermute | solution.py:207
  94.9 1.7 %collective-permute-done.1 = f32[160,640]{1,0:T(8,128)S(1)} collective-permute-done((f32[160,640]{1,0:T(8,128)S(1)}, f32[160,640]{1,0:T(8,128)S(1)}, u32[]{:S(2)}, u32[]{:S(2)}) %collective-permute-start.1) | collective-permute-done | bytes 409632 | tf_op jit(solution)/shard_map/grad_rows/ppermute | solution.py:207
  96.9 0.2 fusion.7
  97.2 0.3 reshape.170
  97.5 0.8 copy.28
  98.3 5.9 %all-to-all-start.3 = ((bf16[32,30,128]{2,1,0:T(8,128)(2,1)}), bf16[32,30,128]{2,1,0:T(8,128)(2,1)S(1)}, u32[]{:S(2)}, u32[]{:S(2)}) async-start(bf16[32,30,128]{2,1,0:T(8,128)(2,1)} %copy.28), calls=%async_computation.3 | async-start | bytes 524288 | tf_op jit(solution)/shard_map/grad_rows/all_to_all | solution.py:18
  104.2 0.6 fusion.13
  104.8 1.0 multiply_convert_fusion
  105.8 0.9 fusion.8
  106.7 1.1 slice_bitcast_fusion
  107.8 11.5 %all-to-all-done.3 = bf16[32,30,128]{2,1,0:T(8,128)(2,1)S(1)} async-done(((bf16[32,30,128]{2,1,0:T(8,128)(2,1)}), bf16[32,30,128]{2,1,0:T(8,128)(2,1)S(1)}, u32[]{:S(2)}, u32[]{:S(2)}) %all-to-all-start.3) | async-done | bytes 245792 | tf_op jit(solution)/shard_map/grad_rows/all_to_all | solution.py:18
  119.4 0.6 convert_element_type.70
  (48 shorter events, 1.8 us)
Async XLA Ops:
  0.6 20.2 %copy-start.3 = (s32[64]{0:T(128)S(1)}, s32[64]{0:T(128)}, u32[]{:S(2)}) copy-start(s32[64]{0:T(128)} %param.12) | copy-start | bytes 772
  0.6 20.2 %copy-start.2 = (s32[64,3]{0,1:T(4,128)S(1)}, s32[64,3]{0,1:T(4,128)}, u32[]{:S(2)}) copy-start(s32[64,3]{0,1:T(4,128)} %param.13) | copy-start | bytes 2308
  4.6 46.0 %all-to-all-start = ((bf16[32,120,128]{2,1,0:T(8,128)(2,1)}), bf16[32,120,128]{2,1,0:T(8,128)(2,1)S(1)}, u32[]{:S(2)}, u32[]{:S(2)}) async-start(bf16[32,120,128]{2,1,0:T(8,128)(2,1)} %broadcast_in_dim.63), calls=%async_computation | async-start | bytes 1966080 | tf_op jit(solution)/shard_map/gather_chips/all_to_all | solution.py:18
  51.6 4.1 %collective-permute-start = (bf16[288,1280]{1,0:T(8,128)(2,1)S(1)}, bf16[288,1280]{1,0:T(8,128)(2,1)S(1)}, u32[]{:S(2)}, u32[]{:S(2)}) collective-permute-start(bf16[288,1280]{1,0:T(8,128)(2,1)S(1)} %fusion.4.mine_ref), channel_id=1, source_target_pairs={{0,8},{8,0},{16,24},{24,16},{32,40},{40,32},{48,56},{56,48},{64,72... | collective-permute-start | bytes 2211848 | tf_op jit(solution)/shard_map/gather_core/ppermute | solution.py:168
  92.9 3.7 %copy-start = (bf16[288,1536]{1,0:T(8,128)(2,1)}, bf16[288,1536]{1,0:T(8,128)(2,1)S(1)}, u32[]{:S(2)}) copy-start(bf16[288,1536]{1,0:T(8,128)(2,1)S(1)} %get-tuple-element.27) | copy-start | bytes 2654212
  92.9 3.6 %collective-permute-start.1 = (f32[160,640]{1,0:T(8,128)S(1)}, f32[160,640]{1,0:T(8,128)S(1)}, u32[]{:S(2)}, u32[]{:S(2)}) collective-permute-start(f32[160,640]{1,0:T(8,128)S(1)} %get-tuple-element.22), channel_id=1, source_target_pairs={{0,8},{8,0},{16,24},{24,16},{32,40},{40,32},{48,56},{56,48},{64,72... | collective-permute-start | bytes 1228808 | tf_op jit(solution)/shard_map/grad_rows/ppermute | solution.py:207
  96.7 7.6 %copy-start.1 = (bf16[288,1536]{1,0:T(8,128)(2,1)S(1)}, bf16[288,1536]{1,0:T(8,128)(2,1)}, u32[]{:S(2)}) copy-start(bf16[288,1536]{1,0:T(8,128)(2,1)} %copy-done) | copy-start | bytes 2654212
  98.3 21.0 %all-to-all-start.3 = ((bf16[32,30,128]{2,1,0:T(8,128)(2,1)}), bf16[32,30,128]{2,1,0:T(8,128)(2,1)S(1)}, u32[]{:S(2)}, u32[]{:S(2)}) async-start(bf16[32,30,128]{2,1,0:T(8,128)(2,1)} %copy.28), calls=%async_computation.3 | async-start | bytes 524288 | tf_op jit(solution)/shard_map/grad_rows/all_to_all | solution.py:18
